TPU v7x, 256 devices: a whole 4x4x8 slice. The times are simulated.
256 devices in a mesh: dp: 4 (over z_hi), comp: 64 (over x, y, z_lo, core).
Axes of the slice: x: 4, y: 4, z: 8 (z_hi: 4, z_lo: 2; z = z_hi * 2 + z_lo), core: 2. Of those that a mesh axis runs over, the one named last changes fastest.
Arguments:
- embeddings: bfloat16 [16384, 1024], P(('dp', 'comp')), may hold values from -6 to 6
- keep: int32 [16384], P(('dp', 'comp')), may hold values from 0 to 1
- means: float32 [8192, 1024], P('comp'), may hold values from -0.6 to 0.6
- variances: float32 [8192, 1024], P('comp'), may hold values from 0.8 to 1.25
- log_weights: float32 [8192], P('comp'), may hold values from -4 to 4
Outputs:
- new_means: float32 [8192, 1024], P('comp')
- new_vars: float32 [8192, 1024], P('comp')
- new_log_weights: float32 [8192], P('comp')
- log_lik: float32 [16384], P(('dp', 'comp'))
All inputs are finite; a program needn't handle non-finite values.
Results may differ from a plain program's by a relative error of at most 0.0039.
The roundings to bfloat16 on the way count: a program that leaves them out, or rounds other values in their place, can miss the bound.
Values may be sent and summed in bfloat16 or wider, within the bound.
No kernel may reach another device: no remote copies, remote signals or barrier semaphores. Data moves between devices by JAX's collectives and lax.ppermute only.
A program may use at most 64 MiB of HBM per device.

v0:
```python
import math

import jax
import jax.numpy as jnp
from jax import lax
from jax.sharding import PartitionSpec as P


def features(rows):
    wide = rows.astype(jnp.float32)
    return jnp.concatenate([(wide * wide).astype(jnp.bfloat16), rows], axis=1)


def update_step(second, first, counts):
    denom = counts[:, None] + 1.0
    mean_part = first / denom
    var_part = (
        second - 2.0 * mean_part * first + mean_part * mean_part * counts[:, None] + 1.0
    ) / denom
    return (mean_part, var_part)


def local(embeddings, keep, means, variances, log_weights):
    width = embeddings.shape[1]
    rows_dev = embeddings.shape[0]
    comp_count = means.shape[0]
    prec = 1.0 / variances
    weights_mat = jnp.concatenate([-0.5 * prec, means * prec], axis=1).astype(jnp.bfloat16).T
    offset = (
        log_weights
        - 0.5 * jnp.sum(means * means * prec + jnp.log(variances), axis=1)
        - 0.5 * width * math.log(2.0 * math.pi)
    )
    keep_rows = keep.astype(jnp.float32).astype(jnp.bfloat16)
    block = (
        jnp.dot(
            features(lax.all_gather(embeddings, "comp", axis=0, tiled=True)),
            weights_mat,
            preferred_element_type=jnp.float32,
        )
        + offset
    )
    flags = lax.all_gather(keep_rows, "comp", axis=0, tiled=True).astype(jnp.float32)
    scores, flags = (block, flags)
    local_max = jnp.max(scores, axis=1)
    top = lax.pmax(local_max, "comp")
    total = lax.psum(jnp.sum(jnp.exp(scores - top[:, None]), axis=1), "comp")
    lse = top + jnp.log(total)
    resp = (jnp.exp(scores - lse[:, None]) * flags[:, None]).astype(jnp.bfloat16)
    counts = jnp.sum(resp.astype(jnp.float32), axis=0)
    kept_total = jnp.sum(flags)
    moments = lax.dot_general(
        resp,
        features(lax.all_gather(embeddings, "comp", axis=0, tiled=True)),
        (((0,), (0,)), ((), ())),
        preferred_element_type=jnp.float32,
    )
    moments, counts, kept_total = lax.psum((moments, counts, kept_total), "dp")
    new_means, new_vars = update_step(moments[:, :width], moments[:, width:], counts)
    new_log_weights = jnp.log((counts + 1.0) / (kept_total + comp_count * lax.axis_size("comp")))
    own_lse = lax.dynamic_slice_in_dim(lse, lax.axis_index("comp") * rows_dev, rows_dev)
    own_wide = embeddings.astype(jnp.float32)
    own_rows = (
        own_lse + 0.5 * jnp.sum(own_wide * own_wide, axis=1) + 0.5 * width * math.log(2.0 * math.pi)
    )
    return (new_means, new_vars, new_log_weights, own_rows)


def solution(mesh):
    placed = (
        P(("dp", "comp"), None),
        P(("dp", "comp")),
        P("comp", None),
        P("comp", None),
        P("comp"),
    )
    return jax.shard_map(
        local,
        mesh=mesh,
        in_specs=placed,
        out_specs=(P("comp", None), P("comp", None), P("comp"), P(("dp", "comp"))),
        check_vma=False,
    )
```

profile of v0, /device:TPU:32, one launch (start us, length us, event | category | flops | bytes accessed | tf_op | source)
XLA Modules:
  0.0 809.1 jit_solution(17220641450012581594)
XLA Ops:
  7.2 0.0 all-gather.2.cloned.1.call-start
  7.2 0.7 all-gather.2.cloned.1.call-update
  7.9 0.0 all-reduce.4.cloned.1.call-start
  8.0 1.3 dynamic-slice
  9.9 0.7 convert_convert_fusion
  10.5 0.2 dynamic-update-slice
  10.7 140.3 %all-reduce = bf16[4096]{0:T(1024)(128)(2,1)S(1)} all-reduce(bf16[4096]{0:T(1024)(128)(2,1)S(1)} %dynamic-update-slice), channel_id=1, replica_groups=mesh['dp'=4,'comp'=64] {'comp'}, use_global_device_ids=true, to_apply=%add | all-reduce | flops 4096 | bytes 16384
  151.1 1.5 multiply_convert_fusion.2
  152.6 0.7 subtract_add_fusion
  153.2 0.0 all-gather.2.cloned.1.call-done
  153.2 9.1 %multiply_convert_fusion = bf16[4096,1024]{1,0:T(8,128)(2,1)} fusion(bf16[4096,1024]{1,0:T(8,128)(2,1)} %all-gather.2.cloned.1.call-done), kind=kLoop, calls=%fused_computation.1 | loop fusion | flops 12582912 | bytes 16777216 | tf_op jit(solution)/shard_map/convert_element_type | solution.py:11
  162.3 9.3 %fusion.11 = (f32[4096]{0:T(1024)S(1)}, f32[4096,128]{0,1:T(8,128)S(1)}) fusion(f32[128]{0:T(128)S(1)} %subtract_add_fusion, bf16[128,1024]{1,0:T(8,128)(2,1)S(1)} %get-tuple-element.8, bf16[128,1024]{1,0:T(8,128)(2,1)S(1)} %get-tuple-element.10, bf16[4096,1024]{1,0:T(8,128)(2,1)} %all-gather.2.cloned.1.call-done, bf16[4096,1024]{1,0:T(8,128)(2,1)} %multiply_convert_fusion), kind=kOutput, calls=%fused_computation.30 | convolution fusion | flops 2183131136 | bytes 19415552 | tf_op jit(solution)/shard_map/dot_general | solution.py:36
  171.7 275.0 %pmax.7 = f32[4096]{0:T(1024)S(1)} all-reduce(f32[4096]{0:T(1024)S(1)} %get-tuple-element.13), channel_id=1, replica_groups=mesh['dp'=4,'comp'=64] {'comp'}, use_global_device_ids=true, to_apply=%region_2.0 | all-reduce | flops 4096 | bytes 32768 | tf_op jit(solution)/shard_map/pmax | solution.py:46
  446.7 0.3 exponential_reduce_fusion
  447.0 275.0 %psum.28 = f32[4096]{0:T(1024)S(1)} all-reduce(f32[4096]{0:T(1024)S(1)} %exponential_reduce_fusion), channel_id=1, replica_groups=mesh['dp'=4,'comp'=64] {'comp'}, use_global_device_ids=true, to_apply=%region_4.0 | all-reduce | flops 4096 | bytes 32768 | tf_op jit(solution)/shard_map/psum | solution.py:47
  722.0 0.0 copy-start
  722.0 8.8 %fusion = f32[128,2048]{1,0:T(8,128)} fusion(bf16[4096,1024]{1,0:T(8,128)(2,1)} %all-gather.2.cloned.1.call-done, bf16[4096,1024]{1,0:T(8,128)(2,1)} %multiply_convert_fusion, f32[4096,128]{0,1:T(8,128)S(1)} %get-tuple-element.14, f32[4096]{0:T(1024)S(1)} %convert_element_type.31, f32[4096]{0:T(1024)S(1)} %log_add_fusion), kind=kOutput, calls=%fused_computation.2 | convolution fusion | flops 2182610944 | bytes 19955712 | tf_op jit(solution)/shard_map/dot_general | solution.py:52
  730.7 0.0 all-reduce.4.cloned.1.call-update
  730.7 0.6 convert_reduce_fusion.1
  731.3 0.0 copy-done
  731.4 0.1 multiply_reduce_fusion
  731.5 0.4 convert_reduce_fusion
  731.9 14.8 %all-reduce.1 = (f32[128]{0:T(128)S(1)}, f32[]{:T(128)}) all-reduce(f32[128]{0:T(128)S(1)} %convert_reduce_fusion, f32[]{:T(128)} %convert_reduce_fusion.1), channel_id=1, replica_groups=mesh['dp'=4,'comp'=64] {'dp'}, use_global_device_ids=true, to_apply=%region_7.0 | all-reduce | flops 129 | bytes 1032 | tf_op jit(solution)/shard_map/psum | solution.py:58
  747.4 0.6 add_add_fusion
  748.0 0.5 divide_log_fusion
  748.5 51.3 %all-reduce.4.cloned.1.call-done = f32[128,2048]{1,0:T(8,128)} async-done(((f32[128,2048]{1,0:T(8,128)}), f32[128,2048]{1,0:T(8,128)}) %all-reduce.4.cloned.1.call-update) | async-done | bytes 1048592 | tf_op jit(solution)/shard_map/psum | solution.py:58
  799.9 2.4 fusion.5
  (3 shorter events, 0.0 us)
Async XLA Ops:
  7.2 146.1 %all-gather.2.cloned.1.call-start = ((), (), s32[]{:S(2)}) async-start(), calls=%async_computation | async-start | bytes 8519680 | tf_op jit(solution)/shard_map/all_gather | solution.py:37
  7.9 792.0 %all-reduce.4.cloned.1.call-start = ((), (), s32[]{:S(2)}) async-start(), calls=%async_computation.1 | async-start | bytes 2097152 | tf_op jit(solution)/shard_map/psum | solution.py:58
  722.0 9.4 %copy-start = (bf16[64,1024]{1,0:T(8,128)(2,1)S(1)}, bf16[64,1024]{1,0:T(8,128)(2,1)}, u32[]{:S(2)}) copy-start(bf16[64,1024]{1,0:T(8,128)(2,1)} %param.5) | copy-start | bytes 393220
Sparse Core Ops, SparseCore 0:
  9.9 116.1 all-gather.1
  730.9 68.9 all-reduce.3
where the time goes:
time: 811 us; the launch traced here: 809 us
  blocking collectives  705 us (87%)
  waiting for transfers between devices  52 us (6%)
  matrix products  18.1 us (2%)
  other arithmetic  16.9 us (2%)
  between operations  15.4 us (2%)
    pmax x1, blocking collectives, local(): top = lax.pmax(local_max, 'comp')  275 us
    psum x1, blocking collectives, local(): total = lax.psum(jnp.sum(jnp.exp(scores - top[:, None]), axis=1), 'comp')  275 us
    unnamed x1, blocking collectives  140 us
    psum x1, waiting for transfers between devices, local(): moments, counts, kept_total = lax.psum((moments, counts, kept_total), 'dp')  51.3 us
  transfers between devices with their start and end apart: 2, of which 1 were waited for; matrix products, arithmetic and copies ran while one was open for 1% of the time, Pallas kernels for 0%

commit v1 on v0

v1 whole, which is shorter than its diff:
```python
import functools
import math

import jax
import jax.numpy as jnp
from jax import lax
from jax.experimental import pallas as pl
from jax.experimental.pallas import tpu as pltpu
from jax.sharding import Mesh, PartitionSpec as P

F32 = jnp.float32
BF16 = jnp.bfloat16
EXT = 128
VMEM = pl.BlockSpec(memory_space=pltpu.VMEM)
SMEM = pl.BlockSpec(memory_space=pltpu.SMEM)
NT = (((1,), (1,)), ((), ()))
INTERPRET = False


def call(kernel, out_shape, n_in, flops=0, nbytes=0, smem=(), **kw):
    many = isinstance(out_shape, (list, tuple))
    n_out = len(out_shape) if many else 1
    specs = dict(
        in_specs=[SMEM if i in smem else VMEM for i in range(n_in)],
        out_specs=[VMEM] * n_out if many else VMEM,
    )
    specs.update(kw)
    return pl.pallas_call(
        kernel,
        out_shape=out_shape,
        compiler_params=pltpu.CompilerParams(vmem_limit_bytes=40 * 2**20),
        cost_estimate=pl.CostEstimate(flops=flops, bytes_accessed=nbytes, transcendentals=0),
        interpret=INTERPRET,
        **specs,
    )


def sds(shape, dtype):
    return jax.ShapeDtypeStruct(shape, dtype)


def parts(col, n):
    out = []
    for _ in range(n):
        top = col.astype(BF16).astype(F32)
        out.append(top)
        col = col - top
    return out


def lanes(cols, rows):
    lane = lax.broadcasted_iota(jnp.int32, (rows, EXT), 1)
    ext = jnp.zeros((rows, EXT), F32)
    for i, col in enumerate(cols):
        ext = jnp.where(lane == i, col, ext)
    return ext


def split_ext(ext):
    counts = ext[:, 0:1] + ext[:, 1:2]
    kept = ext[:, 2:3] + ext[:, 3:4]
    return lanes(parts(counts, 2) + parts(kept, 2), ext.shape[0]).astype(BF16)


def coef_kernel(m_ref, v_ref, w_ref, out_ref):
    rows, width = m_ref.shape
    m, v = m_ref[...], v_ref[...]
    prec = 1.0 / v
    out_ref[:, :width] = (-0.5 * prec).astype(BF16)
    out_ref[:, width : 2 * width] = (m * prec).astype(BF16)
    offset = (
        w_ref[...]
        - 0.5 * jnp.sum(m * m * prec + jnp.log(v), axis=1, keepdims=True)
        - 0.5 * width * math.log(2.0 * math.pi)
    )
    out_ref[:, 2 * width :] = lanes(parts(offset, 3), rows).astype(BF16)


def square(rows):
    wide = rows.astype(F32)
    return (wide * wide).astype(BF16)


def score_tile(e_ref, coef_ref, s_ref):
    width = e_ref.shape[1]
    rows = e_ref[...]
    s = lax.dot_general(coef_ref[:, :width], square(rows), NT, preferred_element_type=F32)
    s = s + lax.dot_general(coef_ref[:, width : 2 * width], rows, NT, preferred_element_type=F32)
    s = s + jnp.sum(coef_ref[:, 2 * width :].astype(F32), axis=1, keepdims=True)
    s_ref[...] = s
    top = jnp.max(s, axis=0, keepdims=True)
    lse = top + jnp.log(jnp.sum(jnp.exp(s - top), axis=0, keepdims=True))
    return [lse[:, i * 128 : (i + 1) * 128] for i in range(lse.shape[1] // 128)]


def score_kernel(e_ref, coef_ref, s_ref, lse_ref):
    rows = score_tile(e_ref, coef_ref, s_ref)
    for i, row in enumerate(rows):
        lse_ref[pl.ds(pl.program_id(0) * len(rows) + i, 1), :] = row


def score_kernel_b(e_ref, coef_ref, other_ref, keep_ref, s_ref, pay_ref):
    rows = score_tile(e_ref, coef_ref, s_ref)
    half = other_ref.shape[0]

    @pl.when(pl.program_id(0) == 0)
    def _():
        row = lax.broadcasted_iota(jnp.int32, (half, 128), 0)
        pay_ref[half:, :] = jnp.where(row == 0, keep_ref[...], 0.0)

    for i, row in enumerate(rows):
        at = pl.ds(pl.program_id(0) * len(rows) + i, 1)
        other = other_ref[at, :]
        top = jnp.maximum(row, other)
        pay_ref[at, :] = top + jnp.log(jnp.exp(row - top) + jnp.exp(other - top))


def moment_body(pay_ref, s_ref, e_ref, out_ref, p_ref):
    groups, _, _ = pay_ref.shape
    half = pay_ref.shape[1] // 2
    comps = s_ref.shape[0]
    width = e_ref.shape[1]
    pay = pay_ref[:, :half, :]
    top = jnp.max(pay, axis=0)
    lse = top + jnp.log(jnp.sum(jnp.exp(pay - top[None]), axis=0))
    total = jnp.zeros((comps, 128), F32)
    kept = jnp.zeros((1, 128), F32)
    for j in range(half):
        at = slice(j * 128, (j + 1) * 128)
        keep = pay_ref[2 * j, half : half + 1, :] + pay_ref[2 * j + 1, half : half + 1, :]
        p = (jnp.exp(s_ref[:, at] - lse[j : j + 1, :]) * keep).astype(BF16)
        p_ref[:, at] = p
        total = total + p.astype(F32)
        kept = kept + keep
    counts = jnp.sum(total, axis=1, keepdims=True)
    kept = jnp.broadcast_to(jnp.sum(kept, axis=1, keepdims=True), (comps, 1))
    rows = e_ref[...]
    p = p_ref[...]
    second = jnp.dot(p, square(rows), preferred_element_type=F32)
    first = jnp.dot(p, rows, preferred_element_type=F32)
    zero = jnp.zeros_like(counts)
    ext = lanes([counts, zero, kept, zero], comps)
    if out_ref.dtype == BF16:
        ext = split_ext(ext)
    out_ref[:, :width] = second.astype(out_ref.dtype)
    out_ref[:, width : 2 * width] = first.astype(out_ref.dtype)
    out_ref[:, 2 * width :] = ext
    return lse


def moment_kernel_b(pay_ref, s_ref, e_ref, out_ref, lse_ref, p_ref):
    lse_ref[...] = moment_body(pay_ref, s_ref, e_ref, out_ref, p_ref)


def moment_kernel(pay_ref, s_ref, e_ref, out_ref, p_ref):
    moment_body(pay_ref, s_ref, e_ref, out_ref, p_ref)


def to_bf16(out_ref, total):
    feats = total.shape[1] - EXT
    out_ref[:, :feats] = total[:, :feats].astype(BF16)
    out_ref[:, feats:] = split_ext(total[:, feats:])


def core_sum_kernel(own_ref, got_ref, up_ref, down_ref, mine_ref):
    rows = mine_ref.shape[0]
    half = rows // 2
    mine_ref[...] = own_ref[:rows, :] + got_ref[:rows, :].astype(F32)
    for i, ref in enumerate((up_ref, down_ref)):
        at = slice(rows + i * half, rows + (i + 1) * half)
        to_bf16(ref, own_ref[at, :] + got_ref[at, :].astype(F32))


def pair_sum_kernel(me_ref, mine_ref, low_ref, high_ref, own_ref, s1_ref, s2_ref, s3_ref, all_ref):
    half = low_ref.shape[0]
    quarter = own_ref.shape[0]
    all_ref[:half, :] = mine_ref[:half, :] + low_ref[...].astype(F32)
    all_ref[half:, :] = mine_ref[half:, :] + high_ref[...].astype(F32)
    me = me_ref[0]

    def rows(shift):
        return all_ref[pl.ds(lax.rem(me + shift, 4) * quarter, quarter), :]

    own_ref[...] = rows(0)
    for shift, ref in ((1, s1_ref), (2, s2_ref), (3, s3_ref)):
        to_bf16(ref, rows(shift))


def finish_kernel(n_comps, own_ref, g1_ref, g2_ref, g3_ref, out_ref):
    total = own_ref[...] + g1_ref[...].astype(F32) + g2_ref[...].astype(F32) + g3_ref[...].astype(F32)
    rows = total.shape[0]
    width = (total.shape[1] - EXT) // 2
    second, first, ext = total[:, :width], total[:, width : 2 * width], total[:, 2 * width :]
    counts = ext[:, 0:1] + ext[:, 1:2]
    kept = ext[:, 2:3] + ext[:, 3:4]
    denom = counts + 1.0
    mean = first / denom
    out_ref[:, :width] = mean.astype(BF16)
    out_ref[:, width : 2 * width] = (
        (second - 2.0 * mean * first + mean * mean * counts + 1.0) / denom
    ).astype(BF16)
    log_w = jnp.log(denom / (kept + float(n_comps)))
    out_ref[:, 2 * width :] = lanes(parts(log_w, 3), rows).astype(BF16)


def place_kernel(me_ref, r0_ref, r1_ref, r2_ref, r3_ref, mean_ref, var_ref, log_ref):
    quarter = r0_ref.shape[0]
    width = mean_ref.shape[1]
    me = me_ref[0]
    for shift, ref in enumerate((r0_ref, r1_ref, r2_ref, r3_ref)):
        at = pl.ds(lax.rem(me + 4 - shift, 4) * quarter, quarter)
        mean_ref[at, :] = ref[:, :width].astype(F32)
        var_ref[at, :] = ref[:, width : 2 * width].astype(F32)
        log_ref[at, :] = jnp.sum(ref[:, 2 * width :].astype(F32), axis=1, keepdims=True)


def ring(n, shift):
    return [(i, (i + shift) % n) for i in range(n)]


def local(embeddings, keep, means, variances, log_weights):
    own, width = embeddings.shape
    comps = means.shape[0]
    n_comps = comps * 64
    cols = 2 * width + EXT
    plane, z, core = ("x", "y"), ("zh", "zl"), "c"
    n_rows = 16 * own
    zh = lax.axis_index("zh").astype(jnp.int32).reshape(1)
    at = lax.axis_index(plane)

    coef = call(coef_kernel, sds((comps, cols), BF16), 3)(means, variances, log_weights[:, None])
    half = comps // 2
    low = lax.ppermute(coef[:half], z, ring(8, 1))
    high = lax.ppermute(coef[half:], z, ring(8, 7))

    rows = lax.all_to_all(
        jnp.broadcast_to(embeddings[None], (16, own, width)), plane, 0, 0
    ).reshape(n_rows, width)

    coef_a = jnp.concatenate([coef, low, high], axis=0)
    coef_b = lax.ppermute(coef_a, core, ring(2, 1))

    flag = keep.astype(F32)
    odd = (at % 2).astype(F32)
    flag = jnp.concatenate([flag * (1.0 - odd), flag * odd]).reshape(1, 2 * own)

    tile = 256
    grid = n_rows // tile
    score_flops = 2 * 2 * comps * n_rows * 2 * width
    e_spec = pl.BlockSpec((tile, width), lambda i: (i, 0))
    s_spec = pl.BlockSpec((2 * comps, tile), lambda i: (0, i))
    s_shape = sds((2 * comps, n_rows), F32)

    def whole(shape):
        return pl.BlockSpec(shape, lambda i: (0,) * len(shape))

    lse_rows = n_rows // 128
    score_a, lse_a = call(
        score_kernel,
        (s_shape, sds((lse_rows, 128), F32)),
        2,
        score_flops,
        grid=(grid,),
        in_specs=[e_spec, whole((2 * comps, cols))],
        out_specs=[s_spec, whole((lse_rows, 128))],
    )(rows, coef_a)
    score_b, pay = call(
        score_kernel_b,
        (s_shape, sds((2 * lse_rows, 128), F32)),
        4,
        score_flops,
        grid=(grid,),
        in_specs=[e_spec, whole((2 * comps, cols)), whole((lse_rows, 128)), whole((1, 128))],
        out_specs=[s_spec, whole((2 * lse_rows, 128))],
    )(rows, coef_b, lse_a, flag)

    pays = lax.all_to_all(jnp.broadcast_to(pay[None], (16,) + pay.shape), plane, 0, 0)

    p_scratch = dict(scratch_shapes=[pltpu.VMEM((2 * comps, n_rows), BF16)])
    send, lse = call(
        moment_kernel_b,
        (sds((2 * comps, cols), BF16), sds((lse_rows, 128), F32)),
        3,
        score_flops,
        **p_scratch,
    )(pays, score_b, rows)
    got = lax.ppermute(send, core, ring(2, 1))
    own_sum = call(moment_kernel, sds((2 * comps, cols), F32), 3, score_flops, **p_scratch)(
        pays, score_a, rows
    )
    up, down, mine = call(
        core_sum_kernel,
        (sds((half, cols), BF16), sds((half, cols), BF16), sds((comps, cols), F32)),
        2,
    )(own_sum, got)
    low = lax.ppermute(up, z, ring(8, 1))
    high = lax.ppermute(down, z, ring(8, 7))
    quarter = comps // 4
    q32, q16 = sds((quarter, cols), F32), sds((quarter, cols), BF16)
    own_q, s1, s2, s3 = call(
        pair_sum_kernel,
        (q32, q16, q16, q16),
        4,
        smem=(0,),
        scratch_shapes=[pltpu.VMEM((comps, cols), F32)],
    )(zh, mine, low, high)
    g = [lax.ppermute(s, "zh", ring(4, i + 1)) for i, s in enumerate((s1, s2, s3))]
    result = call(functools.partial(finish_kernel, n_comps), q16, 4)(own_q, *g)
    r = [result] + [lax.ppermute(result, "zh", ring(4, s)) for s in (1, 2, 3)]
    out = sds((comps, width), F32)
    new_means, new_vars, new_log = call(
        place_kernel, (out, out, sds((comps, 1), F32)), 5, smem=(0,)
    )(zh, *r)

    own_lse = lax.dynamic_slice_in_dim(lse.reshape(-1), at * own, own)
    wide = embeddings.astype(F32)
    log_lik = own_lse + 0.5 * jnp.sum(wide * wide, axis=1) + 0.5 * width * math.log(2.0 * math.pi)
    return new_means, new_vars, new_log.reshape(-1), log_lik


def solution(mesh):
    axes = ("x", "y", "zl", "c")
    fine = Mesh(mesh.devices.reshape(4, 4, 4, 2, 2), ("zh",) + axes)
    both = ("zh",) + axes
    return jax.shard_map(
        local,
        mesh=fine,
        in_specs=(P(both, None), P(both), P(axes, None), P(axes, None), P(axes)),
        out_specs=(P(axes, None), P(axes, None), P(axes), P(both)),
        check_vma=False,
    )
```

time: 811 us -> 114 us (0.14)
  blocking collectives: 705 us -> 11.3 us
  starting transfers between devices: 0.08 us -> 28.2 us
  matrix products: 18.1 us -> 0 us
  other arithmetic: 16.9 us -> 1.5 us
  between operations: 15.4 us -> 0.81 us
  Pallas kernels: 0 us -> 11.2 us
    psum x2 -> x0, blocking collectives: 290 us -> none  [the longest x1 275 us: local(): total = lax.psum(jnp.sum(jnp.exp(scores - top[:, None]), axis=1), 'comp')]
    pmax x1 -> x0, blocking collectives: 275 us -> none  [local(): top = lax.pmax(local_max, 'comp')]
    unnamed x1 -> x0, blocking collectives: 140 us -> none
    psum x1 -> x0, waiting for transfers between devices: 51.3 us -> none  [local(): moments, counts, kept_total = lax.psum((moments, counts, kept_total), 'dp')]
    ppermute x0 -> x12, waiting for transfers between devices: none -> 39.1 us  [the longest x3 13 us: local(): r = [result] + [lax.ppermute(result, 'zh', ring(4, s)) for s in (1, 2, 3)]]
    ppermute x0 -> x12, starting transfers between devices: none -> 21 us  [the longest x3 9.44 us: local(): lax.ppermute(s, 'zh', ring(4, i + 1))]
    all_to_all x0 -> x1, waiting for transfers between devices: none -> 19.5 us  [local(): lax.all_to_all(jnp.broadcast_to(embeddings[None], (16, own, width)), plan...]
    dot_general x2 -> x0, matrix products: 18.1 us -> none  [the longest x1 9.32 us: local(): jnp.dot(features(lax.all_gather(embeddings, 'comp', axis=0, tiled=True)),...]
  transfers between devices with their start and end apart: 2 -> 13, of which waited for: 1 -> 11; matrix products, arithmetic and copies ran while one was open for 1% -> 1% of each run, Pallas kernels for 0% -> 4%
where the time goes in v1:
time: 114 us
  waiting for transfers between devices  58.6 us (51%)
  starting transfers between devices  28.2 us (25%)
  blocking collectives  11.3 us (10%)
  Pallas kernels  11.2 us (10%)
  local copies, waits for them, and re-layouts  2.69 us (2%)
  other arithmetic  1.5 us (1%)
    all_to_all x1, waiting for transfers between devices, local(): lax.all_to_all(jnp.broadcast_to(embeddings[None], (16, own, width)), plan...  19.5 us
    ppermute x3, waiting for transfers between devices, local(): r = [result] + [lax.ppermute(result, 'zh', ring(4, s)) for s in (1, 2, 3)]  13 us
    all_to_all x1, blocking collectives, local(): lax.all_to_all(jnp.broadcast_to(pay[None], (16,) + pay.shape), plane, 0, 0)  11.3 us
    ppermute x3, starting transfers between devices, local(): lax.ppermute(s, 'zh', ring(4, i + 1))  9.44 us
    ppermute x3, waiting for transfers between devices, local(): lax.ppermute(s, 'zh', ring(4, i + 1))  8.44 us
    ppermute x3, starting transfers between devices, local(): r = [result] + [lax.ppermute(result, 'zh', ring(4, s)) for s in (1, 2, 3)]  7.19 us
    all_to_all x1, starting transfers between devices, local(): lax.all_to_all(jnp.broadcast_to(embeddings[None], (16, own, width)), plan...  7.17 us
    ppermute x1, waiting for transfers between devices, local(): low = lax.ppermute(up, z, ring(8, 1))  6.67 us
  transfers between devices with their start and end apart: 13, of which 11 were waited for; matrix products, arithmetic and copies ran while one was open for 1% of the time, Pallas kernels for 4%

profile of v1, /device:TPU:32, one launch (start us, length us, event | category | flops | bytes accessed | tf_op | source)
XLA Modules:
  0.0 114.2 jit_solution(11718819801022488827)
XLA Ops:
  0.6 2.5 %broadcast_in_dim.6 = bf16[16,64,1024]{2,1,0:T(8,128)(2,1)} broadcast(bf16[64,1024]{1,0:T(8,128)(2,1)} %param.5), dimensions={1,2} | broadcast | bytes 2228224 | tf_op jit(solution)/shard_map/broadcast_in_dim | solution.py:237
  3.1 7.2 %all-to-all-start = ((bf16[16,64,1024]{2,1,0:T(8,128)(2,1)}), bf16[16,64,1024]{2,1,0:T(8,128)(2,1)S(1)}, u32[]{:S(2)}, u32[]{:S(2)}) async-start(bf16[16,64,1024]{2,1,0:T(8,128)(2,1)} %broadcast_in_dim.6), calls=%async_computation | async-start | bytes 4194304 | tf_op jit(solution)/shard_map/all_to_all | solution.py:236
  10.4 0.4 shard_map.84
  10.9 2.0 %collective-permute-start = (bf16[64,2176]{1,0:T(8,128)(2,1)S(1)}, bf16[64,2176]{1,0:T(8,128)(2,1)S(1)}, u32[]{:S(2)}, u32[]{:S(2)}) collective-permute-start(bf16[64,2176]{1,0:T(8,128)(2,1)S(1)} %get-tuple-element.36), channel_id=1, source_target_pairs={{0,2},{2,64},{64,66},{66,128},{128,130},{130,192},{192,194},{194,0... | collective-permute-start | bytes 835592 | tf_op jit(solution)/shard_map/ppermute | solution.py:233
  13.0 6.1 %collective-permute-done = bf16[64,2176]{1,0:T(8,128)(2,1)S(1)} collective-permute-done((bf16[64,2176]{1,0:T(8,128)(2,1)S(1)}, bf16[64,2176]{1,0:T(8,128)(2,1)S(1)}, u32[]{:S(2)}, u32[]{:S(2)}) %collective-permute-start) | collective-permute-done | bytes 278560 | tf_op jit(solution)/shard_map/ppermute | solution.py:233
  19.1 1.8 %collective-permute-done.1 = bf16[64,2176]{1,0:T(8,128)(2,1)S(1)} collective-permute-done((bf16[64,2176]{1,0:T(8,128)(2,1)S(1)}, bf16[64,2176]{1,0:T(8,128)(2,1)S(1)}, u32[]{:S(2)}, u32[]{:S(2)}) %collective-permute-start.1) | collective-permute-done | bytes 278560 | tf_op jit(solution)/shard_map/ppermute | solution.py:234
  21.2 19.5 %all-to-all-done = bf16[16,64,1024]{2,1,0:T(8,128)(2,1)S(1)} async-done(((bf16[16,64,1024]{2,1,0:T(8,128)(2,1)}), bf16[16,64,1024]{2,1,0:T(8,128)(2,1)S(1)}, u32[]{:S(2)}, u32[]{:S(2)}) %all-to-all-start) | async-done | bytes 2097184 | tf_op jit(solution)/shard_map/all_to_all | solution.py:236
  40.7 2.2 %shard_map.85 = (f32[256,1024]{1,0:T(8,128)S(1)}, f32[8,128]{1,0:T(8,128)S(1)}) custom-call(bf16[1024,1024]{1,0:T(8,128)(2,1)S(1)} %bitcast.6, bf16[256,2176]{1,0:T(8,128)(2,1)S(1)} %pad_maximum_fusion.coef_ref), custom_call_target="tpu_custom_call" | custom-call | flops 1073741824 | tf_op jit(solution)/shard_map/pallas_call | solution.py:258
  42.9 3.6 %shard_map.86 = (f32[256,1024]{1,0:T(8,128)S(1)}, f32[16,128]{1,0:T(8,128)S(1)}) custom-call(bf16[1024,1024]{1,0:T(8,128)(2,1)S(1)} %bitcast.7, bf16[256,2176]{1,0:T(8,128)(2,1)} %collective-permute-done.2.coef_ref, f32[8,128]{1,0:T(8,128)S(1)} %get-tuple-element.20.other_ref, f32[1,128]{1,0:T(1,128)S(1)} %maximum_bitcast_fusion.keep_ref), custom_call_target="tpu_custom_call" | custom-call | flops 1073741824 | tf_op jit(solution)/shard_map/pallas_call | solution.py:267
  46.5 11.3 %all_to_all.10.pay_ref = f32[16,16,128]{2,1,0:T(8,128)S(1)} all-to-all(f32[16,16,128]{2,1,0:T(8,128)S(1)} %broadcast_in_dim.8), channel_id=1, replica_groups=mesh['zh'=4,'x'=4,'y'=4,'zl'=2,'c'=2] {'x','y'}, dimensions={0} | all-to-all | bytes 262144 | tf_op jit(solution)/shard_map/all_to_all | solution.py:277
  57.8 1.6 %shard_map.88 = (bf16[256,2176]{1,0:T(8,128)(2,1)S(1)}, f32[8,128]{1,0:T(8,128)S(1)}) custom-call(f32[16,16,128]{2,1,0:T(8,128)S(1)} %all_to_all.10.pay_ref, f32[256,1024]{1,0:T(8,128)S(1)} %get-tuple-element.23.s_ref, bf16[1024,1024]{1,0:T(8,128)(2,1)S(1)} %bitcast.8), custom_call_target="tpu_custom_call" | custom-call | flops 1073741824 | tf_op jit(solution)/shard_map/pallas_call | solution.py:280
  59.5 1.5 %shard_map.87.own_ref = f32[256,2176]{1,0:T(8,128)S(1)} custom-call(f32[16,16,128]{2,1,0:T(8,128)S(1)} %all_to_all.10.pay_ref, f32[256,1024]{1,0:T(8,128)S(1)} %get-tuple-element.22.s_ref, bf16[1024,1024]{1,0:T(8,128)(2,1)S(1)} %bitcast.9), custom_call_target="tpu_custom_call" | custom-call | flops 1073741824 | tf_op jit(solution)/shard_map/pallas_call | solution.py:288
  61.0 1.2 %collective-permute-done.3.got_ref = bf16[256,2176]{1,0:T(8,128)(2,1)S(1)} collective-permute-done((bf16[256,2176]{1,0:T(8,128)(2,1)S(1)}, bf16[256,2176]{1,0:T(8,128)(2,1)S(1)}, u32[]{:S(2)}, u32[]{:S(2)}) %collective-permute-start.3) | collective-permute-done | bytes 1114144 | tf_op jit(solution)/shard_map/ppermute | solution.py:287
  62.2 0.4 shard_map.89
  62.6 2.0 %collective-permute-start.4 = (bf16[64,2176]{1,0:T(8,128)(2,1)S(1)}, bf16[64,2176]{1,0:T(8,128)(2,1)S(1)}, u32[]{:S(2)}, u32[]{:S(2)}) collective-permute-start(bf16[64,2176]{1,0:T(8,128)(2,1)S(1)} %get-tuple-element.26), channel_id=1, source_target_pairs={{0,2},{2,64},{64,66},{66,128},{128,130},{130,192},{192,194},{194,0... | collective-permute-start | bytes 835592 | tf_op jit(solution)/shard_map/ppermute | solution.py:296
  64.7 6.7 %collective-permute-done.4.low_ref = bf16[64,2176]{1,0:T(8,128)(2,1)S(1)} collective-permute-done((bf16[64,2176]{1,0:T(8,128)(2,1)S(1)}, bf16[64,2176]{1,0:T(8,128)(2,1)S(1)}, u32[]{:S(2)}, u32[]{:S(2)}) %collective-permute-start.4) | collective-permute-done | bytes 278560 | tf_op jit(solution)/shard_map/ppermute | solution.py:296
  71.4 1.8 %collective-permute-done.5.high_ref = bf16[64,2176]{1,0:T(8,128)(2,1)S(1)} collective-permute-done((bf16[64,2176]{1,0:T(8,128)(2,1)S(1)}, bf16[64,2176]{1,0:T(8,128)(2,1)S(1)}, u32[]{:S(2)}, u32[]{:S(2)}) %collective-permute-start.5) | collective-permute-done | bytes 278560 | tf_op jit(solution)/shard_map/ppermute | solution.py:297
  73.2 0.3 shard_map.90
  73.5 5.6 %collective-permute-start.6 = (bf16[32,2176]{1,0:T(8,128)(2,1)S(1)}, bf16[32,2176]{1,0:T(8,128)(2,1)S(1)}, u32[]{:S(2)}, u32[]{:S(2)}) collective-permute-start(bf16[32,2176]{1,0:T(8,128)(2,1)S(1)} %get-tuple-element.29), channel_id=1, source_target_pairs={{0,64},{64,128},{128,192},{192,0},{1,65},{65,129},{129,193},{193,1... | collective-permute-start | bytes 417800 | tf_op jit(solution)/shard_map/ppermute | solution.py:307
  79.1 1.7 %collective-permute-start.7 = (bf16[32,2176]{1,0:T(8,128)(2,1)S(1)}, bf16[32,2176]{1,0:T(8,128)(2,1)S(1)}, u32[]{:S(2)}, u32[]{:S(2)}) collective-permute-start(bf16[32,2176]{1,0:T(8,128)(2,1)S(1)} %get-tuple-element.30), channel_id=1, source_target_pairs={{0,128},{64,192},{128,0},{192,64},{1,129},{65,193},{129,1},{193,65... | collective-permute-start | bytes 417800 | tf_op jit(solution)/shard_map/ppermute | solution.py:307
  80.9 2.1 %collective-permute-start.8 = (bf16[32,2176]{1,0:T(8,128)(2,1)S(1)}, bf16[32,2176]{1,0:T(8,128)(2,1)S(1)}, u32[]{:S(2)}, u32[]{:S(2)}) collective-permute-start(bf16[32,2176]{1,0:T(8,128)(2,1)S(1)} %get-tuple-element.31), channel_id=1, source_target_pairs={{0,192},{64,0},{128,64},{192,128},{1,193},{65,1},{129,65},{193,129... | collective-permute-start | bytes 417800 | tf_op jit(solution)/shard_map/ppermute | solution.py:307
  83.1 4.5 %collective-permute-done.6.g1_ref = bf16[32,2176]{1,0:T(8,128)(2,1)S(1)} collective-permute-done((bf16[32,2176]{1,0:T(8,128)(2,1)S(1)}, bf16[32,2176]{1,0:T(8,128)(2,1)S(1)}, u32[]{:S(2)}, u32[]{:S(2)}) %collective-permute-start.6) | collective-permute-done | bytes 139296 | tf_op jit(solution)/shard_map/ppermute | solution.py:307
  87.6 4.0 %collective-permute-done.7.g2_ref = bf16[32,2176]{1,0:T(8,128)(2,1)S(1)} collective-permute-done((bf16[32,2176]{1,0:T(8,128)(2,1)S(1)}, bf16[32,2176]{1,0:T(8,128)(2,1)S(1)}, u32[]{:S(2)}, u32[]{:S(2)}) %collective-permute-start.7) | collective-permute-done | bytes 139296 | tf_op jit(solution)/shard_map/ppermute | solution.py:307
  91.5 0.3 shard_map.91.r0_ref
  91.8 3.6 %collective-permute-start.10 = (bf16[32,2176]{1,0:T(8,128)(2,1)S(1)}, bf16[32,2176]{1,0:T(8,128)(2,1)S(1)}, u32[]{:S(2)}, u32[]{:S(2)}) collective-permute-start(bf16[32,2176]{1,0:T(8,128)(2,1)S(1)} %shard_map.91.r0_ref), channel_id=1, source_target_pairs={{0,128},{64,192},{128,0},{192,64},{1,129},{65,193},{129,1},{193,65... | collective-permute-start | bytes 417800 | tf_op jit(solution)/shard_map/ppermute | solution.py:309
  95.4 3.6 %collective-permute-start.11 = (bf16[32,2176]{1,0:T(8,128)(2,1)S(1)}, bf16[32,2176]{1,0:T(8,128)(2,1)S(1)}, u32[]{:S(2)}, u32[]{:S(2)}) collective-permute-start(bf16[32,2176]{1,0:T(8,128)(2,1)S(1)} %shard_map.91.r0_ref), channel_id=1, source_target_pairs={{0,192},{64,0},{128,64},{192,128},{1,193},{65,1},{129,65},{193,129... | collective-permute-start | bytes 417800 | tf_op jit(solution)/shard_map/ppermute | solution.py:309
  99.0 0.6 add_add_fusion
  99.6 1.4 %collective-permute-done.10.r2_ref = bf16[32,2176]{1,0:T(8,128)(2,1)S(1)} collective-permute-done((bf16[32,2176]{1,0:T(8,128)(2,1)S(1)}, bf16[32,2176]{1,0:T(8,128)(2,1)S(1)}, u32[]{:S(2)}, u32[]{:S(2)}) %collective-permute-start.10) | collective-permute-done | bytes 139296 | tf_op jit(solution)/shard_map/ppermute | solution.py:309
  101.0 5.7 %collective-permute-done.11.r3_ref = bf16[32,2176]{1,0:T(8,128)(2,1)S(1)} collective-permute-done((bf16[32,2176]{1,0:T(8,128)(2,1)S(1)}, bf16[32,2176]{1,0:T(8,128)(2,1)S(1)}, u32[]{:S(2)}, u32[]{:S(2)}) %collective-permute-start.11) | collective-permute-done | bytes 139296 | tf_op jit(solution)/shard_map/ppermute | solution.py:309
  106.6 6.0 %collective-permute-done.9.r1_ref = bf16[32,2176]{1,0:T(8,128)(2,1)S(1)} collective-permute-done((bf16[32,2176]{1,0:T(8,128)(2,1)S(1)}, bf16[32,2176]{1,0:T(8,128)(2,1)S(1)}, u32[]{:S(2)}, u32[]{:S(2)}) %collective-permute-start.9) | collective-permute-done | bytes 139296 | tf_op jit(solution)/shard_map/ppermute | solution.py:309
  112.6 1.0 shard_map.92
  113.6 0.6 reduce
  (24 shorter events, 0.9 us)
Async XLA Ops:
  3.1 7.2 %copy-start.3 = (f32[128]{0:T(128)S(1)}, f32[128]{0:T(128)}, u32[]{:S(2)}) copy-start(f32[128]{0:T(128)} %param.9) | copy-start | bytes 1540
  3.1 7.3 %copy-start = (f32[128,1024]{1,0:T(8,128)S(1)}, f32[128,1024]{1,0:T(8,128)}, u32[]{:S(2)}) copy-start(f32[128,1024]{1,0:T(8,128)} %m_ref.1) | copy-start | bytes 1572868
  3.1 7.3 %copy-start.1 = (f32[128,1024]{1,0:T(8,128)S(1)}, f32[128,1024]{1,0:T(8,128)}, u32[]{:S(2)}) copy-start(f32[128,1024]{1,0:T(8,128)} %v_ref.1) | copy-start | bytes 1572868
  3.1 37.6 %all-to-all-start = ((bf16[16,64,1024]{2,1,0:T(8,128)(2,1)}), bf16[16,64,1024]{2,1,0:T(8,128)(2,1)S(1)}, u32[]{:S(2)}, u32[]{:S(2)}) async-start(bf16[16,64,1024]{2,1,0:T(8,128)(2,1)} %broadcast_in_dim.6), calls=%async_computation | async-start | bytes 4194304 | tf_op jit(solution)/shard_map/all_to_all | solution.py:236
  10.9 8.2 %collective-permute-start = (bf16[64,2176]{1,0:T(8,128)(2,1)S(1)}, bf16[64,2176]{1,0:T(8,128)(2,1)S(1)}, u32[]{:S(2)}, u32[]{:S(2)}) collective-permute-start(bf16[64,2176]{1,0:T(8,128)(2,1)S(1)} %get-tuple-element.36), channel_id=1, source_target_pairs={{0,2},{2,64},{64,66},{66,128},{128,130},{130,192},{192,194},{194,0... | collective-permute-start | bytes 835592 | tf_op jit(solution)/shard_map/ppermute | solution.py:233
  12.9 8.2 %copy-start.4 = (s32[64]{0:T(128)S(1)}, s32[64]{0:T(128)}, u32[]{:S(2)}) copy-start(s32[64]{0:T(128)} %param.6) | copy-start | bytes 772
  12.9 8.0 %collective-permute-start.1 = (bf16[64,2176]{1,0:T(8,128)(2,1)S(1)}, bf16[64,2176]{1,0:T(8,128)(2,1)S(1)}, u32[]{:S(2)}, u32[]{:S(2)}) collective-permute-start(bf16[64,2176]{1,0:T(8,128)(2,1)S(1)} %get-tuple-element.37), channel_id=1, source_target_pairs={{0,194},{2,0},{64,2},{66,64},{128,66},{130,128},{192,130},{194,192... | collective-permute-start | bytes 835592 | tf_op jit(solution)/shard_map/ppermute | solution.py:234
  21.0 21.9 %collective-permute-start.2 = (bf16[256,2176]{1,0:T(8,128)(2,1)S(1)}, bf16[256,2176]{1,0:T(8,128)(2,1)}, u32[]{:S(2)}, u32[]{:S(2)}) collective-permute-start(bf16[256,2176]{1,0:T(8,128)(2,1)S(1)} %pad_maximum_fusion.coef_ref), channel_id=1, source_target_pairs={{0,1},{1,0},{2,3},{3,2},{4,5},{5,4},{6,7},{7,6},{8,9},{9,8},{10,11... | collective-permute-start | bytes 3342344 | tf_op jit(solution)/shard_map/ppermute | solution.py:241
  59.4 2.8 %collective-permute-start.3 = (bf16[256,2176]{1,0:T(8,128)(2,1)S(1)}, bf16[256,2176]{1,0:T(8,128)(2,1)S(1)}, u32[]{:S(2)}, u32[]{:S(2)}) collective-permute-start(bf16[256,2176]{1,0:T(8,128)(2,1)S(1)} %get-tuple-element.24), channel_id=1, source_target_pairs={{0,1},{1,0},{2,3},{3,2},{4,5},{5,4},{6,7},{7,6},{8,9},{9,8},{10,11... | collective-permute-start | bytes 3342344 | tf_op jit(solution)/shard_map/ppermute | solution.py:287
  62.6 20.4 %copy-start.2 = (bf16[64,1024]{1,0:T(8,128)(2,1)S(1)}, bf16[64,1024]{1,0:T(8,128)(2,1)}, u32[]{:S(2)}) copy-start(bf16[64,1024]{1,0:T(8,128)(2,1)} %param.5) | copy-start | bytes 393220
  62.6 8.8 %collective-permute-start.4 = (bf16[64,2176]{1,0:T(8,128)(2,1)S(1)}, bf16[64,2176]{1,0:T(8,128)(2,1)S(1)}, u32[]{:S(2)}, u32[]{:S(2)}) collective-permute-start(bf16[64,2176]{1,0:T(8,128)(2,1)S(1)} %get-tuple-element.26), channel_id=1, source_target_pairs={{0,2},{2,64},{64,66},{66,128},{128,130},{130,192},{192,194},{194,0... | collective-permute-start | bytes 835592 | tf_op jit(solution)/shard_map/ppermute | solution.py:296
  64.6 8.6 %collective-permute-start.5 = (bf16[64,2176]{1,0:T(8,128)(2,1)S(1)}, bf16[64,2176]{1,0:T(8,128)(2,1)S(1)}, u32[]{:S(2)}, u32[]{:S(2)}) collective-permute-start(bf16[64,2176]{1,0:T(8,128)(2,1)S(1)} %get-tuple-element.27), channel_id=1, source_target_pairs={{0,194},{2,0},{64,2},{66,64},{128,66},{130,128},{192,130},{194,192... | collective-permute-start | bytes 835592 | tf_op jit(solution)/shard_map/ppermute | solution.py:297
  73.5 14.0 %collective-permute-start.6 = (bf16[32,2176]{1,0:T(8,128)(2,1)S(1)}, bf16[32,2176]{1,0:T(8,128)(2,1)S(1)}, u32[]{:S(2)}, u32[]{:S(2)}) collective-permute-start(bf16[32,2176]{1,0:T(8,128)(2,1)S(1)} %get-tuple-element.29), channel_id=1, source_target_pairs={{0,64},{64,128},{128,192},{192,0},{1,65},{65,129},{129,193},{193,1... | collective-permute-start | bytes 417800 | tf_op jit(solution)/shard_map/ppermute | solution.py:307
  79.1 12.4 %collective-permute-start.7 = (bf16[32,2176]{1,0:T(8,128)(2,1)S(1)}, bf16[32,2176]{1,0:T(8,128)(2,1)S(1)}, u32[]{:S(2)}, u32[]{:S(2)}) collective-permute-start(bf16[32,2176]{1,0:T(8,128)(2,1)S(1)} %get-tuple-element.30), channel_id=1, source_target_pairs={{0,128},{64,192},{128,0},{192,64},{1,129},{65,193},{129,1},{193,65... | collective-permute-start | bytes 417800 | tf_op jit(solution)/shard_map/ppermute | solution.py:307
  80.9 10.7 %collective-permute-start.8 = (bf16[32,2176]{1,0:T(8,128)(2,1)S(1)}, bf16[32,2176]{1,0:T(8,128)(2,1)S(1)}, u32[]{:S(2)}, u32[]{:S(2)}) collective-permute-start(bf16[32,2176]{1,0:T(8,128)(2,1)S(1)} %get-tuple-element.31), channel_id=1, source_target_pairs={{0,192},{64,0},{128,64},{192,128},{1,193},{65,1},{129,65},{193,129... | collective-permute-start | bytes 417800 | tf_op jit(solution)/shard_map/ppermute | solution.py:307
  91.8 9.1 %collective-permute-start.10 = (bf16[32,2176]{1,0:T(8,128)(2,1)S(1)}, bf16[32,2176]{1,0:T(8,128)(2,1)S(1)}, u32[]{:S(2)}, u32[]{:S(2)}) collective-permute-start(bf16[32,2176]{1,0:T(8,128)(2,1)S(1)} %shard_map.91.r0_ref), channel_id=1, source_target_pairs={{0,128},{64,192},{128,0},{192,64},{1,129},{65,193},{129,1},{193,65... | collective-permute-start | bytes 417800 | tf_op jit(solution)/shard_map/ppermute | solution.py:309
  95.4 11.2 %collective-permute-start.11 = (bf16[32,2176]{1,0:T(8,128)(2,1)S(1)}, bf16[32,2176]{1,0:T(8,128)(2,1)S(1)}, u32[]{:S(2)}, u32[]{:S(2)}) collective-permute-start(bf16[32,2176]{1,0:T(8,128)(2,1)S(1)} %shard_map.91.r0_ref), channel_id=1, source_target_pairs={{0,192},{64,0},{128,64},{192,128},{1,193},{65,1},{129,65},{193,129... | collective-permute-start | bytes 417800 | tf_op jit(solution)/shard_map/ppermute | solution.py:309
  99.0 13.6 %collective-permute-start.9 = (bf16[32,2176]{1,0:T(8,128)(2,1)S(1)}, bf16[32,2176]{1,0:T(8,128)(2,1)S(1)}, u32[]{:S(2)}, u32[]{:S(2)}) collective-permute-start(bf16[32,2176]{1,0:T(8,128)(2,1)S(1)} %shard_map.91.r0_ref), channel_id=1, source_target_pairs={{0,64},{64,128},{128,192},{192,0},{1,65},{65,129},{129,193},{193,1... | collective-permute-start | bytes 417800 | tf_op jit(solution)/shard_map/ppermute | solution.py:309

commit v2 on v1

v2 whole, which is shorter than its diff:
```python
import functools
import math

import jax
import jax.numpy as jnp
from jax import lax
from jax.experimental import pallas as pl
from jax.experimental.pallas import tpu as pltpu
from jax.sharding import Mesh, PartitionSpec as P

F32 = jnp.float32
BF16 = jnp.bfloat16
EXT = 128
VMEM = pl.BlockSpec(memory_space=pltpu.VMEM)
SMEM = pl.BlockSpec(memory_space=pltpu.SMEM)
NT = (((1,), (1,)), ((), ()))
SHIFTS = (0, 1, 3, 2)
INTERPRET = False


def call(kernel, out_shape, n_in, flops=0, nbytes=0, smem=(), **kw):
    many = isinstance(out_shape, (list, tuple))
    n_out = len(out_shape) if many else 1
    specs = dict(
        in_specs=[SMEM if i in smem else VMEM for i in range(n_in)],
        out_specs=[VMEM] * n_out if many else VMEM,
    )
    specs.update(kw)
    return pl.pallas_call(
        kernel,
        out_shape=out_shape,
        compiler_params=pltpu.CompilerParams(vmem_limit_bytes=40 * 2**20),
        cost_estimate=pl.CostEstimate(flops=flops, bytes_accessed=nbytes, transcendentals=0),
        interpret=INTERPRET,
        **specs,
    )


def sds(shape, dtype):
    return jax.ShapeDtypeStruct(shape, dtype)


def parts(col, n):
    out = []
    for _ in range(n):
        top = col.astype(BF16).astype(F32)
        out.append(top)
        col = col - top
    return out


def lanes(cols, rows):
    lane = lax.broadcasted_iota(jnp.int32, (rows, EXT), 1)
    ext = jnp.zeros((rows, EXT), F32)
    for i, col in enumerate(cols):
        ext = jnp.where(lane == i, col, ext)
    return ext


def split_ext(ext):
    counts = ext[:, 0:1] + ext[:, 1:2]
    kept = ext[:, 2:3] + ext[:, 3:4]
    return lanes(parts(counts, 2) + parts(kept, 2), ext.shape[0]).astype(BF16)


def coef_kernel(m_ref, v_ref, w_ref, out_ref):
    rows, width = m_ref.shape
    m, v = m_ref[...], v_ref[...]
    prec = 1.0 / v
    out_ref[:, :width] = (-0.5 * prec).astype(BF16)
    out_ref[:, width : 2 * width] = (m * prec).astype(BF16)
    offset = (
        w_ref[...]
        - 0.5 * jnp.sum(m * m * prec + jnp.log(v), axis=1, keepdims=True)
        - 0.5 * width * math.log(2.0 * math.pi)
    )
    out_ref[:, 2 * width :] = lanes(parts(offset, 3), rows).astype(BF16)


def square(rows):
    wide = rows.astype(F32)
    return (wide * wide).astype(BF16)


def slot(ids_ref, piece, k):
    return lax.rem(ids_ref[0] + 4 - SHIFTS[k], 4) * 4 + lax.rem(ids_ref[1] + 4 - SHIFTS[piece], 4)


def score_kernel(e_ref, coef_a_ref, coef_b_ref, s_a_ref, s_b_ref, lse_ref):
    width = e_ref.shape[1]
    rows = e_ref[...]
    squares = square(rows)
    tops = []
    for coef_ref, s_ref in ((coef_a_ref, s_a_ref), (coef_b_ref, s_b_ref)):
        s = lax.dot_general(coef_ref[:, :width], squares, NT, preferred_element_type=F32)
        s = s + lax.dot_general(coef_ref[:, width : 2 * width], rows, NT, preferred_element_type=F32)
        s = s + jnp.sum(coef_ref[:, 2 * width :].astype(F32), axis=1, keepdims=True)
        s_ref[...] = s
        tops.append(jnp.max(s, axis=0, keepdims=True))
    top = jnp.maximum(*tops)
    total = sum(jnp.sum(jnp.exp(ref[...] - top), axis=0, keepdims=True) for ref in (s_a_ref, s_b_ref))
    lse_ref[...] = top + jnp.log(total)


def pay_kernel(ids_ref, keep_ref, l0_ref, l1_ref, l2_ref, l3_ref, pay_ref):
    lane = lax.broadcasted_iota(jnp.int32, (1, 128), 1)
    for piece, ref in enumerate((l0_ref, l1_ref, l2_ref, l3_ref)):
        for k in range(4):
            row = ref[:, (k // 2) * 128 : (k // 2 + 1) * 128]
            if k % 2:
                row = pltpu.roll(row, 64, 1)
            pay_ref[pl.ds(slot(ids_ref, piece, k), 1), :] = jnp.where(lane < 64, row, 0.0)
    pay_ref[0:1, :] = jnp.where(lane < 64, pay_ref[0:1, :], keep_ref[...])


def moment_body(ids_ref, pay_ref, lse_ref, s_refs, e_refs, out_ref):
    comps = s_refs[0].shape[0]
    width = e_refs[0].shape[1]
    pay = pay_ref[...]
    top = jnp.max(pay, axis=0)
    lse_ref[...] = top + jnp.log(jnp.sum(jnp.exp(pay - top[None]), axis=0))
    lane = lax.broadcasted_iota(jnp.int32, (1, 128), 1)
    total = jnp.zeros((comps, 128), F32)
    kept = jnp.zeros((1, 128), F32)
    second = first = None
    for piece, (s_ref, e_ref) in enumerate(zip(s_refs, e_refs, strict=True)):
        ps = []
        for j in range(2):
            at = [slot(ids_ref, piece, 2 * j + i) for i in range(2)]
            left, right = (lse_ref[pl.ds(i, 1), :] for i in at)
            lse = jnp.where(lane < 64, left, pltpu.roll(right, 64, 1))
            left, right = (pay_ref[i, 0:1, :] for i in at)
            keep = jnp.where(lane < 64, pltpu.roll(left, 64, 1), right)
            p = (jnp.exp(s_ref[:, j * 128 : (j + 1) * 128] - lse) * keep).astype(BF16)
            total = total + p.astype(F32)
            kept = kept + keep
            ps.append(p)
        p = jnp.concatenate(ps, axis=1)
        rows = e_ref[...]
        add2 = jnp.dot(p, square(rows), preferred_element_type=F32)
        add1 = jnp.dot(p, rows, preferred_element_type=F32)
        second = add2 if piece == 0 else second + add2
        first = add1 if piece == 0 else first + add1
    counts = jnp.sum(total, axis=1, keepdims=True)
    kept = jnp.broadcast_to(jnp.sum(kept, axis=1, keepdims=True), (comps, 1))
    zero = jnp.zeros_like(counts)
    ext = lanes([counts, zero, kept, zero], comps)
    if out_ref.dtype == BF16:
        ext = split_ext(ext)
    out_ref[:, :width] = second.astype(out_ref.dtype)
    out_ref[:, width : 2 * width] = first.astype(out_ref.dtype)
    out_ref[:, 2 * width :] = ext


def moment_kernel_b(ids_ref, pay_ref, s0, s1, s2, s3, e0, e1, e2, e3, out_ref, own_ref, lse_ref):
    moment_body(ids_ref, pay_ref, lse_ref, (s0, s1, s2, s3), (e0, e1, e2, e3), out_ref)
    own_ref[...] = lse_ref[pl.ds(slot(ids_ref, 0, 0), 1), :]


def moment_kernel(ids_ref, pay_ref, s0, s1, s2, s3, e0, e1, e2, e3, out_ref, lse_ref):
    moment_body(ids_ref, pay_ref, lse_ref, (s0, s1, s2, s3), (e0, e1, e2, e3), out_ref)


def to_bf16(out_ref, total):
    feats = total.shape[1] - EXT
    out_ref[:, :feats] = total[:, :feats].astype(BF16)
    out_ref[:, feats:] = split_ext(total[:, feats:])


def core_sum_kernel(own_ref, got_ref, up_ref, down_ref, mine_ref):
    rows = mine_ref.shape[0]
    half = rows // 2
    mine_ref[...] = own_ref[:rows, :] + got_ref[:rows, :].astype(F32)
    for i, ref in enumerate((up_ref, down_ref)):
        at = slice(rows + i * half, rows + (i + 1) * half)
        to_bf16(ref, own_ref[at, :] + got_ref[at, :].astype(F32))


def pair_sum_kernel(me_ref, mine_ref, low_ref, high_ref, own_ref, s1_ref, s2_ref, s3_ref, all_ref):
    half = low_ref.shape[0]
    quarter = own_ref.shape[0]
    all_ref[:half, :] = mine_ref[:half, :] + low_ref[...].astype(F32)
    all_ref[half:, :] = mine_ref[half:, :] + high_ref[...].astype(F32)
    me = me_ref[2]

    def rows(shift):
        return all_ref[pl.ds(lax.rem(me + shift, 4) * quarter, quarter), :]

    own_ref[...] = rows(0)
    for shift, ref in ((1, s1_ref), (2, s2_ref), (3, s3_ref)):
        to_bf16(ref, rows(shift))


def finish_kernel(n_comps, own_ref, g1_ref, g2_ref, g3_ref, out_ref):
    total = own_ref[...] + g1_ref[...].astype(F32) + g2_ref[...].astype(F32) + g3_ref[...].astype(F32)
    rows = total.shape[0]
    width = (total.shape[1] - EXT) // 2
    second, first, ext = total[:, :width], total[:, width : 2 * width], total[:, 2 * width :]
    counts = ext[:, 0:1] + ext[:, 1:2]
    kept = ext[:, 2:3] + ext[:, 3:4]
    denom = counts + 1.0
    mean = first / denom
    out_ref[:, :width] = mean.astype(BF16)
    out_ref[:, width : 2 * width] = (
        (second - 2.0 * mean * first + mean * mean * counts + 1.0) / denom
    ).astype(BF16)
    log_w = jnp.log(denom / (kept + float(n_comps)))
    out_ref[:, 2 * width :] = lanes(parts(log_w, 3), rows).astype(BF16)


def place_kernel(me_ref, r0_ref, r1_ref, r2_ref, r3_ref, mean_ref, var_ref, log_ref, ext_ref):
    quarter = r0_ref.shape[0]
    width = mean_ref.shape[1]
    me = me_ref[2]
    for shift, ref in enumerate((r0_ref, r1_ref, r2_ref, r3_ref)):
        at = pl.ds(lax.rem(me + 4 - shift, 4) * quarter, quarter)
        mean_ref[at, :] = ref[:, :width].astype(F32)
        var_ref[at, :] = ref[:, width : 2 * width].astype(F32)
        ext_ref[at, :] = ref[:, 2 * width :].astype(F32)
    ones = jnp.ones((8, EXT), BF16)
    log_ref[...] = lax.dot_general(ones, ext_ref[...].astype(BF16), NT, preferred_element_type=F32)[0:1, :]


def ring(n, shift):
    return [(i, (i + shift) % n) for i in range(n)]


def local(embeddings, keep, means, variances, log_weights):
    own, width = embeddings.shape
    comps = means.shape[0]
    n_comps = comps * 64
    cols = 2 * width + EXT
    plane, z, core = ("x", "y"), ("zh", "zl"), "c"
    ids = jnp.stack([lax.axis_index(a) for a in ("x", "y", "zh")]).astype(jnp.int32)

    line = [embeddings] + [lax.ppermute(embeddings, "x", ring(4, s)) for s in SHIFTS[1:]]
    line = jnp.concatenate(line, axis=0)
    pieces = [line] + [lax.ppermute(line, "y", ring(4, s)) for s in SHIFTS[1:]]

    coef = call(coef_kernel, sds((comps, cols), BF16), 3)(means, variances, log_weights[:, None])
    coef_a = jnp.concatenate([coef, lax.ppermute(coef, "zl", ring(2, 1))], axis=0)
    coef_b = lax.ppermute(coef_a, core, ring(2, 1))

    tile = 4 * own
    flops = 2 * 2 * comps * tile * 2 * width
    half_s = sds((2 * comps, tile), F32)
    scores = [
        call(score_kernel, (half_s, half_s, sds((1, tile), F32)), 3, 2 * flops)(p, coef_a, coef_b)
        for p in pieces
    ]
    flag = jnp.pad(keep.astype(F32), (own, 0)).reshape(1, 2 * own)
    pay = call(pay_kernel, sds((16, 128), F32), 6, smem=(0,))(ids, flag, *[s[2] for s in scores])
    pays = lax.all_to_all(jnp.broadcast_to(pay[None], (16,) + pay.shape), plane, 0, 0)

    lse_scratch = dict(smem=(0,), scratch_shapes=[pltpu.VMEM((16, 128), F32)])
    send, own_lse = call(
        moment_kernel_b, (sds((2 * comps, cols), BF16), sds((1, 128), F32)), 10, 4 * flops, **lse_scratch
    )(ids, pays, *[s[1] for s in scores], *pieces)
    got = lax.ppermute(send, core, ring(2, 1))
    own_sum = call(moment_kernel, sds((2 * comps, cols), F32), 10, 4 * flops, **lse_scratch)(
        ids, pays, *[s[0] for s in scores], *pieces
    )
    half = comps // 2
    up, down, mine = call(
        core_sum_kernel,
        (sds((half, cols), BF16), sds((half, cols), BF16), sds((comps, cols), F32)),
        2,
    )(own_sum, got)
    low = lax.ppermute(up, z, ring(8, 1))
    high = lax.ppermute(down, z, ring(8, 7))
    quarter = comps // 4
    q32, q16 = sds((quarter, cols), F32), sds((quarter, cols), BF16)
    own_q, s1, s2, s3 = call(
        pair_sum_kernel,
        (q32, q16, q16, q16),
        4,
        smem=(0,),
        scratch_shapes=[pltpu.VMEM((comps, cols), F32)],
    )(ids, mine, low, high)
    g = [lax.ppermute(s, "zh", ring(4, i)) for i, s in ((2, s2), (1, s1), (3, s3))]
    result = call(functools.partial(finish_kernel, n_comps), q16, 4)(own_q, *g)
    r2, r1, r3 = [lax.ppermute(result, "zh", ring(4, s)) for s in (2, 1, 3)]
    out = sds((comps, width), F32)
    new_means, new_vars, new_log = call(
        place_kernel,
        (out, out, sds((1, comps), F32)),
        5,
        smem=(0,),
        scratch_shapes=[pltpu.VMEM((comps, EXT), F32)],
    )(ids, result, r1, r2, r3)

    wide = embeddings.astype(F32)
    own_norm = 0.5 * jnp.sum(wide * wide, axis=1) + 0.5 * width * math.log(2.0 * math.pi)
    return new_means, new_vars, new_log.reshape(-1), own_lse[0, :own] + own_norm


def solution(mesh):
    axes = ("x", "y", "zl", "c")
    fine = Mesh(mesh.devices.reshape(4, 4, 4, 2, 2), ("zh",) + axes)
    both = ("zh",) + axes
    return jax.shard_map(
        local,
        mesh=fine,
        in_specs=(P(both, None), P(both), P(axes, None), P(axes, None), P(axes)),
        out_specs=(P(axes, None), P(axes, None), P(axes), P(both)),
        check_vma=False,
    )
```

time: 114 us -> 132 us (1.16)
  the two profiles are of different devices: /device:TPU:32 before, /device:TPU:1 now
where the time goes in v2:
time: 132 us
  waiting for transfers between devices  67.5 us (51%)
  starting transfers between devices  32.2 us (24%)
  Pallas kernels  15.1 us (11%)
  blocking collectives  12.4 us (9%)
  local copies, waits for them, and re-layouts  2.98 us (2%)
    ppermute x3, waiting for transfers between devices, local(): pieces = [line] + [lax.ppermute(line, 'y', ring(4, s)) for s in SHIFTS[1:]]  19.7 us
    all_to_all x1, blocking collectives, local(): lax.all_to_all(jnp.broadcast_to(pay[None], (16,) + pay.shape), plane, 0, 0)  12.4 us
    ppermute x1, waiting for transfers between devices, local(): lax.ppermute(coef, 'zl', ring(2, 1))  11.3 us
    ppermute x3, waiting for transfers between devices, local(): lax.ppermute(s, 'zh', ring(4, i))  11 us
    ppermute x3, waiting for transfers between devices, local(): r2, r1, r3 = [lax.ppermute(result, 'zh', ring(4, s)) for s in (2, 1, 3)]  10.7 us
    ppermute x1, waiting for transfers between devices, local(): high = lax.ppermute(down, z, ring(8, 7))  6.07 us
    ppermute x3, waiting for transfers between devices, local(): lax.ppermute(embeddings, 'x', ring(4, s))  5.78 us
    ppermute x3, starting transfers between devices, local(): r2, r1, r3 = [lax.ppermute(result, 'zh', ring(4, s)) for s in (2, 1, 3)]  5.65 us
  transfers between devices with their start and end apart: 17, of which 11 were waited for; matrix products, arithmetic and copies ran while one was open for 1% of the time, Pallas kernels for 5%

profile of v2, /device:TPU:1, one launch (start us, length us, event | category | flops | bytes accessed | tf_op | source)
XLA Modules:
  0.0 131.8 jit_solution(7212072975470051350)
XLA Ops:
  1.4 1.0 copy-done
  2.4 1.0 copy-done.1
  3.9 2.6 %collective-permute-start.3 = (bf16[128,2176]{1,0:T(8,128)(2,1)S(1)}, bf16[128,2176]{1,0:T(8,128)(2,1)S(1)}, u32[]{:S(2)}, u32[]{:S(2)}) collective-permute-start(bf16[128,2176]{1,0:T(8,128)(2,1)S(1)} %shard_map.84), channel_id=1, source_target_pairs={{0,2},{2,0},{1,3},{3,1},{4,6},{6,4},{5,7},{7,5},{8,10},{10,8},{9,1... | collective-permute-start | bytes 1671176 | tf_op jit(solution)/shard_map/ppermute | solution.py:241
  6.4 11.3 %collective-permute-done.3 = bf16[128,2176]{1,0:T(8,128)(2,1)S(1)} collective-permute-done((bf16[128,2176]{1,0:T(8,128)(2,1)S(1)}, bf16[128,2176]{1,0:T(8,128)(2,1)S(1)}, u32[]{:S(2)}, u32[]{:S(2)}) %collective-permute-start.3) | collective-permute-done | bytes 557088 | tf_op jit(solution)/shard_map/ppermute | solution.py:241
  17.8 2.4 %collective-permute-start.4 = (bf16[256,2176]{1,0:T(8,128)(2,1)S(1)}, bf16[256,2176]{1,0:T(8,128)(2,1)S(1)}, u32[]{:S(2)}, u32[]{:S(2)}) collective-permute-start(bf16[256,2176]{1,0:T(8,128)(2,1)S(1)} %pad_maximum_fusion.coef_a_ref), channel_id=1, source_target_pairs={{0,1},{1,0},{2,3},{3,2},{4,5},{5,4},{6,7},{7,6},{8,9},{9,8},{10,11... | collective-permute-start | bytes 3342344 | tf_op jit(solution)/shard_map/ppermute | solution.py:242
  20.2 1.2 collective-permute-start
  21.4 1.5 %collective-permute-start.1 = (bf16[64,1024]{1,0:T(8,128)(2,1)S(1)}, bf16[64,1024]{1,0:T(8,128)(2,1)S(1)}, u32[]{:S(2)}, u32[]{:S(2)}) collective-permute-start(bf16[64,1024]{1,0:T(8,128)(2,1)S(1)} %copy-done.2), channel_id=1, source_target_pairs={{0,48},{16,0},{32,16},{48,32},{1,49},{17,1},{33,17},{49,33},{2,50}... | collective-permute-start | bytes 393224 | tf_op jit(solution)/shard_map/ppermute | solution.py:236
  22.9 1.5 %collective-permute-start.2 = (bf16[64,1024]{1,0:T(8,128)(2,1)S(1)}, bf16[64,1024]{1,0:T(8,128)(2,1)S(1)}, u32[]{:S(2)}, u32[]{:S(2)}) collective-permute-start(bf16[64,1024]{1,0:T(8,128)(2,1)S(1)} %copy-done.2), channel_id=1, source_target_pairs={{0,32},{16,48},{32,0},{48,16},{1,33},{17,49},{33,1},{49,17},{2,34}... | collective-permute-start | bytes 393224 | tf_op jit(solution)/shard_map/ppermute | solution.py:236
  24.4 2.0 %collective-permute-done = bf16[64,1024]{1,0:T(8,128)(2,1)S(1)} collective-permute-done((bf16[64,1024]{1,0:T(8,128)(2,1)S(1)}, bf16[64,1024]{1,0:T(8,128)(2,1)S(1)}, u32[]{:S(2)}, u32[]{:S(2)}) %collective-permute-start) | collective-permute-done | bytes 131104 | tf_op jit(solution)/shard_map/ppermute | solution.py:236
  26.5 3.8 %collective-permute-done.2 = bf16[64,1024]{1,0:T(8,128)(2,1)S(1)} collective-permute-done((bf16[64,1024]{1,0:T(8,128)(2,1)S(1)}, bf16[64,1024]{1,0:T(8,128)(2,1)S(1)}, u32[]{:S(2)}, u32[]{:S(2)}) %collective-permute-start.2) | collective-permute-done | bytes 131104 | tf_op jit(solution)/shard_map/ppermute | solution.py:236
  30.3 3.0 %collective-permute-start.7 = (bf16[256,1024]{1,0:T(8,128)(2,1)S(1)}, bf16[256,1024]{1,0:T(8,128)(2,1)S(1)}, u32[]{:S(2)}, u32[]{:S(2)}) collective-permute-start(bf16[256,1024]{1,0:T(8,128)(2,1)S(1)} %constant_dynamic-update-slice_fusion.e_ref.e0), channel_id=1, source_target_pairs={{0,8},{4,12},{8,0},{12,4},{1,9},{5,13},{9,1},{13,5},{2,10},{6,14},... | collective-permute-start | bytes 1572872 | tf_op jit(solution)/shard_map/ppermute | solution.py:238
  35.7 8.7 %collective-permute-done.7.e_ref.e3 = bf16[256,1024]{1,0:T(8,128)(2,1)S(1)} collective-permute-done((bf16[256,1024]{1,0:T(8,128)(2,1)S(1)}, bf16[256,1024]{1,0:T(8,128)(2,1)S(1)}, u32[]{:S(2)}, u32[]{:S(2)}) %collective-permute-start.7) | collective-permute-done | bytes 524320 | tf_op jit(solution)/shard_map/ppermute | solution.py:238
  45.3 10.9 %collective-permute-done.6.e_ref.e2 = bf16[256,1024]{1,0:T(8,128)(2,1)} collective-permute-done((bf16[256,1024]{1,0:T(8,128)(2,1)S(1)}, bf16[256,1024]{1,0:T(8,128)(2,1)}, u32[]{:S(2)}, u32[]{:S(2)}) %collective-permute-start.6) | collective-permute-done | bytes 524320 | tf_op jit(solution)/shard_map/ppermute | solution.py:238
  56.3 1.9 %shard_map.87 = (f32[256,256]{1,0:T(8,128)S(1)}, f32[256,256]{1,0:T(8,128)S(1)}, f32[1,256]{1,0:T(1,128)S(1)}) custom-call(bf16[256,1024]{1,0:T(8,128)(2,1)} %collective-permute-done.6.e_ref.e2, bf16[256,2176]{1,0:T(8,128)(2,1)S(1)} %pad_maximum_fusion.coef_a_ref, bf16[256,2176]{1,0:T(8,128)(2,1)S(1)} %collective-permute-done.4.coef_b_ref), custom_call_target="tpu_custom_call" | custom-call | flops 536870912 | tf_op jit(solution)/shard_map/pallas_call | solution.py:248
  58.2 1.9 %shard_map.86 = (f32[256,256]{1,0:T(8,128)S(1)}, f32[256,256]{1,0:T(8,128)S(1)}, f32[1,256]{1,0:T(1,128)S(1)}) custom-call(bf16[256,1024]{1,0:T(8,128)(2,1)} %collective-permute-done.5.e_ref.e1, bf16[256,2176]{1,0:T(8,128)(2,1)S(1)} %pad_maximum_fusion.coef_a_ref, bf16[256,2176]{1,0:T(8,128)(2,1)S(1)} %collective-permute-done.4.coef_b_ref), custom_call_target="tpu_custom_call" | custom-call | flops 536870912 | tf_op jit(solution)/shard_map/pallas_call | solution.py:248
  60.7 12.4 %all_to_all.5.pay_ref = f32[16,16,128]{2,1,0:T(8,128)S(1)} all-to-all(f32[16,16,128]{2,1,0:T(8,128)S(1)} %broadcast_in_dim.10), channel_id=1, replica_groups=mesh['zh'=4,'x'=4,'y'=4,'zl'=2,'c'=2] {'x','y'}, dimensions={0} | all-to-all | bytes 262144 | tf_op jit(solution)/shard_map/all_to_all | solution.py:253
  73.1 2.8 %shard_map.91 = (bf16[256,2176]{1,0:T(8,128)(2,1)S(1)}, f32[1,128]{1,0:T(1,128)S(1)}) custom-call(s32[3]{0:T(128)S(1)} %pad_add_fusion.ids_ref.me_ref, f32[16,16,128]{2,1,0:T(8,128)S(1)} %all_to_all.5.pay_ref, f32[256,256]{1,0:T(8,128)S(1)} %get-tuple-element.36.s0, f32[256,256]{1,0:T(8,128)S(1)} %get-tuple-element.37.s1, ...), custom_call_target="tpu_custom_call" | custom-call | flops 1073741824 | tf_op jit(solution)/shard_map/pallas_call | solution.py:256
  75.8 1.9 %collective-permute-start.8 = (bf16[256,2176]{1,0:T(8,128)(2,1)S(1)}, bf16[256,2176]{1,0:T(8,128)(2,1)S(1)}, u32[]{:S(2)}, u32[]{:S(2)}) collective-permute-start(bf16[256,2176]{1,0:T(8,128)(2,1)S(1)} %get-tuple-element.40), channel_id=1, source_target_pairs={{0,1},{1,0},{2,3},{3,2},{4,5},{5,4},{6,7},{7,6},{8,9},{9,8},{10,11... | collective-permute-start | bytes 3342344 | tf_op jit(solution)/shard_map/ppermute | solution.py:259
  77.7 2.7 %shard_map.90.own_ref = f32[256,2176]{1,0:T(8,128)S(1)} custom-call(s32[3]{0:T(128)S(1)} %pad_add_fusion.ids_ref.me_ref, f32[16,16,128]{2,1,0:T(8,128)S(1)} %all_to_all.5.pay_ref, f32[256,256]{1,0:T(8,128)S(1)} %get-tuple-element.32.s0, f32[256,256]{1,0:T(8,128)S(1)} %get-tuple-element.33.s1, f32[256,256]{1,0:T(8,128)S(1)} %get-tuple-element.34.s2, ...), custom_call_target="tpu_custom_call" | custom-call | flops 1073741824 | tf_op jit(solution)/shard_map/pallas_call | solution.py:260
  80.9 5.6 %collective-permute-start.10 = (bf16[64,2176]{1,0:T(8,128)(2,1)S(1)}, bf16[64,2176]{1,0:T(8,128)(2,1)S(1)}, u32[]{:S(2)}, u32[]{:S(2)}) collective-permute-start(bf16[64,2176]{1,0:T(8,128)(2,1)S(1)} %get-tuple-element.43), channel_id=1, source_target_pairs={{0,194},{2,0},{64,2},{66,64},{128,66},{130,128},{192,130},{194,192... | collective-permute-start | bytes 835592 | tf_op jit(solution)/shard_map/ppermute | solution.py:270
  86.5 6.1 %collective-permute-done.10.high_ref = bf16[64,2176]{1,0:T(8,128)(2,1)S(1)} collective-permute-done((bf16[64,2176]{1,0:T(8,128)(2,1)S(1)}, bf16[64,2176]{1,0:T(8,128)(2,1)S(1)}, u32[]{:S(2)}, u32[]{:S(2)}) %collective-permute-start.10) | collective-permute-done | bytes 278560 | tf_op jit(solution)/shard_map/ppermute | solution.py:270
  92.6 3.1 %collective-permute-done.9.low_ref = bf16[64,2176]{1,0:T(8,128)(2,1)S(1)} collective-permute-done((bf16[64,2176]{1,0:T(8,128)(2,1)S(1)}, bf16[64,2176]{1,0:T(8,128)(2,1)S(1)}, u32[]{:S(2)}, u32[]{:S(2)}) %collective-permute-start.9) | collective-permute-done | bytes 278560 | tf_op jit(solution)/shard_map/ppermute | solution.py:269
  96.6 1.8 %collective-permute-start.11 = (bf16[32,2176]{1,0:T(8,128)(2,1)S(1)}, bf16[32,2176]{1,0:T(8,128)(2,1)S(1)}, u32[]{:S(2)}, u32[]{:S(2)}) collective-permute-start(bf16[32,2176]{1,0:T(8,128)(2,1)S(1)} %get-tuple-element.45), channel_id=1, source_target_pairs={{0,128},{64,192},{128,0},{192,64},{1,129},{65,193},{129,1},{193,65... | collective-permute-start | bytes 417800 | tf_op jit(solution)/shard_map/ppermute | solution.py:280
  98.7 3.3 %collective-permute-start.13 = (bf16[32,2176]{1,0:T(8,128)(2,1)S(1)}, bf16[32,2176]{1,0:T(8,128)(2,1)S(1)}, u32[]{:S(2)}, u32[]{:S(2)}) collective-permute-start(bf16[32,2176]{1,0:T(8,128)(2,1)S(1)} %get-tuple-element.47), channel_id=1, source_target_pairs={{0,192},{64,0},{128,64},{192,128},{1,193},{65,1},{129,65},{193,129... | collective-permute-start | bytes 417800 | tf_op jit(solution)/shard_map/ppermute | solution.py:280
  102.2 8.2 %collective-permute-done.11.g1_ref = bf16[32,2176]{1,0:T(8,128)(2,1)S(1)} collective-permute-done((bf16[32,2176]{1,0:T(8,128)(2,1)S(1)}, bf16[32,2176]{1,0:T(8,128)(2,1)S(1)}, u32[]{:S(2)}, u32[]{:S(2)}) %collective-permute-start.11) | collective-permute-done | bytes 139296 | tf_op jit(solution)/shard_map/ppermute | solution.py:280
  110.3 2.8 %collective-permute-done.13.g3_ref = bf16[32,2176]{1,0:T(8,128)(2,1)S(1)} collective-permute-done((bf16[32,2176]{1,0:T(8,128)(2,1)S(1)}, bf16[32,2176]{1,0:T(8,128)(2,1)S(1)}, u32[]{:S(2)}, u32[]{:S(2)}) %collective-permute-start.13) | collective-permute-done | bytes 139296 | tf_op jit(solution)/shard_map/ppermute | solution.py:280
  113.4 1.3 collective-permute-start.14
  114.7 2.9 %collective-permute-start.15 = (bf16[32,2176]{1,0:T(8,128)(2,1)S(1)}, bf16[32,2176]{1,0:T(8,128)(2,1)S(1)}, u32[]{:S(2)}, u32[]{:S(2)}) collective-permute-start(bf16[32,2176]{1,0:T(8,128)(2,1)S(1)} %shard_map.94.r0_ref), channel_id=1, source_target_pairs={{0,128},{64,192},{128,0},{192,64},{1,129},{65,193},{129,1},{193,65... | collective-permute-start | bytes 417800 | tf_op jit(solution)/shard_map/ppermute | solution.py:282
  117.6 1.5 %collective-permute-start.16 = (bf16[32,2176]{1,0:T(8,128)(2,1)S(1)}, bf16[32,2176]{1,0:T(8,128)(2,1)S(1)}, u32[]{:S(2)}, u32[]{:S(2)}) collective-permute-start(bf16[32,2176]{1,0:T(8,128)(2,1)S(1)} %shard_map.94.r0_ref), channel_id=1, source_target_pairs={{0,192},{64,0},{128,64},{192,128},{1,193},{65,1},{129,65},{193,129... | collective-permute-start | bytes 417800 | tf_op jit(solution)/shard_map/ppermute | solution.py:282
  119.6 1.1 collective-permute-done.14.r1_ref
  120.6 9.6 %collective-permute-done.15.r2_ref = bf16[32,2176]{1,0:T(8,128)(2,1)S(1)} collective-permute-done((bf16[32,2176]{1,0:T(8,128)(2,1)S(1)}, bf16[32,2176]{1,0:T(8,128)(2,1)S(1)}, u32[]{:S(2)}, u32[]{:S(2)}) %collective-permute-start.15) | collective-permute-done | bytes 139296 | tf_op jit(solution)/shard_map/ppermute | solution.py:282
  130.2 1.6 %shard_map.95 = (f32[128,1024]{1,0:T(8,128)}, f32[128,1024]{1,0:T(8,128)}, f32[1,128]{1,0:T(1,128)}) custom-call(s32[3]{0:T(128)S(1)} %pad_add_fusion.ids_ref.me_ref, bf16[32,2176]{1,0:T(8,128)(2,1)S(1)} %shard_map.94.r0_ref, bf16[32,2176]{1,0:T(8,128)(2,1)S(1)} %collective-permute-done.14.r1_ref, bf16[32,2176]{1,0:T(8,128)(2,1)S(1)} %collective-permute-done.15.r2_ref, ...), custom_call_target="tpu_custom_call" | custom-call | tf_op jit(solution)/shard_map/pallas_call | solution.py:284
  (35 shorter events, 7.8 us)
Async XLA Ops:
  1.4 1.0 copy-start
  2.4 1.0 copy-start.1
  3.9 16.3 %copy-start.2 = (bf16[64,1024]{1,0:T(8,128)(2,1)S(1)}, bf16[64,1024]{1,0:T(8,128)(2,1)}, u32[]{:S(2)}) copy-start(bf16[64,1024]{1,0:T(8,128)(2,1)} %param.5) | copy-start | bytes 393220
  3.9 30.9 %copy-start.3 = (s32[64]{0:T(128)S(1)}, s32[64]{0:T(128)}, u32[]{:S(2)}) copy-start(s32[64]{0:T(128)} %param.6) | copy-start | bytes 772
  3.9 13.8 %collective-permute-start.3 = (bf16[128,2176]{1,0:T(8,128)(2,1)S(1)}, bf16[128,2176]{1,0:T(8,128)(2,1)S(1)}, u32[]{:S(2)}, u32[]{:S(2)}) collective-permute-start(bf16[128,2176]{1,0:T(8,128)(2,1)S(1)} %shard_map.84), channel_id=1, source_target_pairs={{0,2},{2,0},{1,3},{3,1},{4,6},{6,4},{5,7},{7,5},{8,10},{10,8},{9,1... | collective-permute-start | bytes 1671176 | tf_op jit(solution)/shard_map/ppermute | solution.py:241
  17.8 17.1 %collective-permute-start.4 = (bf16[256,2176]{1,0:T(8,128)(2,1)S(1)}, bf16[256,2176]{1,0:T(8,128)(2,1)S(1)}, u32[]{:S(2)}, u32[]{:S(2)}) collective-permute-start(bf16[256,2176]{1,0:T(8,128)(2,1)S(1)} %pad_maximum_fusion.coef_a_ref), channel_id=1, source_target_pairs={{0,1},{1,0},{2,3},{3,2},{4,5},{5,4},{6,7},{7,6},{8,9},{9,8},{10,11... | collective-permute-start | bytes 3342344 | tf_op jit(solution)/shard_map/ppermute | solution.py:242
  20.2 6.3 %collective-permute-start = (bf16[64,1024]{1,0:T(8,128)(2,1)S(1)}, bf16[64,1024]{1,0:T(8,128)(2,1)S(1)}, u32[]{:S(2)}, u32[]{:S(2)}) collective-permute-start(bf16[64,1024]{1,0:T(8,128)(2,1)S(1)} %copy-done.2), channel_id=1, source_target_pairs={{0,16},{16,32},{32,48},{48,0},{1,17},{17,33},{33,49},{49,1},{2,18}... | collective-permute-start | bytes 393224 | tf_op jit(solution)/shard_map/ppermute | solution.py:236
  21.4 5.1 %collective-permute-start.1 = (bf16[64,1024]{1,0:T(8,128)(2,1)S(1)}, bf16[64,1024]{1,0:T(8,128)(2,1)S(1)}, u32[]{:S(2)}, u32[]{:S(2)}) collective-permute-start(bf16[64,1024]{1,0:T(8,128)(2,1)S(1)} %copy-done.2), channel_id=1, source_target_pairs={{0,48},{16,0},{32,16},{48,32},{1,49},{17,1},{33,17},{49,33},{2,50}... | collective-permute-start | bytes 393224 | tf_op jit(solution)/shard_map/ppermute | solution.py:236
  22.9 7.4 %collective-permute-start.2 = (bf16[64,1024]{1,0:T(8,128)(2,1)S(1)}, bf16[64,1024]{1,0:T(8,128)(2,1)S(1)}, u32[]{:S(2)}, u32[]{:S(2)}) collective-permute-start(bf16[64,1024]{1,0:T(8,128)(2,1)S(1)} %copy-done.2), channel_id=1, source_target_pairs={{0,32},{16,48},{32,0},{48,16},{1,33},{17,49},{33,1},{49,17},{2,34}... | collective-permute-start | bytes 393224 | tf_op jit(solution)/shard_map/ppermute | solution.py:236
  30.3 14.2 %collective-permute-start.7 = (bf16[256,1024]{1,0:T(8,128)(2,1)S(1)}, bf16[256,1024]{1,0:T(8,128)(2,1)S(1)}, u32[]{:S(2)}, u32[]{:S(2)}) collective-permute-start(bf16[256,1024]{1,0:T(8,128)(2,1)S(1)} %constant_dynamic-update-slice_fusion.e_ref.e0), channel_id=1, source_target_pairs={{0,8},{4,12},{8,0},{12,4},{1,9},{5,13},{9,1},{13,5},{2,10},{6,14},... | collective-permute-start | bytes 1572872 | tf_op jit(solution)/shard_map/ppermute | solution.py:238
  33.3 23.0 %collective-permute-start.6 = (bf16[256,1024]{1,0:T(8,128)(2,1)S(1)}, bf16[256,1024]{1,0:T(8,128)(2,1)}, u32[]{:S(2)}, u32[]{:S(2)}) collective-permute-start(bf16[256,1024]{1,0:T(8,128)(2,1)S(1)} %constant_dynamic-update-slice_fusion.e_ref.e0), channel_id=1, source_target_pairs={{0,12},{4,0},{8,4},{12,8},{1,13},{5,1},{9,5},{13,9},{2,14},{6,2},{... | collective-permute-start | bytes 1572872 | tf_op jit(solution)/shard_map/ppermute | solution.py:238
  34.0 24.1 %collective-permute-start.5 = (bf16[256,1024]{1,0:T(8,128)(2,1)S(1)}, bf16[256,1024]{1,0:T(8,128)(2,1)}, u32[]{:S(2)}, u32[]{:S(2)}) collective-permute-start(bf16[256,1024]{1,0:T(8,128)(2,1)S(1)} %constant_dynamic-update-slice_fusion.e_ref.e0), channel_id=1, source_target_pairs={{0,4},{4,8},{8,12},{12,0},{1,5},{5,9},{9,13},{13,1},{2,6},{6,10},{... | collective-permute-start | bytes 1572872 | tf_op jit(solution)/shard_map/ppermute | solution.py:238
  75.8 4.7 %collective-permute-start.8 = (bf16[256,2176]{1,0:T(8,128)(2,1)S(1)}, bf16[256,2176]{1,0:T(8,128)(2,1)S(1)}, u32[]{:S(2)}, u32[]{:S(2)}) collective-permute-start(bf16[256,2176]{1,0:T(8,128)(2,1)S(1)} %get-tuple-element.40), channel_id=1, source_target_pairs={{0,1},{1,0},{2,3},{3,2},{4,5},{5,4},{6,7},{7,6},{8,9},{9,8},{10,11... | collective-permute-start | bytes 3342344 | tf_op jit(solution)/shard_map/ppermute | solution.py:259
  80.9 11.7 %collective-permute-start.10 = (bf16[64,2176]{1,0:T(8,128)(2,1)S(1)}, bf16[64,2176]{1,0:T(8,128)(2,1)S(1)}, u32[]{:S(2)}, u32[]{:S(2)}) collective-permute-start(bf16[64,2176]{1,0:T(8,128)(2,1)S(1)} %get-tuple-element.43), channel_id=1, source_target_pairs={{0,194},{2,0},{64,2},{66,64},{128,66},{130,128},{192,130},{194,192... | collective-permute-start | bytes 835592 | tf_op jit(solution)/shard_map/ppermute | solution.py:270
  86.5 9.2 %collective-permute-start.9 = (bf16[64,2176]{1,0:T(8,128)(2,1)S(1)}, bf16[64,2176]{1,0:T(8,128)(2,1)S(1)}, u32[]{:S(2)}, u32[]{:S(2)}) collective-permute-start(bf16[64,2176]{1,0:T(8,128)(2,1)S(1)} %get-tuple-element.42), channel_id=1, source_target_pairs={{0,2},{2,64},{64,66},{66,128},{128,130},{130,192},{192,194},{194,0... | collective-permute-start | bytes 835592 | tf_op jit(solution)/shard_map/ppermute | solution.py:269
  96.6 13.7 %collective-permute-start.11 = (bf16[32,2176]{1,0:T(8,128)(2,1)S(1)}, bf16[32,2176]{1,0:T(8,128)(2,1)S(1)}, u32[]{:S(2)}, u32[]{:S(2)}) collective-permute-start(bf16[32,2176]{1,0:T(8,128)(2,1)S(1)} %get-tuple-element.45), channel_id=1, source_target_pairs={{0,128},{64,192},{128,0},{192,64},{1,129},{65,193},{129,1},{193,65... | collective-permute-start | bytes 417800 | tf_op jit(solution)/shard_map/ppermute | solution.py:280
  98.5 11.9 %collective-permute-start.12 = (bf16[32,2176]{1,0:T(8,128)(2,1)S(1)}, bf16[32,2176]{1,0:T(8,128)(2,1)S(1)}, u32[]{:S(2)}, u32[]{:S(2)}) collective-permute-start(bf16[32,2176]{1,0:T(8,128)(2,1)S(1)} %get-tuple-element.46), channel_id=1, source_target_pairs={{0,64},{64,128},{128,192},{192,0},{1,65},{65,129},{129,193},{193,1... | collective-permute-start | bytes 417800 | tf_op jit(solution)/shard_map/ppermute | solution.py:280
  98.7 14.4 %collective-permute-start.13 = (bf16[32,2176]{1,0:T(8,128)(2,1)S(1)}, bf16[32,2176]{1,0:T(8,128)(2,1)S(1)}, u32[]{:S(2)}, u32[]{:S(2)}) collective-permute-start(bf16[32,2176]{1,0:T(8,128)(2,1)S(1)} %get-tuple-element.47), channel_id=1, source_target_pairs={{0,192},{64,0},{128,64},{192,128},{1,193},{65,1},{129,65},{193,129... | collective-permute-start | bytes 417800 | tf_op jit(solution)/shard_map/ppermute | solution.py:280
  113.4 7.3 %collective-permute-start.14 = (bf16[32,2176]{1,0:T(8,128)(2,1)S(1)}, bf16[32,2176]{1,0:T(8,128)(2,1)S(1)}, u32[]{:S(2)}, u32[]{:S(2)}) collective-permute-start(bf16[32,2176]{1,0:T(8,128)(2,1)S(1)} %shard_map.94.r0_ref), channel_id=1, source_target_pairs={{0,64},{64,128},{128,192},{192,0},{1,65},{65,129},{129,193},{193,1... | collective-permute-start | bytes 417800 | tf_op jit(solution)/shard_map/ppermute | solution.py:282
  114.7 15.5 %collective-permute-start.15 = (bf16[32,2176]{1,0:T(8,128)(2,1)S(1)}, bf16[32,2176]{1,0:T(8,128)(2,1)S(1)}, u32[]{:S(2)}, u32[]{:S(2)}) collective-permute-start(bf16[32,2176]{1,0:T(8,128)(2,1)S(1)} %shard_map.94.r0_ref), channel_id=1, source_target_pairs={{0,128},{64,192},{128,0},{192,64},{1,129},{65,193},{129,1},{193,65... | collective-permute-start | bytes 417800 | tf_op jit(solution)/shard_map/ppermute | solution.py:282
  117.6 12.6 %collective-permute-start.16 = (bf16[32,2176]{1,0:T(8,128)(2,1)S(1)}, bf16[32,2176]{1,0:T(8,128)(2,1)S(1)}, u32[]{:S(2)}, u32[]{:S(2)}) collective-permute-start(bf16[32,2176]{1,0:T(8,128)(2,1)S(1)} %shard_map.94.r0_ref), channel_id=1, source_target_pairs={{0,192},{64,0},{128,64},{192,128},{1,193},{65,1},{129,65},{193,129... | collective-permute-start | bytes 417800 | tf_op jit(solution)/shard_map/ppermute | solution.py:282

commit v3 on v2

--- a/solution.py
+++ b/solution.py
@@ -12,24 +12,29 @@
 BF16 = jnp.bfloat16
 EXT = 128
 VMEM = pl.BlockSpec(memory_space=pltpu.VMEM)
-SMEM = pl.BlockSpec(memory_space=pltpu.SMEM)
 NT = (((1,), (1,)), ((), ()))
 SHIFTS = (0, 1, 3, 2)
+SLOTS = (
+    tuple((s, 0) for s in SHIFTS),
+    ((0, 1), (0, 3), (1, 1), (1, 3)),
+    ((3, 1), (3, 3), (2, 1), (2, 3)),
+    tuple((s, 2) for s in SHIFTS),
+)
 INTERPRET = False
 
 
-def call(kernel, out_shape, n_in, flops=0, nbytes=0, smem=(), **kw):
+def call(kernel, out_shape, n_in, flops=0, nbytes=0, **kw):
     many = isinstance(out_shape, (list, tuple))
     n_out = len(out_shape) if many else 1
     specs = dict(
-        in_specs=[SMEM if i in smem else VMEM for i in range(n_in)],
+        in_specs=[VMEM] * n_in,
         out_specs=[VMEM] * n_out if many else VMEM,
     )
     specs.update(kw)
     return pl.pallas_call(
         kernel,
         out_shape=out_shape,
-        compiler_params=pltpu.CompilerParams(vmem_limit_bytes=40 * 2**20),
+        compiler_params=pltpu.CompilerParams(vmem_limit_bytes=16 * 2**20),
         cost_estimate=pl.CostEstimate(flops=flops, bytes_accessed=nbytes, transcendentals=0),
         interpret=INTERPRET,
         **specs,
@@ -69,8 +74,10 @@
     prec = 1.0 / v
     out_ref[:, :width] = (-0.5 * prec).astype(BF16)
     out_ref[:, width : 2 * width] = (m * prec).astype(BF16)
+    down = lax.broadcasted_iota(jnp.int32, (rows, rows), 0)
+    across = lax.broadcasted_iota(jnp.int32, (rows, rows), 1)
     offset = (
-        w_ref[...]
+        jnp.sum(jnp.where(down == across, w_ref[...], 0.0), axis=1, keepdims=True)
         - 0.5 * jnp.sum(m * m * prec + jnp.log(v), axis=1, keepdims=True)
         - 0.5 * width * math.log(2.0 * math.pi)
     )
@@ -82,40 +89,46 @@
     return (wide * wide).astype(BF16)
 
 
-def slot(ids_ref, piece, k):
-    return lax.rem(ids_ref[0] + 4 - SHIFTS[k], 4) * 4 + lax.rem(ids_ref[1] + 4 - SHIFTS[piece], 4)
-
-
-def score_kernel(e_ref, coef_a_ref, coef_b_ref, s_a_ref, s_b_ref, lse_ref):
-    width = e_ref.shape[1]
-    rows = e_ref[...]
-    squares = square(rows)
-    tops = []
-    for coef_ref, s_ref in ((coef_a_ref, s_a_ref), (coef_b_ref, s_b_ref)):
-        s = lax.dot_general(coef_ref[:, :width], squares, NT, preferred_element_type=F32)
-        s = s + lax.dot_general(coef_ref[:, width : 2 * width], rows, NT, preferred_element_type=F32)
-        s = s + jnp.sum(coef_ref[:, 2 * width :].astype(F32), axis=1, keepdims=True)
-        s_ref[...] = s
-        tops.append(jnp.max(s, axis=0, keepdims=True))
-    top = jnp.maximum(*tops)
-    total = sum(jnp.sum(jnp.exp(ref[...] - top), axis=0, keepdims=True) for ref in (s_a_ref, s_b_ref))
-    lse_ref[...] = top + jnp.log(total)
-
-
-def pay_kernel(ids_ref, keep_ref, l0_ref, l1_ref, l2_ref, l3_ref, pay_ref):
+def slot(group, k):
+    back_x, back_y = SLOTS[group][k]
+    x, y = lax.axis_index("x"), lax.axis_index("y")
+    return lax.rem(x + 4 - back_x, 4) * 4 + lax.rem(y + 4 - back_y, 4)
+
+
+def joined(refs):
+    return refs[0][...] if len(refs) == 1 else jnp.concatenate([r[...] for r in refs], axis=0)
+
+
+def score_kernel(*refs):
+    *e_refs, coef_ref, s_ref, lse_ref = refs
+    rows = joined(e_refs)
+    width = rows.shape[1]
+    s = lax.dot_general(coef_ref[:, :width], square(rows), NT, preferred_element_type=F32)
+    s = s + lax.dot_general(coef_ref[:, width : 2 * width], rows, NT, preferred_element_type=F32)
+    s = s + jnp.sum(coef_ref[:, 2 * width :].astype(F32), axis=1, keepdims=True)
+    s_ref[...] = s
+    top = jnp.max(s, axis=0, keepdims=True)
+    lse_ref[...] = top + jnp.log(jnp.sum(jnp.exp(s - top), axis=0, keepdims=True))
+
+
+def pay_kernel(keep_ref, *refs):
+    *lse_refs, pay_ref = refs
     lane = lax.broadcasted_iota(jnp.int32, (1, 128), 1)
-    for piece, ref in enumerate((l0_ref, l1_ref, l2_ref, l3_ref)):
+    for group in range(4):
+        a, b = lse_refs[group][...], lse_refs[4 + group][...]
+        top = jnp.maximum(a, b)
+        both = top + jnp.log(jnp.exp(a - top) + jnp.exp(b - top))
         for k in range(4):
-            row = ref[:, (k // 2) * 128 : (k // 2 + 1) * 128]
+            row = both[:, (k // 2) * 128 : (k // 2 + 1) * 128]
             if k % 2:
                 row = pltpu.roll(row, 64, 1)
-            pay_ref[pl.ds(slot(ids_ref, piece, k), 1), :] = jnp.where(lane < 64, row, 0.0)
+            pay_ref[pl.ds(slot(group, k), 1), :] = jnp.where(lane < 64, row, 0.0)
     pay_ref[0:1, :] = jnp.where(lane < 64, pay_ref[0:1, :], keep_ref[...])
 
 
-def moment_body(ids_ref, pay_ref, lse_ref, s_refs, e_refs, out_ref):
+def moment_body(pay_ref, lse_ref, s_refs, e_refs, out_ref):
     comps = s_refs[0].shape[0]
-    width = e_refs[0].shape[1]
+    width = e_refs[0][0].shape[1]
     pay = pay_ref[...]
     top = jnp.max(pay, axis=0)
     lse_ref[...] = top + jnp.log(jnp.sum(jnp.exp(pay - top[None]), axis=0))
@@ -123,10 +136,10 @@
     total = jnp.zeros((comps, 128), F32)
     kept = jnp.zeros((1, 128), F32)
     second = first = None
-    for piece, (s_ref, e_ref) in enumerate(zip(s_refs, e_refs, strict=True)):
+    for group, (s_ref, e_group) in enumerate(zip(s_refs, e_refs, strict=True)):
         ps = []
         for j in range(2):
-            at = [slot(ids_ref, piece, 2 * j + i) for i in range(2)]
+            at = [slot(group, 2 * j + i) for i in range(2)]
             left, right = (lse_ref[pl.ds(i, 1), :] for i in at)
             lse = jnp.where(lane < 64, left, pltpu.roll(right, 64, 1))
             left, right = (pay_ref[i, 0:1, :] for i in at)
@@ -136,11 +149,11 @@
             kept = kept + keep
             ps.append(p)
         p = jnp.concatenate(ps, axis=1)
-        rows = e_ref[...]
+        rows = joined(e_group)
         add2 = jnp.dot(p, square(rows), preferred_element_type=F32)
         add1 = jnp.dot(p, rows, preferred_element_type=F32)
-        second = add2 if piece == 0 else second + add2
-        first = add1 if piece == 0 else first + add1
+        second = add2 if group == 0 else second + add2
+        first = add1 if group == 0 else first + add1
     counts = jnp.sum(total, axis=1, keepdims=True)
     kept = jnp.broadcast_to(jnp.sum(kept, axis=1, keepdims=True), (comps, 1))
     zero = jnp.zeros_like(counts)
@@ -152,13 +165,22 @@
     out_ref[:, 2 * width :] = ext
 
 
-def moment_kernel_b(ids_ref, pay_ref, s0, s1, s2, s3, e0, e1, e2, e3, out_ref, own_ref, lse_ref):
-    moment_body(ids_ref, pay_ref, lse_ref, (s0, s1, s2, s3), (e0, e1, e2, e3), out_ref)
-    own_ref[...] = lse_ref[pl.ds(slot(ids_ref, 0, 0), 1), :]
-
-
-def moment_kernel(ids_ref, pay_ref, s0, s1, s2, s3, e0, e1, e2, e3, out_ref, lse_ref):
-    moment_body(ids_ref, pay_ref, lse_ref, (s0, s1, s2, s3), (e0, e1, e2, e3), out_ref)
+def moment_refs(refs):
+    pay_ref, s0, s1, s2, s3, e0, e1, e2, e3, e4, e5 = refs
+    return pay_ref, (s0, s1, s2, s3), ((e0,), (e1, e2), (e3, e4), (e5,))
+
+
+def moment_kernel_b(*refs):
+    *refs, out_ref, own_ref, lse_ref = refs
+    pay_ref, s_refs, e_refs = moment_refs(refs)
+    moment_body(pay_ref, lse_ref, s_refs, e_refs, out_ref)
+    own_ref[...] = lse_ref[pl.ds(slot(0, 0), 1), :]
+
+
+def moment_kernel(*refs):
+    *refs, out_ref, lse_ref = refs
+    pay_ref, s_refs, e_refs = moment_refs(refs)
+    moment_body(pay_ref, lse_ref, s_refs, e_refs, out_ref)
 
 
 def to_bf16(out_ref, total):
@@ -176,12 +198,12 @@
         to_bf16(ref, own_ref[at, :] + got_ref[at, :].astype(F32))
 
 
-def pair_sum_kernel(me_ref, mine_ref, low_ref, high_ref, own_ref, s1_ref, s2_ref, s3_ref, all_ref):
+def pair_sum_kernel(mine_ref, low_ref, high_ref, own_ref, s1_ref, s2_ref, s3_ref, all_ref):
     half = low_ref.shape[0]
     quarter = own_ref.shape[0]
     all_ref[:half, :] = mine_ref[:half, :] + low_ref[...].astype(F32)
     all_ref[half:, :] = mine_ref[half:, :] + high_ref[...].astype(F32)
-    me = me_ref[2]
+    me = lax.axis_index("zh")
 
     def rows(shift):
         return all_ref[pl.ds(lax.rem(me + shift, 4) * quarter, quarter), :]
@@ -208,10 +230,10 @@
     out_ref[:, 2 * width :] = lanes(parts(log_w, 3), rows).astype(BF16)
 
 
-def place_kernel(me_ref, r0_ref, r1_ref, r2_ref, r3_ref, mean_ref, var_ref, log_ref, ext_ref):
+def place_kernel(r0_ref, r2_ref, r1_ref, r3_ref, mean_ref, var_ref, log_ref, ext_ref):
     quarter = r0_ref.shape[0]
     width = mean_ref.shape[1]
-    me = me_ref[2]
+    me = lax.axis_index("zh")
     for shift, ref in enumerate((r0_ref, r1_ref, r2_ref, r3_ref)):
         at = pl.ds(lax.rem(me + 4 - shift, 4) * quarter, quarter)
         mean_ref[at, :] = ref[:, :width].astype(F32)
@@ -231,34 +253,47 @@
     n_comps = comps * 64
     cols = 2 * width + EXT
     plane, z, core = ("x", "y"), ("zh", "zl"), "c"
-    ids = jnp.stack([lax.axis_index(a) for a in ("x", "y", "zh")]).astype(jnp.int32)
-
+
+    back_y = [lax.ppermute(embeddings, "y", ring(4, s)) for s in (1, 3)]
     line = [embeddings] + [lax.ppermute(embeddings, "x", ring(4, s)) for s in SHIFTS[1:]]
     line = jnp.concatenate(line, axis=0)
-    pieces = [line] + [lax.ppermute(line, "y", ring(4, s)) for s in SHIFTS[1:]]
-
-    coef = call(coef_kernel, sds((comps, cols), BF16), 3)(means, variances, log_weights[:, None])
+    pair = jnp.concatenate(back_y, axis=0)
+
+    coef = call(coef_kernel, sds((comps, cols), BF16), 3, 4 * 2**20, 2 * 2**20)(
+        means, variances, log_weights[None, :]
+    )
+    coef, pair = lax.optimization_barrier((coef, pair))
     coef_a = jnp.concatenate([coef, lax.ppermute(coef, "zl", ring(2, 1))], axis=0)
+    far = lax.ppermute(line, "y", ring(4, 2))
+    rest = [lax.ppermute(pair, "x", ring(4, s)) for s in SHIFTS[1:]]
+    coef_a, far, rest = lax.optimization_barrier((coef_a, far, rest))
     coef_b = lax.ppermute(coef_a, core, ring(2, 1))
 
+    groups = [[line], [pair, rest[0]], [rest[1], rest[2]], [far]]
+    pieces = [e for group in groups for e in group]
     tile = 4 * own
     flops = 2 * 2 * comps * tile * 2 * width
     half_s = sds((2 * comps, tile), F32)
-    scores = [
-        call(score_kernel, (half_s, half_s, sds((1, tile), F32)), 3, 2 * flops)(p, coef_a, coef_b)
-        for p in pieces
-    ]
+    scores_a, scores_b = (
+        [
+            call(score_kernel, (half_s, sds((1, tile), F32)), 1 + len(group), flops)(*group, coef)
+            for group in groups
+        ]
+        for coef in (coef_a, coef_b)
+    )
     flag = jnp.pad(keep.astype(F32), (own, 0)).reshape(1, 2 * own)
-    pay = call(pay_kernel, sds((16, 128), F32), 6, smem=(0,))(ids, flag, *[s[2] for s in scores])
+    pay = call(pay_kernel, sds((16, 128), F32), 9)(
+        flag, *[s[1] for s in scores_a + scores_b]
+    )
     pays = lax.all_to_all(jnp.broadcast_to(pay[None], (16,) + pay.shape), plane, 0, 0)
 
-    lse_scratch = dict(smem=(0,), scratch_shapes=[pltpu.VMEM((16, 128), F32)])
+    lse_scratch = dict(scratch_shapes=[pltpu.VMEM((16, 128), F32)])
     send, own_lse = call(
-        moment_kernel_b, (sds((2 * comps, cols), BF16), sds((1, 128), F32)), 10, 4 * flops, **lse_scratch
-    )(ids, pays, *[s[1] for s in scores], *pieces)
+        moment_kernel_b, (sds((2 * comps, cols), BF16), sds((1, 128), F32)), 11, 4 * flops, **lse_scratch
+    )(pays, *[s[0] for s in scores_b], *pieces)
     got = lax.ppermute(send, core, ring(2, 1))
-    own_sum = call(moment_kernel, sds((2 * comps, cols), F32), 10, 4 * flops, **lse_scratch)(
-        ids, pays, *[s[0] for s in scores], *pieces
+    own_sum = call(moment_kernel, sds((2 * comps, cols), F32), 11, 4 * flops, **lse_scratch)(
+        pays, *[s[0] for s in scores_a], *pieces
     )
     half = comps // 2
     up, down, mine = call(
@@ -273,10 +308,9 @@
     own_q, s1, s2, s3 = call(
         pair_sum_kernel,
         (q32, q16, q16, q16),
-        4,
-        smem=(0,),
+        3,
         scratch_shapes=[pltpu.VMEM((comps, cols), F32)],
-    )(ids, mine, low, high)
+    )(mine, low, high)
     g = [lax.ppermute(s, "zh", ring(4, i)) for i, s in ((2, s2), (1, s1), (3, s3))]
     result = call(functools.partial(finish_kernel, n_comps), q16, 4)(own_q, *g)
     r2, r1, r3 = [lax.ppermute(result, "zh", ring(4, s)) for s in (2, 1, 3)]
@@ -284,10 +318,9 @@
     new_means, new_vars, new_log = call(
         place_kernel,
         (out, out, sds((1, comps), F32)),
-        5,
-        smem=(0,),
+        4,
         scratch_shapes=[pltpu.VMEM((comps, EXT), F32)],
-    )(ids, result, r1, r2, r3)
+    )(result, r2, r1, r3)
 
     wide = embeddings.astype(F32)
     own_norm = 0.5 * jnp.sum(wide * wide, axis=1) + 0.5 * width * math.log(2.0 * math.pi)

time: 132 us -> 103 us (0.78)
  the two profiles are of different devices: /device:TPU:1 before, /device:TPU:32 now
where the time goes in v3:
time: 103 us; the launch traced here: 102 us
  waiting for transfers between devices  41.6 us (40%)
  starting transfers between devices  32.9 us (32%)
  blocking collectives  12.9 us (13%)
  Pallas kernels  9.89 us (10%)
  local copies, waits for them, and re-layouts  3.23 us (3%)
    all_to_all x1, blocking collectives, local(): lax.all_to_all(jnp.broadcast_to(pay[None], (16,) + pay.shape), plane, 0, 0)  12.9 us
    ppermute x3, waiting for transfers between devices, local(): r2, r1, r3 = [lax.ppermute(result, 'zh', ring(4, s)) for s in (2, 1, 3)]  10.2 us
    ppermute x3, waiting for transfers between devices, local(): lax.ppermute(s, 'zh', ring(4, i))  9.94 us
    ppermute x3, starting transfers between devices, local(): lax.ppermute(s, 'zh', ring(4, i))  9.44 us
    ppermute x3, starting transfers between devices, local(): r2, r1, r3 = [lax.ppermute(result, 'zh', ring(4, s)) for s in (2, 1, 3)]  6.98 us
    ppermute x1, waiting for transfers between devices, local(): low = lax.ppermute(up, z, ring(8, 1))  6.67 us
    ppermute x1, waiting for transfers between devices, local(): lax.ppermute(coef, 'zl', ring(2, 1))  5.49 us
    ppermute x3, starting transfers between devices, local(): lax.ppermute(embeddings, 'x', ring(4, s))  5.05 us
  transfers between devices with their start and end apart: 20, of which 10 were waited for; matrix products, arithmetic and copies ran while one was open for 1% of the time, Pallas kernels for 4%

profile of v3, /device:TPU:32, one launch (start us, length us, event | category | flops | bytes accessed | tf_op | source)
XLA Modules:
  0.0 102.1 jit_solution(7219589678635973532)
XLA Ops:
  0.6 1.7 %collective-permute-start.3 = (bf16[64,1024]{1,0:T(8,128)(2,1)}, bf16[64,1024]{1,0:T(8,128)(2,1)S(1)}, u32[]{:S(2)}, u32[]{:S(2)}) collective-permute-start(bf16[64,1024]{1,0:T(8,128)(2,1)} %param.5), channel_id=1, source_target_pairs={{0,4},{4,8},{8,12},{12,0},{1,5},{5,9},{9,13},{13,1},{2,6},{6,10},{... | collective-permute-start | bytes 393224 | tf_op jit(solution)/shard_map/ppermute | solution.py:257
  2.3 1.7 %collective-permute-start.4 = (bf16[64,1024]{1,0:T(8,128)(2,1)}, bf16[64,1024]{1,0:T(8,128)(2,1)S(1)}, u32[]{:S(2)}, u32[]{:S(2)}) collective-permute-start(bf16[64,1024]{1,0:T(8,128)(2,1)} %param.5), channel_id=1, source_target_pairs={{0,12},{4,0},{8,4},{12,8},{1,13},{5,1},{9,5},{13,9},{2,14},{6,2},{... | collective-permute-start | bytes 393224 | tf_op jit(solution)/shard_map/ppermute | solution.py:257
  3.9 1.5 %collective-permute-start = (bf16[64,1024]{1,0:T(8,128)(2,1)}, bf16[64,1024]{1,0:T(8,128)(2,1)S(1)}, u32[]{:S(2)}, u32[]{:S(2)}) collective-permute-start(bf16[64,1024]{1,0:T(8,128)(2,1)} %param.5), channel_id=1, source_target_pairs={{0,16},{16,32},{32,48},{48,0},{1,17},{17,33},{33,49},{49,1},{2,18}... | collective-permute-start | bytes 393224 | tf_op jit(solution)/shard_map/ppermute | solution.py:258
  5.4 1.7 %collective-permute-start.1 = (bf16[64,1024]{1,0:T(8,128)(2,1)}, bf16[64,1024]{1,0:T(8,128)(2,1)S(1)}, u32[]{:S(2)}, u32[]{:S(2)}) collective-permute-start(bf16[64,1024]{1,0:T(8,128)(2,1)} %param.5), channel_id=1, source_target_pairs={{0,48},{16,0},{32,16},{48,32},{1,49},{17,1},{33,17},{49,33},{2,50}... | collective-permute-start | bytes 393224 | tf_op jit(solution)/shard_map/ppermute | solution.py:258
  7.2 1.8 %collective-permute-start.2 = (bf16[64,1024]{1,0:T(8,128)(2,1)}, bf16[64,1024]{1,0:T(8,128)(2,1)S(1)}, u32[]{:S(2)}, u32[]{:S(2)}) collective-permute-start(bf16[64,1024]{1,0:T(8,128)(2,1)} %param.5), channel_id=1, source_target_pairs={{0,32},{16,48},{32,0},{48,16},{1,33},{17,49},{33,1},{49,17},{2,34}... | collective-permute-start | bytes 393224 | tf_op jit(solution)/shard_map/ppermute | solution.py:258
  9.0 1.0 %copy-done = f32[128,1024]{1,0:T(8,128)S(1)} copy-done((f32[128,1024]{1,0:T(8,128)S(1)}, f32[128,1024]{1,0:T(8,128)}, u32[]{:S(2)}) %copy-start) | copy-done | bytes 524312
  10.0 1.0 %copy-done.1 = f32[128,1024]{1,0:T(8,128)S(1)} copy-done((f32[128,1024]{1,0:T(8,128)S(1)}, f32[128,1024]{1,0:T(8,128)}, u32[]{:S(2)}) %copy-start.1) | copy-done | bytes 524312
  11.1 0.7 copy-done.2
  12.7 1.4 %collective-permute-done.2 = bf16[64,1024]{1,0:T(8,128)(2,1)S(1)} collective-permute-done((bf16[64,1024]{1,0:T(8,128)(2,1)}, bf16[64,1024]{1,0:T(8,128)(2,1)S(1)}, u32[]{:S(2)}, u32[]{:S(2)}) %collective-permute-start.2) | collective-permute-done | bytes 131104 | tf_op jit(solution)/shard_map/ppermute | solution.py:258
  14.2 2.1 %collective-permute-start.6 = (bf16[256,1024]{1,0:T(8,128)(2,1)S(1)}, bf16[256,1024]{1,0:T(8,128)(2,1)S(1)}, u32[]{:S(2)}, u32[]{:S(2)}) collective-permute-start(bf16[256,1024]{1,0:T(8,128)(2,1)S(1)} %constant_dynamic-update-slice_fusion.refs_0_.refs_5_), channel_id=1, source_target_pairs={{0,8},{4,12},{8,0},{12,4},{1,9},{5,13},{9,1},{13,5},{2,10},{6,14},... | collective-permute-start | bytes 1572872 | tf_op jit(solution)/shard_map/ppermute | solution.py:267
  16.2 0.8 collective-permute-start.7
  17.1 2.4 %collective-permute-start.8 = (bf16[128,1024]{1,0:T(8,128)(2,1)S(1)}, bf16[128,1024]{1,0:T(8,128)(2,1)S(1)}, u32[]{:S(2)}, u32[]{:S(2)}) collective-permute-start(bf16[128,1024]{1,0:T(8,128)(2,1)S(1)} %pad_maximum_fusion.1.refs_0_.refs_6_), channel_id=1, source_target_pairs={{0,48},{16,0},{32,16},{48,32},{1,49},{17,1},{33,17},{49,33},{2,50}... | collective-permute-start | bytes 786440 | tf_op jit(solution)/shard_map/ppermute | solution.py:268
  19.8 5.5 %collective-permute-done.5 = bf16[128,2176]{1,0:T(8,128)(2,1)S(1)} collective-permute-done((bf16[128,2176]{1,0:T(8,128)(2,1)S(1)}, bf16[128,2176]{1,0:T(8,128)(2,1)S(1)}, u32[]{:S(2)}, u32[]{:S(2)}) %collective-permute-start.5) | collective-permute-done | bytes 557088 | tf_op jit(solution)/shard_map/ppermute | solution.py:266
  25.4 4.5 %collective-permute-done.7.refs_1_.refs_7_ = bf16[128,1024]{1,0:T(8,128)(2,1)S(1)} collective-permute-done((bf16[128,1024]{1,0:T(8,128)(2,1)S(1)}, bf16[128,1024]{1,0:T(8,128)(2,1)S(1)}, u32[]{:S(2)}, u32[]{:S(2)}) %collective-permute-start.7) | collective-permute-done | bytes 262176 | tf_op jit(solution)/shard_map/ppermute | solution.py:268
  31.7 0.5 shard_map.87
  35.1 12.9 %all_to_all.5.refs_0_ = f32[16,16,128]{2,1,0:T(8,128)S(1)} all-to-all(f32[16,16,128]{2,1,0:T(8,128)S(1)} %broadcast_in_dim.10), channel_id=1, replica_groups=mesh['zh'=4,'x'=4,'y'=4,'zl'=2,'c'=2] {'x','y'}, dimensions={0} | all-to-all | bytes 262144 | tf_op jit(solution)/shard_map/all_to_all | solution.py:288
  47.9 1.6 %shard_map.95 = (bf16[256,2176]{1,0:T(8,128)(2,1)S(1)}, f32[1,128]{1,0:T(1,128)S(1)}) custom-call(f32[16,16,128]{2,1,0:T(8,128)S(1)} %all_to_all.5.refs_0_, f32[256,256]{1,0:T(8,128)S(1)} %get-tuple-element.58.refs_1_, f32[256,256]{1,0:T(8,128)S(1)} %get-tuple-element.59.refs_2_, f32[256,256]{1,0:T(8,128)S(1)} %get-tuple-element.60.refs_3_, ...), custom_call_target="tpu_custom_call" | custom-call | flops 1073741824 | tf_op jit(solution)/shard_map/pallas_call | solution.py:291
  49.6 1.6 %shard_map.94.own_ref = f32[256,2176]{1,0:T(8,128)S(1)} custom-call(f32[16,16,128]{2,1,0:T(8,128)S(1)} %all_to_all.5.refs_0_, f32[256,256]{1,0:T(8,128)S(1)} %get-tuple-element.54.refs_1_, f32[256,256]{1,0:T(8,128)S(1)} %get-tuple-element.55.refs_2_, f32[256,256]{1,0:T(8,128)S(1)} %get-tuple-element.56.refs_3_, f32[256,256]{1,0:T(8,128)S(1)} %get-tuple-element.57.refs_4_, ...), custom_call_target="tpu_custom_call" | custom-call | flops 1073741824 | tf_op jit(solution)/shard_map/pallas_call | solution.py:295
  51.2 1.2 %collective-permute-done.11.got_ref = bf16[256,2176]{1,0:T(8,128)(2,1)S(1)} collective-permute-done((bf16[256,2176]{1,0:T(8,128)(2,1)S(1)}, bf16[256,2176]{1,0:T(8,128)(2,1)S(1)}, u32[]{:S(2)}, u32[]{:S(2)}) %collective-permute-start.11) | collective-permute-done | bytes 1114144 | tf_op jit(solution)/shard_map/ppermute | solution.py:294
  52.8 2.0 %collective-permute-start.12 = (bf16[64,2176]{1,0:T(8,128)(2,1)S(1)}, bf16[64,2176]{1,0:T(8,128)(2,1)S(1)}, u32[]{:S(2)}, u32[]{:S(2)}) collective-permute-start(bf16[64,2176]{1,0:T(8,128)(2,1)S(1)} %get-tuple-element.64), channel_id=1, source_target_pairs={{0,2},{2,64},{64,66},{66,128},{128,130},{130,192},{192,194},{194,0... | collective-permute-start | bytes 835592 | tf_op jit(solution)/shard_map/ppermute | solution.py:304
  54.9 6.7 %collective-permute-done.12.low_ref = bf16[64,2176]{1,0:T(8,128)(2,1)S(1)} collective-permute-done((bf16[64,2176]{1,0:T(8,128)(2,1)S(1)}, bf16[64,2176]{1,0:T(8,128)(2,1)S(1)}, u32[]{:S(2)}, u32[]{:S(2)}) %collective-permute-start.12) | collective-permute-done | bytes 278560 | tf_op jit(solution)/shard_map/ppermute | solution.py:304
  61.5 1.8 %collective-permute-done.13.high_ref = bf16[64,2176]{1,0:T(8,128)(2,1)S(1)} collective-permute-done((bf16[64,2176]{1,0:T(8,128)(2,1)S(1)}, bf16[64,2176]{1,0:T(8,128)(2,1)S(1)}, u32[]{:S(2)}, u32[]{:S(2)}) %collective-permute-start.13) | collective-permute-done | bytes 278560 | tf_op jit(solution)/shard_map/ppermute | solution.py:305
  63.7 5.3 %collective-permute-start.14 = (bf16[32,2176]{1,0:T(8,128)(2,1)S(1)}, bf16[32,2176]{1,0:T(8,128)(2,1)S(1)}, u32[]{:S(2)}, u32[]{:S(2)}) collective-permute-start(bf16[32,2176]{1,0:T(8,128)(2,1)S(1)} %get-tuple-element.67), channel_id=1, source_target_pairs={{0,128},{64,192},{128,0},{192,64},{1,129},{65,193},{129,1},{193,65... | collective-permute-start | bytes 417800 | tf_op jit(solution)/shard_map/ppermute | solution.py:314
  69.0 2.0 %collective-permute-start.15 = (bf16[32,2176]{1,0:T(8,128)(2,1)S(1)}, bf16[32,2176]{1,0:T(8,128)(2,1)S(1)}, u32[]{:S(2)}, u32[]{:S(2)}) collective-permute-start(bf16[32,2176]{1,0:T(8,128)(2,1)S(1)} %get-tuple-element.68), channel_id=1, source_target_pairs={{0,64},{64,128},{128,192},{192,0},{1,65},{65,129},{129,193},{193,1... | collective-permute-start | bytes 417800 | tf_op jit(solution)/shard_map/ppermute | solution.py:314
  71.0 2.1 %collective-permute-start.16 = (bf16[32,2176]{1,0:T(8,128)(2,1)S(1)}, bf16[32,2176]{1,0:T(8,128)(2,1)S(1)}, u32[]{:S(2)}, u32[]{:S(2)}) collective-permute-start(bf16[32,2176]{1,0:T(8,128)(2,1)S(1)} %get-tuple-element.69), channel_id=1, source_target_pairs={{0,192},{64,0},{128,64},{192,128},{1,193},{65,1},{129,65},{193,129... | collective-permute-start | bytes 417800 | tf_op jit(solution)/shard_map/ppermute | solution.py:314
  73.2 9.9 %collective-permute-done.15.g2_ref = bf16[32,2176]{1,0:T(8,128)(2,1)S(1)} collective-permute-done((bf16[32,2176]{1,0:T(8,128)(2,1)S(1)}, bf16[32,2176]{1,0:T(8,128)(2,1)S(1)}, u32[]{:S(2)}, u32[]{:S(2)}) %collective-permute-start.15) | collective-permute-done | bytes 139296 | tf_op jit(solution)/shard_map/ppermute | solution.py:314
  83.4 2.8 %collective-permute-start.17 = (bf16[32,2176]{1,0:T(8,128)(2,1)S(1)}, bf16[32,2176]{1,0:T(8,128)(2,1)S(1)}, u32[]{:S(2)}, u32[]{:S(2)}) collective-permute-start(bf16[32,2176]{1,0:T(8,128)(2,1)S(1)} %shard_map.98.r0_ref), channel_id=1, source_target_pairs={{0,128},{64,192},{128,0},{192,64},{1,129},{65,193},{129,1},{193,65... | collective-permute-start | bytes 417800 | tf_op jit(solution)/shard_map/ppermute | solution.py:316
  86.3 0.7 collective-permute-start.18
  87.0 3.4 %collective-permute-start.19 = (bf16[32,2176]{1,0:T(8,128)(2,1)S(1)}, bf16[32,2176]{1,0:T(8,128)(2,1)S(1)}, u32[]{:S(2)}, u32[]{:S(2)}) collective-permute-start(bf16[32,2176]{1,0:T(8,128)(2,1)S(1)} %shard_map.98.r0_ref), channel_id=1, source_target_pairs={{0,192},{64,0},{128,64},{192,128},{1,193},{65,1},{129,65},{193,129... | collective-permute-start | bytes 417800 | tf_op jit(solution)/shard_map/ppermute | solution.py:316
  90.9 6.1 %collective-permute-done.17.r2_ref = bf16[32,2176]{1,0:T(8,128)(2,1)S(1)} collective-permute-done((bf16[32,2176]{1,0:T(8,128)(2,1)S(1)}, bf16[32,2176]{1,0:T(8,128)(2,1)S(1)}, u32[]{:S(2)}, u32[]{:S(2)}) %collective-permute-start.17) | collective-permute-done | bytes 139296 | tf_op jit(solution)/shard_map/ppermute | solution.py:316
  97.1 4.0 %collective-permute-done.18.r1_ref = bf16[32,2176]{1,0:T(8,128)(2,1)S(1)} collective-permute-done((bf16[32,2176]{1,0:T(8,128)(2,1)S(1)}, bf16[32,2176]{1,0:T(8,128)(2,1)S(1)}, u32[]{:S(2)}, u32[]{:S(2)}) %collective-permute-start.18) | collective-permute-done | bytes 139296 | tf_op jit(solution)/shard_map/ppermute | solution.py:316
  101.1 1.0 %shard_map.99 = (f32[128,1024]{1,0:T(8,128)}, f32[128,1024]{1,0:T(8,128)}, f32[1,128]{1,0:T(1,128)}) custom-call(bf16[32,2176]{1,0:T(8,128)(2,1)S(1)} %shard_map.98.r0_ref, bf16[32,2176]{1,0:T(8,128)(2,1)S(1)} %collective-permute-done.17.r2_ref, bf16[32,2176]{1,0:T(8,128)(2,1)S(1)} %collective-permute-done.18.r1_ref, ...), custom_call_target="tpu_custom_call" | custom-call | tf_op jit(solution)/shard_map/pallas_call | solution.py:318
  (46 shorter events, 7.7 us)
Async XLA Ops:
  0.6 11.4 %collective-permute-start.3 = (bf16[64,1024]{1,0:T(8,128)(2,1)}, bf16[64,1024]{1,0:T(8,128)(2,1)S(1)}, u32[]{:S(2)}, u32[]{:S(2)}) collective-permute-start(bf16[64,1024]{1,0:T(8,128)(2,1)} %param.5), channel_id=1, source_target_pairs={{0,4},{4,8},{8,12},{12,0},{1,5},{5,9},{9,13},{13,1},{2,6},{6,10},{... | collective-permute-start | bytes 393224 | tf_op jit(solution)/shard_map/ppermute | solution.py:257
  2.3 9.8 %collective-permute-start.4 = (bf16[64,1024]{1,0:T(8,128)(2,1)}, bf16[64,1024]{1,0:T(8,128)(2,1)S(1)}, u32[]{:S(2)}, u32[]{:S(2)}) collective-permute-start(bf16[64,1024]{1,0:T(8,128)(2,1)} %param.5), channel_id=1, source_target_pairs={{0,12},{4,0},{8,4},{12,8},{1,13},{5,1},{9,5},{13,9},{2,14},{6,2},{... | collective-permute-start | bytes 393224 | tf_op jit(solution)/shard_map/ppermute | solution.py:257
  3.9 8.7 %collective-permute-start = (bf16[64,1024]{1,0:T(8,128)(2,1)}, bf16[64,1024]{1,0:T(8,128)(2,1)S(1)}, u32[]{:S(2)}, u32[]{:S(2)}) collective-permute-start(bf16[64,1024]{1,0:T(8,128)(2,1)} %param.5), channel_id=1, source_target_pairs={{0,16},{16,32},{32,48},{48,0},{1,17},{17,33},{33,49},{49,1},{2,18}... | collective-permute-start | bytes 393224 | tf_op jit(solution)/shard_map/ppermute | solution.py:258
  5.4 7.2 %collective-permute-start.1 = (bf16[64,1024]{1,0:T(8,128)(2,1)}, bf16[64,1024]{1,0:T(8,128)(2,1)S(1)}, u32[]{:S(2)}, u32[]{:S(2)}) collective-permute-start(bf16[64,1024]{1,0:T(8,128)(2,1)} %param.5), channel_id=1, source_target_pairs={{0,48},{16,0},{32,16},{48,32},{1,49},{17,1},{33,17},{49,33},{2,50}... | collective-permute-start | bytes 393224 | tf_op jit(solution)/shard_map/ppermute | solution.py:258
  7.2 6.9 %collective-permute-start.2 = (bf16[64,1024]{1,0:T(8,128)(2,1)}, bf16[64,1024]{1,0:T(8,128)(2,1)S(1)}, u32[]{:S(2)}, u32[]{:S(2)}) collective-permute-start(bf16[64,1024]{1,0:T(8,128)(2,1)} %param.5), channel_id=1, source_target_pairs={{0,32},{16,48},{32,0},{48,16},{1,33},{17,49},{33,1},{49,17},{2,34}... | collective-permute-start | bytes 393224 | tf_op jit(solution)/shard_map/ppermute | solution.py:258
  9.0 1.0 %copy-start = (f32[128,1024]{1,0:T(8,128)S(1)}, f32[128,1024]{1,0:T(8,128)}, u32[]{:S(2)}) copy-start(f32[128,1024]{1,0:T(8,128)} %m_ref.1) | copy-start | bytes 1572868
  10.0 1.0 %copy-start.1 = (f32[128,1024]{1,0:T(8,128)S(1)}, f32[128,1024]{1,0:T(8,128)}, u32[]{:S(2)}) copy-start(f32[128,1024]{1,0:T(8,128)} %v_ref.1) | copy-start | bytes 1572868
  11.1 0.7 copy-start.2
  11.7 0.9 copy-start.3
  12.1 13.2 %collective-permute-start.5 = (bf16[128,2176]{1,0:T(8,128)(2,1)S(1)}, bf16[128,2176]{1,0:T(8,128)(2,1)S(1)}, u32[]{:S(2)}, u32[]{:S(2)}) collective-permute-start(bf16[128,2176]{1,0:T(8,128)(2,1)S(1)} %shard_map.84), channel_id=1, source_target_pairs={{0,2},{2,0},{1,3},{3,1},{4,6},{6,4},{5,7},{7,5},{8,10},{10,8},{9,1... | collective-permute-start | bytes 1671176 | tf_op jit(solution)/shard_map/ppermute | solution.py:266
  14.1 15.9 %copy-start.4 = (s32[64]{0:T(128)S(1)}, s32[64]{0:T(128)}, u32[]{:S(2)}) copy-start(s32[64]{0:T(128)} %param.6) | copy-start | bytes 772
  14.2 15.7 %collective-permute-start.6 = (bf16[256,1024]{1,0:T(8,128)(2,1)S(1)}, bf16[256,1024]{1,0:T(8,128)(2,1)S(1)}, u32[]{:S(2)}, u32[]{:S(2)}) collective-permute-start(bf16[256,1024]{1,0:T(8,128)(2,1)S(1)} %constant_dynamic-update-slice_fusion.refs_0_.refs_5_), channel_id=1, source_target_pairs={{0,8},{4,12},{8,0},{12,4},{1,9},{5,13},{9,1},{13,5},{2,10},{6,14},... | collective-permute-start | bytes 1572872 | tf_op jit(solution)/shard_map/ppermute | solution.py:267
  16.2 13.7 %collective-permute-start.7 = (bf16[128,1024]{1,0:T(8,128)(2,1)S(1)}, bf16[128,1024]{1,0:T(8,128)(2,1)S(1)}, u32[]{:S(2)}, u32[]{:S(2)}) collective-permute-start(bf16[128,1024]{1,0:T(8,128)(2,1)S(1)} %pad_maximum_fusion.1.refs_0_.refs_6_), channel_id=1, source_target_pairs={{0,16},{16,32},{32,48},{48,0},{1,17},{17,33},{33,49},{49,1},{2,18}... | collective-permute-start | bytes 786440 | tf_op jit(solution)/shard_map/ppermute | solution.py:268
  17.1 12.8 %collective-permute-start.8 = (bf16[128,1024]{1,0:T(8,128)(2,1)S(1)}, bf16[128,1024]{1,0:T(8,128)(2,1)S(1)}, u32[]{:S(2)}, u32[]{:S(2)}) collective-permute-start(bf16[128,1024]{1,0:T(8,128)(2,1)S(1)} %pad_maximum_fusion.1.refs_0_.refs_6_), channel_id=1, source_target_pairs={{0,48},{16,0},{32,16},{48,32},{1,49},{17,1},{33,17},{49,33},{2,50}... | collective-permute-start | bytes 786440 | tf_op jit(solution)/shard_map/ppermute | solution.py:268
  19.5 10.4 %collective-permute-start.9 = (bf16[128,1024]{1,0:T(8,128)(2,1)S(1)}, bf16[128,1024]{1,0:T(8,128)(2,1)S(1)}, u32[]{:S(2)}, u32[]{:S(2)}) collective-permute-start(bf16[128,1024]{1,0:T(8,128)(2,1)S(1)} %pad_maximum_fusion.1.refs_0_.refs_6_), channel_id=1, source_target_pairs={{0,32},{16,48},{32,0},{48,16},{1,33},{17,49},{33,1},{49,17},{2,34}... | collective-permute-start | bytes 786440 | tf_op jit(solution)/shard_map/ppermute | solution.py:268
  29.9 2.8 %collective-permute-start.10 = (bf16[256,2176]{1,0:T(8,128)(2,1)S(1)}, bf16[256,2176]{1,0:T(8,128)(2,1)S(1)}, u32[]{:S(2)}, u32[]{:S(2)}) collective-permute-start(bf16[256,2176]{1,0:T(8,128)(2,1)S(1)} %pad_maximum_fusion.refs_1_.refs_2_), channel_id=1, source_target_pairs={{0,1},{1,0},{2,3},{3,2},{4,5},{5,4},{6,7},{7,6},{8,9},{9,8},{10,11... | collective-permute-start | bytes 3342344 | tf_op jit(solution)/shard_map/ppermute | solution.py:270
  49.5 2.8 %collective-permute-start.11 = (bf16[256,2176]{1,0:T(8,128)(2,1)S(1)}, bf16[256,2176]{1,0:T(8,128)(2,1)S(1)}, u32[]{:S(2)}, u32[]{:S(2)}) collective-permute-start(bf16[256,2176]{1,0:T(8,128)(2,1)S(1)} %get-tuple-element.62), channel_id=1, source_target_pairs={{0,1},{1,0},{2,3},{3,2},{4,5},{5,4},{6,7},{7,6},{8,9},{9,8},{10,11... | collective-permute-start | bytes 3342344 | tf_op jit(solution)/shard_map/ppermute | solution.py:294
  52.8 8.8 %collective-permute-start.12 = (bf16[64,2176]{1,0:T(8,128)(2,1)S(1)}, bf16[64,2176]{1,0:T(8,128)(2,1)S(1)}, u32[]{:S(2)}, u32[]{:S(2)}) collective-permute-start(bf16[64,2176]{1,0:T(8,128)(2,1)S(1)} %get-tuple-element.64), channel_id=1, source_target_pairs={{0,2},{2,64},{64,66},{66,128},{128,130},{130,192},{192,194},{194,0... | collective-permute-start | bytes 835592 | tf_op jit(solution)/shard_map/ppermute | solution.py:304
  54.8 8.6 %collective-permute-start.13 = (bf16[64,2176]{1,0:T(8,128)(2,1)S(1)}, bf16[64,2176]{1,0:T(8,128)(2,1)S(1)}, u32[]{:S(2)}, u32[]{:S(2)}) collective-permute-start(bf16[64,2176]{1,0:T(8,128)(2,1)S(1)} %get-tuple-element.65), channel_id=1, source_target_pairs={{0,194},{2,0},{64,2},{66,64},{128,66},{130,128},{192,130},{194,192... | collective-permute-start | bytes 835592 | tf_op jit(solution)/shard_map/ppermute | solution.py:305
  63.7 9.6 %collective-permute-start.14 = (bf16[32,2176]{1,0:T(8,128)(2,1)S(1)}, bf16[32,2176]{1,0:T(8,128)(2,1)S(1)}, u32[]{:S(2)}, u32[]{:S(2)}) collective-permute-start(bf16[32,2176]{1,0:T(8,128)(2,1)S(1)} %get-tuple-element.67), channel_id=1, source_target_pairs={{0,128},{64,192},{128,0},{192,64},{1,129},{65,193},{129,1},{193,65... | collective-permute-start | bytes 417800 | tf_op jit(solution)/shard_map/ppermute | solution.py:314
  69.0 14.2 %collective-permute-start.15 = (bf16[32,2176]{1,0:T(8,128)(2,1)S(1)}, bf16[32,2176]{1,0:T(8,128)(2,1)S(1)}, u32[]{:S(2)}, u32[]{:S(2)}) collective-permute-start(bf16[32,2176]{1,0:T(8,128)(2,1)S(1)} %get-tuple-element.68), channel_id=1, source_target_pairs={{0,64},{64,128},{128,192},{192,0},{1,65},{65,129},{129,193},{193,1... | collective-permute-start | bytes 417800 | tf_op jit(solution)/shard_map/ppermute | solution.py:314
  71.0 12.2 %collective-permute-start.16 = (bf16[32,2176]{1,0:T(8,128)(2,1)S(1)}, bf16[32,2176]{1,0:T(8,128)(2,1)S(1)}, u32[]{:S(2)}, u32[]{:S(2)}) collective-permute-start(bf16[32,2176]{1,0:T(8,128)(2,1)S(1)} %get-tuple-element.69), channel_id=1, source_target_pairs={{0,192},{64,0},{128,64},{192,128},{1,193},{65,1},{129,65},{193,129... | collective-permute-start | bytes 417800 | tf_op jit(solution)/shard_map/ppermute | solution.py:314
  83.4 13.6 %collective-permute-start.17 = (bf16[32,2176]{1,0:T(8,128)(2,1)S(1)}, bf16[32,2176]{1,0:T(8,128)(2,1)S(1)}, u32[]{:S(2)}, u32[]{:S(2)}) collective-permute-start(bf16[32,2176]{1,0:T(8,128)(2,1)S(1)} %shard_map.98.r0_ref), channel_id=1, source_target_pairs={{0,128},{64,192},{128,0},{192,64},{1,129},{65,193},{129,1},{193,65... | collective-permute-start | bytes 417800 | tf_op jit(solution)/shard_map/ppermute | solution.py:316
  86.3 14.8 %collective-permute-start.18 = (bf16[32,2176]{1,0:T(8,128)(2,1)S(1)}, bf16[32,2176]{1,0:T(8,128)(2,1)S(1)}, u32[]{:S(2)}, u32[]{:S(2)}) collective-permute-start(bf16[32,2176]{1,0:T(8,128)(2,1)S(1)} %shard_map.98.r0_ref), channel_id=1, source_target_pairs={{0,64},{64,128},{128,192},{192,0},{1,65},{65,129},{129,193},{193,1... | collective-permute-start | bytes 417800 | tf_op jit(solution)/shard_map/ppermute | solution.py:316
  87.0 14.1 %collective-permute-start.19 = (bf16[32,2176]{1,0:T(8,128)(2,1)S(1)}, bf16[32,2176]{1,0:T(8,128)(2,1)S(1)}, u32[]{:S(2)}, u32[]{:S(2)}) collective-permute-start(bf16[32,2176]{1,0:T(8,128)(2,1)S(1)} %shard_map.98.r0_ref), channel_id=1, source_target_pairs={{0,192},{64,0},{128,64},{192,128},{1,193},{65,1},{129,65},{193,129... | collective-permute-start | bytes 417800 | tf_op jit(solution)/shard_map/ppermute | solution.py:316

commit v4 on v3

v4 whole, which is shorter than its diff:
```python
import functools
import math

import jax
import jax.numpy as jnp
from jax import lax
from jax.experimental import pallas as pl
from jax.experimental.pallas import tpu as pltpu
from jax.sharding import Mesh, PartitionSpec as P

F32 = jnp.float32
BF16 = jnp.bfloat16
EXT = 128
VMEM = pl.BlockSpec(memory_space=pltpu.VMEM)
NT = (((1,), (1,)), ((), ()))
SHIFTS = (0, 1, 3, 2)
SLOTS = (
    tuple((s, 0) for s in SHIFTS),
    ((0, 1), (0, 3), (1, 1), (1, 3)),
    ((3, 1), (3, 3), (2, 1), (2, 3)),
    tuple((s, 2) for s in SHIFTS),
)
DROPPED = 1e30
INTERPRET = False


def call(kernel, out_shape, n_in, flops=0, nbytes=0, **kw):
    many = isinstance(out_shape, (list, tuple))
    n_out = len(out_shape) if many else 1
    specs = dict(
        in_specs=[VMEM] * n_in,
        out_specs=[VMEM] * n_out if many else VMEM,
    )
    specs.update(kw)
    return pl.pallas_call(
        kernel,
        out_shape=out_shape,
        compiler_params=pltpu.CompilerParams(vmem_limit_bytes=16 * 2**20),
        cost_estimate=pl.CostEstimate(flops=flops, bytes_accessed=nbytes, transcendentals=0),
        interpret=INTERPRET,
        **specs,
    )


def sds(shape, dtype):
    return jax.ShapeDtypeStruct(shape, dtype)


def parts(col, n):
    out = []
    for _ in range(n):
        top = col.astype(BF16).astype(F32)
        out.append(top)
        col = col - top
    return out


def lanes(cols, rows):
    lane = lax.broadcasted_iota(jnp.int32, (rows, EXT), 1)
    ext = jnp.zeros((rows, EXT), F32)
    for i, col in enumerate(cols):
        ext = jnp.where(lane == i, col, ext)
    return ext


def split_ext(ext):
    counts = ext[:, 0:1] + ext[:, 1:2]
    kept = ext[:, 2:3] + ext[:, 3:4]
    return lanes(parts(counts, 2) + parts(kept, 2), ext.shape[0]).astype(BF16)


def coef_kernel(m_ref, v_ref, w_ref, out_ref):
    rows, width = m_ref.shape
    m, v = m_ref[...], v_ref[...]
    prec = 1.0 / v
    out_ref[:, :width] = (-0.5 * prec).astype(BF16)
    out_ref[:, width : 2 * width] = (m * prec).astype(BF16)
    down = lax.broadcasted_iota(jnp.int32, (rows, rows), 0)
    across = lax.broadcasted_iota(jnp.int32, (rows, rows), 1)
    offset = (
        jnp.sum(jnp.where(down == across, w_ref[...], 0.0), axis=1, keepdims=True)
        - 0.5 * jnp.sum(m * m * prec + jnp.log(v), axis=1, keepdims=True)
        - 0.5 * width * math.log(2.0 * math.pi)
    )
    out_ref[:, 2 * width :] = lanes(parts(offset, 3), rows).astype(BF16)


def square(rows):
    wide = rows.astype(F32)
    return (wide * wide).astype(BF16)


def slot(group, k):
    back_x, back_y = SLOTS[group][k]
    x, y = lax.axis_index("x"), lax.axis_index("y")
    return lax.rem(x + 4 - back_x, 4) * 4 + lax.rem(y + 4 - back_y, 4)


def score_kernel(e0_ref, e1_ref, e2_ref, e3_ref, coef_ref, s_ref, lse_ref, feats_ref):
    rows, width = e0_ref.shape
    for i, e_ref in enumerate((e0_ref, e1_ref, e2_ref, e3_ref)):
        at = slice(i * rows, (i + 1) * rows)
        feats_ref[at, :width] = square(e_ref[...])
        feats_ref[at, width:] = e_ref[...]
        s = lax.dot_general(
            coef_ref[:, : 2 * width], feats_ref[at, :], NT, preferred_element_type=F32
        )
        s = s + jnp.sum(coef_ref[:, 2 * width :].astype(F32), axis=1, keepdims=True)
        s_ref[:, at] = s
        top = jnp.max(s, axis=0, keepdims=True)
        lse_ref[:, at] = top + jnp.log(jnp.sum(jnp.exp(s - top), axis=0, keepdims=True))


def pay_kernel(keep_ref, own_ref, other_ref, pay_ref, true_ref):
    lane = lax.broadcasted_iota(jnp.int32, (1, 128), 1)
    first = lax.axis_index("c") == 0
    for i in range(16):
        at = slice((i // 2) * 128, (i // 2 + 1) * 128)
        own, other = own_ref[:, at], other_ref[:, at]
        if i == 0:
            true_ref[...] = own
            own = jnp.where((lane < 64) & (keep_ref[...] == 0.0), DROPPED, own)
        left, right = jnp.where(first, own, other), jnp.where(first, other, own)
        if i % 2:
            left = pltpu.roll(left, 64, 1)
        else:
            right = pltpu.roll(right, 64, 1)
        pay_ref[pl.ds(slot(i // 4, i % 4), 1), :] = jnp.where(lane < 64, left, right)


def logsumexp(x):
    top = jnp.max(x, axis=0)
    return top + jnp.log(jnp.sum(jnp.exp(x - top[None]), axis=0))


def moment_body(at_comp, refs, lse_ref):
    pay_ref, s_refs, feats_refs = refs[0], refs[1:3], refs[3:5]
    comps = 128
    lse = logsumexp(pay_ref[...])
    lse_ref[0] = lse
    lse_ref[1] = pltpu.roll(lse, 64, 1)
    lane = lax.broadcasted_iota(jnp.int32, (1, 128), 1)
    core = lax.axis_index("c")
    total = jnp.zeros((comps, 128), F32)
    moments = None
    for i, (s_ref, feats_ref) in enumerate(zip(s_refs, feats_refs, strict=True)):
        half = core if i == 0 else 1 - core
        ps = []
        for j in range(8):
            left, right = (slot(j // 2, 2 * (j % 2) + k) for k in range(2))
            there = jnp.where(
                lane < 64, lse_ref[half, pl.ds(left, 1), :], lse_ref[1 - half, pl.ds(right, 1), :]
            )
            s = s_ref[at_comp : at_comp + comps, j * 128 : (j + 1) * 128]
            p = jnp.exp(s - there).astype(BF16)
            total = total + p.astype(F32)
            ps.append(p)
        add = jnp.dot(jnp.concatenate(ps, axis=1), feats_ref[...], preferred_element_type=F32)
        moments = add if i == 0 else moments + add
    counts = jnp.sum(total, axis=1, keepdims=True)
    kept = jnp.sum(jnp.where(lse < 0.5 * DROPPED, 1.0, 0.0), axis=(0, 1), keepdims=True)
    zero = jnp.zeros_like(counts)
    ext = lanes([counts, zero, jnp.broadcast_to(kept, counts.shape), zero], comps)
    return moments, ext


def moment_kernel(at_comp, *refs):
    *refs, out_ref, lse_ref = refs
    moments, ext = moment_body(at_comp, refs, lse_ref)
    out_ref[:, : moments.shape[1]] = moments
    out_ref[:, moments.shape[1] :] = ext


def moment_kernel_send(at_comp, *refs):
    *refs, true_ref, up_ref, down_ref, own_ref, lse_ref = refs
    pay_ref = refs[0]
    moments, ext = moment_body(at_comp, refs, lse_ref)
    half, feats = up_ref.shape[0], moments.shape[1]
    ext = split_ext(ext)
    for i, ref in enumerate((up_ref, down_ref)):
        at = slice(i * half, (i + 1) * half)
        ref[:, :feats] = moments[at].astype(BF16)
        ref[:, feats:] = ext[at]
    core = lax.axis_index("c")
    place = slot(0, 0)
    values = pay_ref[:, pl.ds(place, 1), :]
    source = lax.broadcasted_iota(jnp.int32, values.shape, 0)
    true = true_ref[...]
    true = jnp.where(core == 0, true, pltpu.roll(true, 64, 1))
    lse = logsumexp(jnp.where(source == 2 * place + core, true[None], values))
    own_ref[...] = jnp.where(core == 0, lse, pltpu.roll(lse, 64, 1))


def pair_sum_kernel(mine_ref, low_ref, high_ref, own_ref, s1_ref, s2_ref, s3_ref, all_ref):
    half = low_ref.shape[0]
    quarter = own_ref.shape[0]
    for at, ref in ((slice(0, half), low_ref), (slice(half, 2 * half), high_ref)):
        all_ref[at, :] = mine_ref[at, :] + ref[...].astype(F32)
    me = lax.axis_index("zh")

    def rows(shift):
        return all_ref[pl.ds(lax.rem(me + shift, 4) * quarter, quarter), :]

    ext = all_ref[:, -EXT:]
    across = lax.broadcasted_iota(jnp.int32, ext.shape, 1)
    down = lax.broadcasted_iota(jnp.int32, ext.shape, 0)
    counts = jnp.sum(jnp.where(across == down, ext[:, 0:1] + ext[:, 1:2], 0.0), axis=0, keepdims=True)
    kept = jnp.broadcast_to(ext[0:1, 2:3] + ext[0:1, 3:4], counts.shape)
    block = jnp.zeros((quarter, EXT), F32)
    for i, row in enumerate(parts(counts, 2) + parts(kept, 2)):
        block = jnp.where(down[:quarter] == i, row, block)
    feats = all_ref.shape[1] - EXT
    own_ref[:, :feats] = rows(0)[:, :feats]
    own_ref[:, feats:] = block
    for shift, ref in ((1, s1_ref), (2, s2_ref), (3, s3_ref)):
        ref[:, :feats] = rows(shift)[:, :feats].astype(BF16)
        ref[:, feats:] = block.astype(BF16)


def finish_kernel(n_comps, own_ref, g2_ref, g1_ref, g3_ref, out_ref, log_ref, ext_ref):
    rows, cols = own_ref.shape
    feats = cols - EXT
    width = feats // 2
    me = lax.axis_index("zh")
    refs = (own_ref, g1_ref, g2_ref, g3_ref)
    for shift, ref in enumerate(refs):
        ext_ref[lax.rem(me + 4 - shift, 4)] = ref[:8, feats:].astype(F32)
    counts = sum(ext_ref[i, 0:1, :] + ext_ref[i, 1:2, :] for i in range(4))
    kept = sum(ext_ref[i, 2:3, :] + ext_ref[i, 3:4, :] for i in range(4))
    log_ref[...] = jnp.log((counts + 1.0) / (kept + float(n_comps)))
    across = lax.broadcasted_iota(jnp.int32, (rows, EXT), 1)
    down = lax.broadcasted_iota(jnp.int32, (rows, EXT), 0)
    counts = jnp.sum(jnp.where(across == down + me * rows, counts, 0.0), axis=1, keepdims=True)
    second = sum(ref[:, :width].astype(F32) for ref in refs)
    first = sum(ref[:, width:feats].astype(F32) for ref in refs)
    denom = counts + 1.0
    mean = first / denom
    out_ref[:, :width] = mean.astype(BF16)
    out_ref[:, width:] = (
        (second - 2.0 * mean * first + mean * mean * counts + 1.0) / denom
    ).astype(BF16)


def place_kernel(got_ref, mean_ref, var_ref):
    _, quarter, _ = got_ref.shape
    width = mean_ref.shape[1]
    for j in range(4):
        at = slice(j * quarter, (j + 1) * quarter)
        mean_ref[at, :] = got_ref[j, :, :width].astype(F32)
        var_ref[at, :] = got_ref[j, :, width:].astype(F32)


def ring(n, shift):
    return [(i, (i + shift) % n) for i in range(n)]


def local(embeddings, keep, means, variances, log_weights):
    own, width = embeddings.shape
    comps = means.shape[0]
    n_comps = comps * 64
    cols = 2 * width + EXT
    plane, z, core = ("x", "y"), ("zh", "zl"), "c"

    back_y = [lax.ppermute(embeddings, "y", ring(4, s)) for s in (1, 3)]
    line = [embeddings] + [lax.ppermute(embeddings, "x", ring(4, s)) for s in SHIFTS[1:]]
    line = jnp.concatenate(line, axis=0)
    pair = jnp.concatenate(back_y, axis=0)

    coef = call(coef_kernel, sds((comps, cols), BF16), 3, 4 * 2**20, 2 * 2**20)(
        means, variances, log_weights[None, :]
    )
    coef, pair = lax.optimization_barrier((coef, pair))
    coef = jnp.concatenate([coef, lax.ppermute(coef, "zl", ring(2, 1))], axis=0)
    far = lax.ppermute(line, "y", ring(4, 2))
    rest = [lax.ppermute(pair, "x", ring(4, s)) for s in SHIFTS[1:]]
    coef, far, rest = lax.optimization_barrier((coef, far, rest))

    groups = [line, jnp.concatenate([pair, rest[0]]), jnp.concatenate(rest[1:]), far]
    groups += [lax.ppermute(e, core, ring(2, 1)) for e in groups]
    n_rows = 16 * own
    flops = 2 * 2 * comps * n_rows * 2 * width
    scores, lses, feats = zip(
        *[
            call(
                score_kernel,
                (
                    sds((2 * comps, n_rows), F32),
                    sds((1, n_rows), F32),
                    sds((n_rows, 2 * width), BF16),
                ),
                5,
                flops,
            )(*es, coef)
            for es in (groups[:4], groups[4:])
        ]
    )
    flag = jnp.pad(keep.astype(F32), (0, own)).reshape(1, 2 * own)
    lse_row = sds((1, 128), F32)
    pay, true = call(pay_kernel, (sds((16, 128), F32), lse_row), 3)(flag, *lses)
    pays = lax.all_to_all(jnp.broadcast_to(pay[None], (32,) + pay.shape), plane + (core,), 0, 0)

    def moments(kernel, at, outs, *more):
        return call(
            functools.partial(kernel, at),
            outs,
            5 + len(more),
            flops,
            scratch_shapes=[pltpu.VMEM((2, 16, 128), F32)],
        )(pays, *scores, *feats, *more)

    half_sum = sds((comps // 2, cols), BF16)
    up, down, own_lse = moments(moment_kernel_send, comps, (half_sum, half_sum, lse_row), true)
    low = lax.ppermute(up, z, ring(8, 1))
    high = lax.ppermute(down, z, ring(8, 7))
    pays, up = lax.optimization_barrier((pays, up))
    mine = moments(moment_kernel, 0, sds((comps, cols), F32))
    quarter = comps // 4
    q32, q16 = sds((quarter, cols), F32), sds((quarter, cols), BF16)
    own_q, s1, s2, s3 = call(
        pair_sum_kernel,
        (q32, q16, q16, q16),
        3,
        scratch_shapes=[pltpu.VMEM((comps, cols), F32)],
    )(mine, low, high)
    g = [lax.ppermute(s, "zh", ring(4, i)) for i, s in ((2, s2), (1, s1), (3, s3))]
    result, new_log = call(
        functools.partial(finish_kernel, n_comps),
        (sds((quarter, 2 * width), BF16), sds((1, comps), F32)),
        4,
        scratch_shapes=[pltpu.VMEM((4, 8, EXT), F32)],
    )(own_q, *g)
    out = sds((comps, width), F32)
    new_means, new_vars = call(place_kernel, (out, out), 1)(lax.all_gather(result, "zh"))

    wide = embeddings.astype(F32)
    own_norm = 0.5 * jnp.sum(wide * wide, axis=1) + 0.5 * width * math.log(2.0 * math.pi)
    return new_means, new_vars, new_log.reshape(-1), own_lse[0, :own] + own_norm


def solution(mesh):
    axes = ("x", "y", "zl", "c")
    fine = Mesh(mesh.devices.reshape(4, 4, 4, 2, 2), ("zh",) + axes)
    both = ("zh",) + axes
    return jax.shard_map(
        local,
        mesh=fine,
        in_specs=(P(both, None), P(both), P(axes, None), P(axes, None), P(axes)),
        out_specs=(P(axes, None), P(axes, None), P(axes), P(both)),
        check_vma=False,
    )
```

time: 103 us -> 101 us (0.981)
  blocking collectives: 12.9 us -> 30.7 us
  waiting for transfers between devices: 41.6 us -> 28.4 us
  starting transfers between devices: 32.9 us -> 26.8 us
  Pallas kernels: 9.89 us -> 8.57 us
    all_gather x0 -> x1, blocking collectives: none -> 16.4 us  [local(): lax.all_gather(result, 'zh')]
    ppermute x6 -> x5, waiting for transfers between devices: 17.3 us -> 6.36 us  [the longest x1 5.46 us: local(): coef = jnp.concatenate([coef, lax.ppermute(coef, 'zl', ring(2, 1))], axis=0)]
    ppermute x6 -> x5, starting transfers between devices: 7.36 us -> 1.15 us  [the longest x4 0.95 us: local(): groups += [lax.ppermute(e, core, ring(2, 1)) for e in groups]]
    ppermute x1, waiting for transfers between devices: 6.67 us -> 4.91 us  [local(): low = lax.ppermute(up, z, ring(8, 1))]
    all_to_all x1, blocking collectives: 12.9 us -> 14.3 us  [local(): lax.all_to_all(jnp.broadcast_to(pay[None], (32,) + pay.shape), plane + (c...]
    pallas_call x14 -> x7, Pallas kernels: 9.3 us -> 7.98 us  [the longest x2 3.17 us: local(): call(score_kernel, (sds((2 * comps, n_rows), F32), sds((1, n_rows), F32),...]
    unnamed x13 -> x15, local copies, waits for them, and re-layouts: 3.13 us -> 3.72 us
  transfers between devices with their start and end apart: 20 -> 19, of which waited for: 10 -> 8; matrix products, arithmetic and copies ran while one was open for 1% -> 2% of each run, Pallas kernels for 4% -> 3%
where the time goes in v4:
time: 101 us; the launch traced here: 99.8 us
  blocking collectives  30.7 us (30%)
  waiting for transfers between devices  28.4 us (28%)
  starting transfers between devices  26.8 us (27%)
  Pallas kernels  8.57 us (8%)
  local copies, waits for them, and re-layouts  3.79 us (4%)
    all_gather x1, blocking collectives, local(): lax.all_gather(result, 'zh')  16.4 us
    all_to_all x1, blocking collectives, local(): lax.all_to_all(jnp.broadcast_to(pay[None], (32,) + pay.shape), plane + (c...  14.3 us
    ppermute x3, waiting for transfers between devices, local(): lax.ppermute(s, 'zh', ring(4, i))  9.75 us
    ppermute x3, starting transfers between devices, local(): lax.ppermute(s, 'zh', ring(4, i))  9.26 us
    ppermute x1, waiting for transfers between devices, local(): coef = jnp.concatenate([coef, lax.ppermute(coef, 'zl', ring(2, 1))], axis=0)  5.46 us
    ppermute x3, starting transfers between devices, local(): lax.ppermute(embeddings, 'x', ring(4, s))  5.05 us
    ppermute x1, waiting for transfers between devices, local(): low = lax.ppermute(up, z, ring(8, 1))  4.91 us
    ppermute x3, waiting for transfers between devices, local(): rest = [lax.ppermute(pair, 'x', ring(4, s)) for s in SHIFTS[1:]]  4.51 us
  transfers between devices with their start and end apart: 19, of which 8 were waited for; matrix products, arithmetic and copies ran while one was open for 2% of the time, Pallas kernels for 3%

profile of v4, /device:TPU:32, one launch (start us, length us, event | category | flops | bytes accessed | tf_op | source)
XLA Modules:
  0.0 99.8 jit_solution(16231422600557411930)
XLA Ops:
  0.6 1.7 %collective-permute-start.3 = (bf16[64,1024]{1,0:T(8,128)(2,1)}, bf16[64,1024]{1,0:T(8,128)(2,1)S(1)}, u32[]{:S(2)}, u32[]{:S(2)}) collective-permute-start(bf16[64,1024]{1,0:T(8,128)(2,1)} %param.5), channel_id=1, source_target_pairs={{0,4},{4,8},{8,12},{12,0},{1,5},{5,9},{9,13},{13,1},{2,6},{6,10},{... | collective-permute-start | bytes 393224 | tf_op jit(solution)/shard_map/ppermute | solution.py:264
  2.3 1.7 %collective-permute-start.4 = (bf16[64,1024]{1,0:T(8,128)(2,1)}, bf16[64,1024]{1,0:T(8,128)(2,1)S(1)}, u32[]{:S(2)}, u32[]{:S(2)}) collective-permute-start(bf16[64,1024]{1,0:T(8,128)(2,1)} %param.5), channel_id=1, source_target_pairs={{0,12},{4,0},{8,4},{12,8},{1,13},{5,1},{9,5},{13,9},{2,14},{6,2},{... | collective-permute-start | bytes 393224 | tf_op jit(solution)/shard_map/ppermute | solution.py:264
  3.9 1.5 %collective-permute-start = (bf16[64,1024]{1,0:T(8,128)(2,1)}, bf16[64,1024]{1,0:T(8,128)(2,1)S(1)}, u32[]{:S(2)}, u32[]{:S(2)}) collective-permute-start(bf16[64,1024]{1,0:T(8,128)(2,1)} %param.5), channel_id=1, source_target_pairs={{0,16},{16,32},{32,48},{48,0},{1,17},{17,33},{33,49},{49,1},{2,18}... | collective-permute-start | bytes 393224 | tf_op jit(solution)/shard_map/ppermute | solution.py:265
  5.4 1.7 %collective-permute-start.1 = (bf16[64,1024]{1,0:T(8,128)(2,1)}, bf16[64,1024]{1,0:T(8,128)(2,1)S(1)}, u32[]{:S(2)}, u32[]{:S(2)}) collective-permute-start(bf16[64,1024]{1,0:T(8,128)(2,1)} %param.5), channel_id=1, source_target_pairs={{0,48},{16,0},{32,16},{48,32},{1,49},{17,1},{33,17},{49,33},{2,50}... | collective-permute-start | bytes 393224 | tf_op jit(solution)/shard_map/ppermute | solution.py:265
  7.2 1.8 %collective-permute-start.2 = (bf16[64,1024]{1,0:T(8,128)(2,1)}, bf16[64,1024]{1,0:T(8,128)(2,1)S(1)}, u32[]{:S(2)}, u32[]{:S(2)}) collective-permute-start(bf16[64,1024]{1,0:T(8,128)(2,1)} %param.5), channel_id=1, source_target_pairs={{0,32},{16,48},{32,0},{48,16},{1,33},{17,49},{33,1},{49,17},{2,34}... | collective-permute-start | bytes 393224 | tf_op jit(solution)/shard_map/ppermute | solution.py:265
  9.0 1.0 %copy-done = f32[128,1024]{1,0:T(8,128)S(1)} copy-done((f32[128,1024]{1,0:T(8,128)S(1)}, f32[128,1024]{1,0:T(8,128)}, u32[]{:S(2)}) %copy-start) | copy-done | bytes 524312
  10.0 1.0 %copy-done.1 = f32[128,1024]{1,0:T(8,128)S(1)} copy-done((f32[128,1024]{1,0:T(8,128)S(1)}, f32[128,1024]{1,0:T(8,128)}, u32[]{:S(2)}) %copy-start.1) | copy-done | bytes 524312
  11.1 0.7 copy-done.2
  12.3 0.9 constant_dynamic-update-slice_fusion.3
  13.3 0.9 collective-permute-done.2
  14.2 2.1 %collective-permute-start.6 = (bf16[256,1024]{1,0:T(8,128)(2,1)S(1)}, bf16[256,1024]{1,0:T(8,128)(2,1)S(1)}, u32[]{:S(2)}, u32[]{:S(2)}) collective-permute-start(bf16[256,1024]{1,0:T(8,128)(2,1)S(1)} %constant_dynamic-update-slice_fusion.e0_ref), channel_id=1, source_target_pairs={{0,8},{4,12},{8,0},{12,4},{1,9},{5,13},{9,1},{13,5},{2,10},{6,14},... | collective-permute-start | bytes 1572872 | tf_op jit(solution)/shard_map/ppermute | solution.py:274
  16.2 0.8 collective-permute-start.7
  17.1 2.4 %collective-permute-start.8 = (bf16[128,1024]{1,0:T(8,128)(2,1)S(1)}, bf16[128,1024]{1,0:T(8,128)(2,1)S(1)}, u32[]{:S(2)}, u32[]{:S(2)}) collective-permute-start(bf16[128,1024]{1,0:T(8,128)(2,1)S(1)} %pad_maximum_fusion.1), channel_id=1, source_target_pairs={{0,48},{16,0},{32,16},{48,32},{1,49},{17,1},{33,17},{49,33},{2,50}... | collective-permute-start | bytes 786440 | tf_op jit(solution)/shard_map/ppermute | solution.py:275
  19.8 5.5 %collective-permute-done.5 = bf16[128,2176]{1,0:T(8,128)(2,1)S(1)} collective-permute-done((bf16[128,2176]{1,0:T(8,128)(2,1)S(1)}, bf16[128,2176]{1,0:T(8,128)(2,1)S(1)}, u32[]{:S(2)}, u32[]{:S(2)}) %collective-permute-start.5) | collective-permute-done | bytes 557088 | tf_op jit(solution)/shard_map/ppermute | solution.py:273
  25.4 4.5 %collective-permute-done.7 = bf16[128,1024]{1,0:T(8,128)(2,1)S(1)} collective-permute-done((bf16[128,1024]{1,0:T(8,128)(2,1)S(1)}, bf16[128,1024]{1,0:T(8,128)(2,1)S(1)}, u32[]{:S(2)}, u32[]{:S(2)}) %collective-permute-start.7) | collective-permute-done | bytes 262176 | tf_op jit(solution)/shard_map/ppermute | solution.py:275
  30.1 0.6 collective-permute-start.11
  31.0 1.6 %shard_map.85 = (f32[256,1024]{1,0:T(8,128)S(1)}, f32[1,1024]{1,0:T(1,128)S(1)}, bf16[1024,2048]{1,0:T(8,128)(2,1)S(1)}) custom-call(bf16[256,1024]{1,0:T(8,128)(2,1)S(1)} %constant_dynamic-update-slice_fusion.e0_ref, bf16[256,1024]{1,0:T(8,128)(2,1)S(1)} %constant_dynamic-update-slice_fusion.4.e1_ref, ...), custom_call_target="tpu_custom_call" | custom-call | flops 1073741824 | tf_op jit(solution)/shard_map/pallas_call | solution.py:284
  32.7 0.7 collective-permute-done.13.e3_ref
  33.5 1.6 %shard_map.86 = (f32[256,1024]{1,0:T(8,128)S(1)}, f32[1,1024]{1,0:T(1,128)S(1)}, bf16[1024,2048]{1,0:T(8,128)(2,1)S(1)}) custom-call(bf16[256,1024]{1,0:T(8,128)(2,1)S(1)} %collective-permute-done.10.e0_ref, bf16[256,1024]{1,0:T(8,128)(2,1)S(1)} %collective-permute-done.11.e1_ref, bf16[256,1024]{1,0:T(8,128)(2,1)S(1)} %collective-permute-done.12.e2_ref, ...), custom_call_target="tpu_custom_call" | custom-call | flops 1073741824 | tf_op jit(solution)/shard_map/pallas_call | solution.py:284
  35.2 14.3 %all_to_all.5.refs_0_ = f32[32,16,128]{2,1,0:T(8,128)S(1)} all-to-all(f32[32,16,128]{2,1,0:T(8,128)S(1)} %broadcast_in_dim.10), channel_id=1, replica_groups=mesh['zh'=4,'x'=4,'y'=4,'zl'=2,'c'=2] {'x','y','c'}, dimensions={0} | all-to-all | bytes 524288 | tf_op jit(solution)/shard_map/all_to_all | solution.py:300
  49.5 1.6 %shard_map.88 = (bf16[64,2176]{1,0:T(8,128)(2,1)S(1)}, bf16[64,2176]{1,0:T(8,128)(2,1)S(1)}, f32[1,128]{1,0:T(1,128)S(1)}) custom-call(f32[32,16,128]{2,1,0:T(8,128)S(1)} %all_to_all.5.refs_0_, f32[256,1024]{1,0:T(8,128)S(1)} %get-tuple-element.41.refs_1_, f32[256,1024]{1,0:T(8,128)S(1)} %get-tuple-element.42.refs_2_, ...), custom_call_target="tpu_custom_call" | custom-call | flops 1073741824 | tf_op jit(solution)/shard_map/pallas_call | solution.py:303
  51.1 2.3 %collective-permute-start.14 = (bf16[64,2176]{1,0:T(8,128)(2,1)S(1)}, bf16[64,2176]{1,0:T(8,128)(2,1)S(1)}, u32[]{:S(2)}, u32[]{:S(2)}) collective-permute-start(bf16[64,2176]{1,0:T(8,128)(2,1)S(1)} %get-tuple-element.46), channel_id=1, source_target_pairs={{0,2},{2,64},{64,66},{66,128},{128,130},{130,192},{192,194},{194,0... | collective-permute-start | bytes 835592 | tf_op jit(solution)/shard_map/ppermute | solution.py:313
  53.6 1.6 %shard_map.89.mine_ref = f32[128,2176]{1,0:T(8,128)S(1)} custom-call(f32[32,16,128]{2,1,0:T(8,128)S(1)} %all_to_all.5.refs_0_, f32[256,1024]{1,0:T(8,128)S(1)} %get-tuple-element.41.refs_1_, f32[256,1024]{1,0:T(8,128)S(1)} %get-tuple-element.42.refs_2_, bf16[1024,2048]{1,0:T(8,128)(2,1)S(1)} %get-tuple-element.43.refs_3_, ...), custom_call_target="tpu_custom_call" | custom-call | flops 1073741824 | tf_op jit(solution)/shard_map/pallas_call | solution.py:303
  55.1 4.9 %collective-permute-done.14.low_ref = bf16[64,2176]{1,0:T(8,128)(2,1)S(1)} collective-permute-done((bf16[64,2176]{1,0:T(8,128)(2,1)S(1)}, bf16[64,2176]{1,0:T(8,128)(2,1)S(1)}, u32[]{:S(2)}, u32[]{:S(2)}) %collective-permute-start.14) | collective-permute-done | bytes 278560 | tf_op jit(solution)/shard_map/ppermute | solution.py:313
  60.1 2.0 %collective-permute-done.15.high_ref = bf16[64,2176]{1,0:T(8,128)(2,1)S(1)} collective-permute-done((bf16[64,2176]{1,0:T(8,128)(2,1)S(1)}, bf16[64,2176]{1,0:T(8,128)(2,1)S(1)}, u32[]{:S(2)}, u32[]{:S(2)}) %collective-permute-start.15) | collective-permute-done | bytes 278560 | tf_op jit(solution)/shard_map/ppermute | solution.py:314
  62.3 5.1 %collective-permute-start.16 = (bf16[32,2176]{1,0:T(8,128)(2,1)S(1)}, bf16[32,2176]{1,0:T(8,128)(2,1)S(1)}, u32[]{:S(2)}, u32[]{:S(2)}) collective-permute-start(bf16[32,2176]{1,0:T(8,128)(2,1)S(1)} %get-tuple-element.50), channel_id=1, source_target_pairs={{0,128},{64,192},{128,0},{192,64},{1,129},{65,193},{129,1},{193,65... | collective-permute-start | bytes 417800 | tf_op jit(solution)/shard_map/ppermute | solution.py:325
  67.5 2.0 %collective-permute-start.17 = (bf16[32,2176]{1,0:T(8,128)(2,1)S(1)}, bf16[32,2176]{1,0:T(8,128)(2,1)S(1)}, u32[]{:S(2)}, u32[]{:S(2)}) collective-permute-start(bf16[32,2176]{1,0:T(8,128)(2,1)S(1)} %get-tuple-element.51), channel_id=1, source_target_pairs={{0,64},{64,128},{128,192},{192,0},{1,65},{65,129},{129,193},{193,1... | collective-permute-start | bytes 417800 | tf_op jit(solution)/shard_map/ppermute | solution.py:325
  69.5 2.1 %collective-permute-start.18 = (bf16[32,2176]{1,0:T(8,128)(2,1)S(1)}, bf16[32,2176]{1,0:T(8,128)(2,1)S(1)}, u32[]{:S(2)}, u32[]{:S(2)}) collective-permute-start(bf16[32,2176]{1,0:T(8,128)(2,1)S(1)} %get-tuple-element.52), channel_id=1, source_target_pairs={{0,192},{64,0},{128,64},{192,128},{1,193},{65,1},{129,65},{193,129... | collective-permute-start | bytes 417800 | tf_op jit(solution)/shard_map/ppermute | solution.py:325
  72.1 9.7 %collective-permute-done.17.g1_ref = bf16[32,2176]{1,0:T(8,128)(2,1)S(1)} collective-permute-done((bf16[32,2176]{1,0:T(8,128)(2,1)S(1)}, bf16[32,2176]{1,0:T(8,128)(2,1)S(1)}, u32[]{:S(2)}, u32[]{:S(2)}) %collective-permute-start.17) | collective-permute-done | bytes 139296 | tf_op jit(solution)/shard_map/ppermute | solution.py:325
  81.9 0.5 shard_map.91
  82.4 16.4 %all-gather = bf16[128,2048]{1,0:T(8,128)(2,1)S(1)} all-gather(bf16[32,2048]{1,0:T(8,128)(2,1)S(1)} %get-tuple-element.53), channel_id=2, replica_groups=mesh['zh'=4,'x'=4,'y'=4,'zl'=2,'c'=2] {'zh'}, dimensions={0}, use_global_device_ids=true | all-gather | bytes 655360 | tf_op jit(solution)/shard_map/all_gather | solution.py:333
  98.8 1.0 %shard_map.92 = (f32[128,1024]{1,0:T(8,128)}, f32[128,1024]{1,0:T(8,128)}) custom-call(bf16[4,32,2048]{2,1,0:T(8,128)(2,1)S(1)} %bitcast.7), custom_call_target="tpu_custom_call" | custom-call | tf_op jit(solution)/shard_map/pallas_call | solution.py:333
  (42 shorter events, 2.7 us)
Async XLA Ops:
  0.6 11.4 %collective-permute-start.3 = (bf16[64,1024]{1,0:T(8,128)(2,1)}, bf16[64,1024]{1,0:T(8,128)(2,1)S(1)}, u32[]{:S(2)}, u32[]{:S(2)}) collective-permute-start(bf16[64,1024]{1,0:T(8,128)(2,1)} %param.5), channel_id=1, source_target_pairs={{0,4},{4,8},{8,12},{12,0},{1,5},{5,9},{9,13},{13,1},{2,6},{6,10},{... | collective-permute-start | bytes 393224 | tf_op jit(solution)/shard_map/ppermute | solution.py:264
  2.3 9.8 %collective-permute-start.4 = (bf16[64,1024]{1,0:T(8,128)(2,1)}, bf16[64,1024]{1,0:T(8,128)(2,1)S(1)}, u32[]{:S(2)}, u32[]{:S(2)}) collective-permute-start(bf16[64,1024]{1,0:T(8,128)(2,1)} %param.5), channel_id=1, source_target_pairs={{0,12},{4,0},{8,4},{12,8},{1,13},{5,1},{9,5},{13,9},{2,14},{6,2},{... | collective-permute-start | bytes 393224 | tf_op jit(solution)/shard_map/ppermute | solution.py:264
  3.9 9.3 %collective-permute-start = (bf16[64,1024]{1,0:T(8,128)(2,1)}, bf16[64,1024]{1,0:T(8,128)(2,1)S(1)}, u32[]{:S(2)}, u32[]{:S(2)}) collective-permute-start(bf16[64,1024]{1,0:T(8,128)(2,1)} %param.5), channel_id=1, source_target_pairs={{0,16},{16,32},{32,48},{48,0},{1,17},{17,33},{33,49},{49,1},{2,18}... | collective-permute-start | bytes 393224 | tf_op jit(solution)/shard_map/ppermute | solution.py:265
  5.4 7.8 %collective-permute-start.1 = (bf16[64,1024]{1,0:T(8,128)(2,1)}, bf16[64,1024]{1,0:T(8,128)(2,1)S(1)}, u32[]{:S(2)}, u32[]{:S(2)}) collective-permute-start(bf16[64,1024]{1,0:T(8,128)(2,1)} %param.5), channel_id=1, source_target_pairs={{0,48},{16,0},{32,16},{48,32},{1,49},{17,1},{33,17},{49,33},{2,50}... | collective-permute-start | bytes 393224 | tf_op jit(solution)/shard_map/ppermute | solution.py:265
  7.2 6.9 %collective-permute-start.2 = (bf16[64,1024]{1,0:T(8,128)(2,1)}, bf16[64,1024]{1,0:T(8,128)(2,1)S(1)}, u32[]{:S(2)}, u32[]{:S(2)}) collective-permute-start(bf16[64,1024]{1,0:T(8,128)(2,1)} %param.5), channel_id=1, source_target_pairs={{0,32},{16,48},{32,0},{48,16},{1,33},{17,49},{33,1},{49,17},{2,34}... | collective-permute-start | bytes 393224 | tf_op jit(solution)/shard_map/ppermute | solution.py:265
  9.0 1.0 %copy-start = (f32[128,1024]{1,0:T(8,128)S(1)}, f32[128,1024]{1,0:T(8,128)}, u32[]{:S(2)}) copy-start(f32[128,1024]{1,0:T(8,128)} %m_ref.1) | copy-start | bytes 1572868
  10.0 1.0 %copy-start.1 = (f32[128,1024]{1,0:T(8,128)S(1)}, f32[128,1024]{1,0:T(8,128)}, u32[]{:S(2)}) copy-start(f32[128,1024]{1,0:T(8,128)} %v_ref.1) | copy-start | bytes 1572868
  11.1 0.7 copy-start.2
  12.1 13.2 %collective-permute-start.5 = (bf16[128,2176]{1,0:T(8,128)(2,1)S(1)}, bf16[128,2176]{1,0:T(8,128)(2,1)S(1)}, u32[]{:S(2)}, u32[]{:S(2)}) collective-permute-start(bf16[128,2176]{1,0:T(8,128)(2,1)S(1)} %shard_map.84), channel_id=1, source_target_pairs={{0,2},{2,0},{1,3},{3,1},{4,6},{6,4},{5,7},{7,5},{8,10},{10,8},{9,1... | collective-permute-start | bytes 1671176 | tf_op jit(solution)/shard_map/ppermute | solution.py:273
  14.1 16.8 %copy-start.4 = (s32[64]{0:T(128)S(1)}, s32[64]{0:T(128)}, u32[]{:S(2)}) copy-start(s32[64]{0:T(128)} %param.6) | copy-start | bytes 772
  14.2 15.7 %collective-permute-start.6 = (bf16[256,1024]{1,0:T(8,128)(2,1)S(1)}, bf16[256,1024]{1,0:T(8,128)(2,1)S(1)}, u32[]{:S(2)}, u32[]{:S(2)}) collective-permute-start(bf16[256,1024]{1,0:T(8,128)(2,1)S(1)} %constant_dynamic-update-slice_fusion.e0_ref), channel_id=1, source_target_pairs={{0,8},{4,12},{8,0},{12,4},{1,9},{5,13},{9,1},{13,5},{2,10},{6,14},... | collective-permute-start | bytes 1572872 | tf_op jit(solution)/shard_map/ppermute | solution.py:274
  16.2 13.7 %collective-permute-start.7 = (bf16[128,1024]{1,0:T(8,128)(2,1)S(1)}, bf16[128,1024]{1,0:T(8,128)(2,1)S(1)}, u32[]{:S(2)}, u32[]{:S(2)}) collective-permute-start(bf16[128,1024]{1,0:T(8,128)(2,1)S(1)} %pad_maximum_fusion.1), channel_id=1, source_target_pairs={{0,16},{16,32},{32,48},{48,0},{1,17},{17,33},{33,49},{49,1},{2,18}... | collective-permute-start | bytes 786440 | tf_op jit(solution)/shard_map/ppermute | solution.py:275
  17.1 12.8 %collective-permute-start.8 = (bf16[128,1024]{1,0:T(8,128)(2,1)S(1)}, bf16[128,1024]{1,0:T(8,128)(2,1)S(1)}, u32[]{:S(2)}, u32[]{:S(2)}) collective-permute-start(bf16[128,1024]{1,0:T(8,128)(2,1)S(1)} %pad_maximum_fusion.1), channel_id=1, source_target_pairs={{0,48},{16,0},{32,16},{48,32},{1,49},{17,1},{33,17},{49,33},{2,50}... | collective-permute-start | bytes 786440 | tf_op jit(solution)/shard_map/ppermute | solution.py:275
  19.5 10.4 %collective-permute-start.9 = (bf16[128,1024]{1,0:T(8,128)(2,1)S(1)}, bf16[128,1024]{1,0:T(8,128)(2,1)S(1)}, u32[]{:S(2)}, u32[]{:S(2)}) collective-permute-start(bf16[128,1024]{1,0:T(8,128)(2,1)S(1)} %pad_maximum_fusion.1), channel_id=1, source_target_pairs={{0,32},{16,48},{32,0},{48,16},{1,33},{17,49},{33,1},{49,17},{2,34}... | collective-permute-start | bytes 786440 | tf_op jit(solution)/shard_map/ppermute | solution.py:275
  25.3 7.3 %collective-permute-start.10 = (bf16[256,1024]{1,0:T(8,128)(2,1)S(1)}, bf16[256,1024]{1,0:T(8,128)(2,1)S(1)}, u32[]{:S(2)}, u32[]{:S(2)}) collective-permute-start(bf16[256,1024]{1,0:T(8,128)(2,1)S(1)} %constant_dynamic-update-slice_fusion.e0_ref), channel_id=1, source_target_pairs={{0,1},{1,0},{2,3},{3,2},{4,5},{5,4},{6,7},{7,6},{8,9},{9,8},{10,11... | collective-permute-start | bytes 1572872 | tf_op jit(solution)/shard_map/ppermute | solution.py:279
  30.0 2.6 %collective-permute-start.12 = (bf16[256,1024]{1,0:T(8,128)(2,1)S(1)}, bf16[256,1024]{1,0:T(8,128)(2,1)S(1)}, u32[]{:S(2)}, u32[]{:S(2)}) collective-permute-start(bf16[256,1024]{1,0:T(8,128)(2,1)S(1)} %constant_dynamic-update-slice_fusion.6.e2_ref), channel_id=1, source_target_pairs={{0,1},{1,0},{2,3},{3,2},{4,5},{5,4},{6,7},{7,6},{8,9},{9,8},{10,11... | collective-permute-start | bytes 1572872 | tf_op jit(solution)/shard_map/ppermute | solution.py:279
  30.1 2.6 %collective-permute-start.11 = (bf16[256,1024]{1,0:T(8,128)(2,1)S(1)}, bf16[256,1024]{1,0:T(8,128)(2,1)S(1)}, u32[]{:S(2)}, u32[]{:S(2)}) collective-permute-start(bf16[256,1024]{1,0:T(8,128)(2,1)S(1)} %constant_dynamic-update-slice_fusion.4.e1_ref), channel_id=1, source_target_pairs={{0,1},{1,0},{2,3},{3,2},{4,5},{5,4},{6,7},{7,6},{8,9},{9,8},{10,11... | collective-permute-start | bytes 1572872 | tf_op jit(solution)/shard_map/ppermute | solution.py:279
  30.7 2.8 %collective-permute-start.13 = (bf16[256,1024]{1,0:T(8,128)(2,1)S(1)}, bf16[256,1024]{1,0:T(8,128)(2,1)S(1)}, u32[]{:S(2)}, u32[]{:S(2)}) collective-permute-start(bf16[256,1024]{1,0:T(8,128)(2,1)S(1)} %collective-permute-done.6.e3_ref), channel_id=1, source_target_pairs={{0,1},{1,0},{2,3},{3,2},{4,5},{5,4},{6,7},{7,6},{8,9},{9,8},{10,11... | collective-permute-start | bytes 1572872 | tf_op jit(solution)/shard_map/ppermute | solution.py:279
  49.5 3.9 %copy-start.3 = (bf16[64,1024]{1,0:T(8,128)(2,1)S(1)}, bf16[64,1024]{1,0:T(8,128)(2,1)}, u32[]{:S(2)}) copy-start(bf16[64,1024]{1,0:T(8,128)(2,1)} %param.5) | copy-start | bytes 393220
  51.1 9.0 %collective-permute-start.14 = (bf16[64,2176]{1,0:T(8,128)(2,1)S(1)}, bf16[64,2176]{1,0:T(8,128)(2,1)S(1)}, u32[]{:S(2)}, u32[]{:S(2)}) collective-permute-start(bf16[64,2176]{1,0:T(8,128)(2,1)S(1)} %get-tuple-element.46), channel_id=1, source_target_pairs={{0,2},{2,64},{64,66},{66,128},{128,130},{130,192},{192,194},{194,0... | collective-permute-start | bytes 835592 | tf_op jit(solution)/shard_map/ppermute | solution.py:313
  53.4 8.6 %collective-permute-start.15 = (bf16[64,2176]{1,0:T(8,128)(2,1)S(1)}, bf16[64,2176]{1,0:T(8,128)(2,1)S(1)}, u32[]{:S(2)}, u32[]{:S(2)}) collective-permute-start(bf16[64,2176]{1,0:T(8,128)(2,1)S(1)} %get-tuple-element.48), channel_id=1, source_target_pairs={{0,194},{2,0},{64,2},{66,64},{128,66},{130,128},{192,130},{194,192... | collective-permute-start | bytes 835592 | tf_op jit(solution)/shard_map/ppermute | solution.py:314
  62.3 9.8 %collective-permute-start.16 = (bf16[32,2176]{1,0:T(8,128)(2,1)S(1)}, bf16[32,2176]{1,0:T(8,128)(2,1)S(1)}, u32[]{:S(2)}, u32[]{:S(2)}) collective-permute-start(bf16[32,2176]{1,0:T(8,128)(2,1)S(1)} %get-tuple-element.50), channel_id=1, source_target_pairs={{0,128},{64,192},{128,0},{192,64},{1,129},{65,193},{129,1},{193,65... | collective-permute-start | bytes 417800 | tf_op jit(solution)/shard_map/ppermute | solution.py:325
  67.5 14.4 %collective-permute-start.17 = (bf16[32,2176]{1,0:T(8,128)(2,1)S(1)}, bf16[32,2176]{1,0:T(8,128)(2,1)S(1)}, u32[]{:S(2)}, u32[]{:S(2)}) collective-permute-start(bf16[32,2176]{1,0:T(8,128)(2,1)S(1)} %get-tuple-element.51), channel_id=1, source_target_pairs={{0,64},{64,128},{128,192},{192,0},{1,65},{65,129},{129,193},{193,1... | collective-permute-start | bytes 417800 | tf_op jit(solution)/shard_map/ppermute | solution.py:325
  69.5 12.4 %collective-permute-start.18 = (bf16[32,2176]{1,0:T(8,128)(2,1)S(1)}, bf16[32,2176]{1,0:T(8,128)(2,1)S(1)}, u32[]{:S(2)}, u32[]{:S(2)}) collective-permute-start(bf16[32,2176]{1,0:T(8,128)(2,1)S(1)} %get-tuple-element.52), channel_id=1, source_target_pairs={{0,192},{64,0},{128,64},{192,128},{1,193},{65,1},{129,65},{193,129... | collective-permute-start | bytes 417800 | tf_op jit(solution)/shard_map/ppermute | solution.py:325

commit v5 on v4

--- a/solution.py
+++ b/solution.py
@@ -13,11 +13,11 @@
 EXT = 128
 VMEM = pl.BlockSpec(memory_space=pltpu.VMEM)
 NT = (((1,), (1,)), ((), ()))
-SHIFTS = (0, 1, 3, 2)
+SHIFTS = (0, 2, 1, 3)
 SLOTS = (
     tuple((s, 0) for s in SHIFTS),
-    ((0, 1), (0, 3), (1, 1), (1, 3)),
-    ((3, 1), (3, 3), (2, 1), (2, 3)),
+    ((0, 1), (0, 3), (2, 1), (2, 3)),
+    ((1, 1), (1, 3), (3, 1), (3, 3)),
     tuple((s, 2) for s in SHIFTS),
 )
 DROPPED = 1e30
@@ -69,25 +69,18 @@
     return lanes(parts(counts, 2) + parts(kept, 2), ext.shape[0]).astype(BF16)
 
 
-def coef_kernel(m_ref, v_ref, w_ref, out_ref):
-    rows, width = m_ref.shape
-    m, v = m_ref[...], v_ref[...]
-    prec = 1.0 / v
-    out_ref[:, :width] = (-0.5 * prec).astype(BF16)
-    out_ref[:, width : 2 * width] = (m * prec).astype(BF16)
+def coef_kernel(a_ref, b_ref, offset_ref, out_ref):
+    rows, width = a_ref.shape
+    out_ref[:, :width] = a_ref[...]
+    out_ref[:, width : 2 * width] = b_ref[...]
     down = lax.broadcasted_iota(jnp.int32, (rows, rows), 0)
     across = lax.broadcasted_iota(jnp.int32, (rows, rows), 1)
-    offset = (
-        jnp.sum(jnp.where(down == across, w_ref[...], 0.0), axis=1, keepdims=True)
-        - 0.5 * jnp.sum(m * m * prec + jnp.log(v), axis=1, keepdims=True)
-        - 0.5 * width * math.log(2.0 * math.pi)
-    )
+    offset = jnp.sum(jnp.where(down == across, offset_ref[...], 0.0), axis=1, keepdims=True)
     out_ref[:, 2 * width :] = lanes(parts(offset, 3), rows).astype(BF16)
 
 
 def square(rows):
-    wide = rows.astype(F32)
-    return (wide * wide).astype(BF16)
+    return rows * rows
 
 
 def slot(group, k):
@@ -98,14 +91,16 @@
 
 def score_kernel(e0_ref, e1_ref, e2_ref, e3_ref, coef_ref, s_ref, lse_ref, feats_ref):
     rows, width = e0_ref.shape
+    offset = jnp.sum(coef_ref[:, 2 * width :].astype(F32), axis=1, keepdims=True)
     for i, e_ref in enumerate((e0_ref, e1_ref, e2_ref, e3_ref)):
         at = slice(i * rows, (i + 1) * rows)
         feats_ref[at, :width] = square(e_ref[...])
         feats_ref[at, width:] = e_ref[...]
-        s = lax.dot_general(
+    for i in range(2):
+        at = slice(i * 2 * rows, (i + 1) * 2 * rows)
+        s = offset + lax.dot_general(
             coef_ref[:, : 2 * width], feats_ref[at, :], NT, preferred_element_type=F32
         )
-        s = s + jnp.sum(coef_ref[:, 2 * width :].astype(F32), axis=1, keepdims=True)
         s_ref[:, at] = s
         top = jnp.max(s, axis=0, keepdims=True)
         lse_ref[:, at] = top + jnp.log(jnp.sum(jnp.exp(s - top), axis=0, keepdims=True))
@@ -263,13 +258,19 @@
 
     back_y = [lax.ppermute(embeddings, "y", ring(4, s)) for s in (1, 3)]
     line = [embeddings] + [lax.ppermute(embeddings, "x", ring(4, s)) for s in SHIFTS[1:]]
+    pair = jnp.concatenate(back_y, axis=0)
+
+    prec = 1.0 / variances
+    offset = (
+        log_weights
+        - 0.5 * jnp.sum(means * means * prec + jnp.log(variances), axis=1)
+        - 0.5 * width * math.log(2.0 * math.pi)
+    )
+    coef = call(coef_kernel, sds((comps, cols), BF16), 3, 0, 2**20)(
+        (-0.5 * prec).astype(BF16), (means * prec).astype(BF16), offset[None, :]
+    )
+    coef, line[1] = lax.optimization_barrier((coef, line[1]))
     line = jnp.concatenate(line, axis=0)
-    pair = jnp.concatenate(back_y, axis=0)
-
-    coef = call(coef_kernel, sds((comps, cols), BF16), 3, 4 * 2**20, 2 * 2**20)(
-        means, variances, log_weights[None, :]
-    )
-    coef, pair = lax.optimization_barrier((coef, pair))
     coef = jnp.concatenate([coef, lax.ppermute(coef, "zl", ring(2, 1))], axis=0)
     far = lax.ppermute(line, "y", ring(4, 2))
     rest = [lax.ppermute(pair, "x", ring(4, s)) for s in SHIFTS[1:]]

time: 101 us -> 98.7 us (0.977)
  local copies, waits for them, and re-layouts: 3.79 us -> 1.07 us
  other arithmetic: 0.75 us -> 2.85 us
  blocking collectives: 30.7 us -> 29 us
  starting transfers between devices: 26.8 us -> 28 us
    unnamed x15 -> x9, local copies, waits for them, and re-layouts: 3.72 us -> 0.98 us
    ppermute x3, waiting for transfers between devices: 4.51 us -> 2.69 us  [local(): rest = [lax.ppermute(pair, 'x', ring(4, s)) for s in SHIFTS[1:]]]
    ppermute x1, waiting for transfers between devices: 5.46 us -> 7.1 us  [local(): coef = jnp.concatenate([coef, lax.ppermute(coef, 'zl', ring(2, 1))], axis=0)]
    all_to_all x1, blocking collectives: 14.3 us -> 12.9 us  [local(): lax.all_to_all(jnp.broadcast_to(pay[None], (32,) + pay.shape), plane + (c...]
    reduce_sum x0 -> x1, other arithmetic: none -> 1.47 us  [local(): jnp.sum(means * means * prec + jnp.log(variances), axis=1)]
    ppermute x3, starting transfers between devices: 5.05 us -> 6.35 us  [local(): lax.ppermute(embeddings, 'x', ring(4, s))]
  transfers between devices with their start and end apart: 19 -> 19, of which waited for: 8 -> 7; matrix products, arithmetic and copies ran while one was open for 2% -> 4% of each run, Pallas kernels for 3% -> 3%
where the time goes in v5:
time: 98.7 us; the launch traced here: 97.5 us
  blocking collectives  29 us (29%)
  starting transfers between devices  28 us (28%)
  waiting for transfers between devices  27.4 us (28%)
  Pallas kernels  8.33 us (8%)
  other arithmetic  2.85 us (3%)
  local copies, waits for them, and re-layouts  1.07 us (1%)
    all_gather x1, blocking collectives, local(): lax.all_gather(result, 'zh')  16.2 us
    all_to_all x1, blocking collectives, local(): lax.all_to_all(jnp.broadcast_to(pay[None], (32,) + pay.shape), plane + (c...  12.9 us
    ppermute x3, waiting for transfers between devices, local(): lax.ppermute(s, 'zh', ring(4, i))  9.76 us
    ppermute x3, starting transfers between devices, local(): lax.ppermute(s, 'zh', ring(4, i))  8.79 us
    ppermute x1, waiting for transfers between devices, local(): coef = jnp.concatenate([coef, lax.ppermute(coef, 'zl', ring(2, 1))], axis=0)  7.1 us
    ppermute x3, starting transfers between devices, local(): lax.ppermute(embeddings, 'x', ring(4, s))  6.35 us
    ppermute x1, waiting for transfers between devices, local(): low = lax.ppermute(up, z, ring(8, 1))  4.7 us
    ppermute x3, starting transfers between devices, local(): rest = [lax.ppermute(pair, 'x', ring(4, s)) for s in SHIFTS[1:]]  3.59 us
  transfers between devices with their start and end apart: 19, of which 7 were waited for; matrix products, arithmetic and copies ran while one was open for 4% of the time, Pallas kernels for 3%

profile of v5, /device:TPU:32, one launch (start us, length us, event | category | flops | bytes accessed | tf_op | source)
XLA Modules:
  0.0 97.5 jit_solution(13409179105635666175)
XLA Ops:
  0.6 3.1 %collective-permute-start = (bf16[64,1024]{1,0:T(8,128)(2,1)}, bf16[64,1024]{1,0:T(8,128)(2,1)S(1)}, u32[]{:S(2)}, u32[]{:S(2)}) collective-permute-start(bf16[64,1024]{1,0:T(8,128)(2,1)} %param.5), channel_id=1, source_target_pairs={{0,32},{16,48},{32,0},{48,16},{1,33},{17,49},{33,1},{49,17},{2,34}... | collective-permute-start | bytes 393224 | tf_op jit(solution)/shard_map/ppermute | solution.py:260
  3.7 0.6 collective-permute-start.1
  4.3 2.6 %collective-permute-start.2 = (bf16[64,1024]{1,0:T(8,128)(2,1)}, bf16[64,1024]{1,0:T(8,128)(2,1)S(1)}, u32[]{:S(2)}, u32[]{:S(2)}) collective-permute-start(bf16[64,1024]{1,0:T(8,128)(2,1)} %param.5), channel_id=1, source_target_pairs={{0,48},{16,0},{32,16},{48,32},{1,49},{17,1},{33,17},{49,33},{2,50}... | collective-permute-start | bytes 393224 | tf_op jit(solution)/shard_map/ppermute | solution.py:260
  7.0 1.6 %collective-permute-start.3 = (bf16[64,1024]{1,0:T(8,128)(2,1)}, bf16[64,1024]{1,0:T(8,128)(2,1)S(1)}, u32[]{:S(2)}, u32[]{:S(2)}) collective-permute-start(bf16[64,1024]{1,0:T(8,128)(2,1)} %param.5), channel_id=1, source_target_pairs={{0,4},{4,8},{8,12},{12,0},{1,5},{5,9},{9,13},{13,1},{2,6},{6,10},{... | collective-permute-start | bytes 393224 | tf_op jit(solution)/shard_map/ppermute | solution.py:259
  8.6 1.7 %collective-permute-start.4 = (bf16[64,1024]{1,0:T(8,128)(2,1)}, bf16[64,1024]{1,0:T(8,128)(2,1)S(1)}, u32[]{:S(2)}, u32[]{:S(2)}) collective-permute-start(bf16[64,1024]{1,0:T(8,128)(2,1)} %param.5), channel_id=1, source_target_pairs={{0,12},{4,0},{8,4},{12,8},{1,13},{5,1},{9,5},{13,9},{2,14},{6,2},{... | collective-permute-start | bytes 393224 | tf_op jit(solution)/shard_map/ppermute | solution.py:259
  10.2 1.5 %add_reduce_fusion = (f32[128]{0:T(128)S(1)}, bf16[128,1024]{1,0:T(8,128)(2,1)S(1)}, bf16[128,1024]{1,0:T(8,128)(2,1)S(1)}) fusion(f32[128,1024]{1,0:T(8,128)} %param.8, f32[128,1024]{1,0:T(8,128)} %param.7), kind=kLoop, calls=%fused_computation.1 | loop fusion | flops 1179520 | bytes 1573376 | tf_op jit(solution)/shard_map/reduce_sum | solution.py:266
  11.7 0.7 add_bitcast_fusion.offset_ref
  12.3 0.9 constant_dynamic-update-slice_fusion.3
  13.7 2.1 %collective-permute-start.6 = (bf16[256,1024]{1,0:T(8,128)(2,1)S(1)}, bf16[256,1024]{1,0:T(8,128)(2,1)S(1)}, u32[]{:S(2)}, u32[]{:S(2)}) collective-permute-start(bf16[256,1024]{1,0:T(8,128)(2,1)S(1)} %constant_dynamic-update-slice_fusion.e0_ref), channel_id=1, source_target_pairs={{0,8},{4,12},{8,0},{12,4},{1,9},{5,13},{9,1},{13,5},{2,10},{6,14},... | collective-permute-start | bytes 1572872 | tf_op jit(solution)/shard_map/ppermute | solution.py:275
  15.8 0.4 collective-permute-start.7
  16.2 1.9 %collective-permute-start.8 = (bf16[128,1024]{1,0:T(8,128)(2,1)S(1)}, bf16[128,1024]{1,0:T(8,128)(2,1)S(1)}, u32[]{:S(2)}, u32[]{:S(2)}) collective-permute-start(bf16[128,1024]{1,0:T(8,128)(2,1)S(1)} %get-tuple-element.61), channel_id=1, source_target_pairs={{0,16},{16,32},{32,48},{48,0},{1,17},{17,33},{33,49},{49,1},{2,18}... | collective-permute-start | bytes 786440 | tf_op jit(solution)/shard_map/ppermute | solution.py:276
  18.0 1.3 %collective-permute-start.9 = (bf16[128,1024]{1,0:T(8,128)(2,1)S(1)}, bf16[128,1024]{1,0:T(8,128)(2,1)S(1)}, u32[]{:S(2)}, u32[]{:S(2)}) collective-permute-start(bf16[128,1024]{1,0:T(8,128)(2,1)S(1)} %get-tuple-element.61), channel_id=1, source_target_pairs={{0,48},{16,0},{32,16},{48,32},{1,49},{17,1},{33,17},{49,33},{2,50}... | collective-permute-start | bytes 786440 | tf_op jit(solution)/shard_map/ppermute | solution.py:276
  19.4 7.1 %collective-permute-done.5 = bf16[128,2176]{1,0:T(8,128)(2,1)S(1)} collective-permute-done((bf16[128,2176]{1,0:T(8,128)(2,1)S(1)}, bf16[128,2176]{1,0:T(8,128)(2,1)S(1)}, u32[]{:S(2)}, u32[]{:S(2)}) %collective-permute-start.5) | collective-permute-done | bytes 557088 | tf_op jit(solution)/shard_map/ppermute | solution.py:274
  26.6 2.7 %collective-permute-done.8 = bf16[128,1024]{1,0:T(8,128)(2,1)S(1)} collective-permute-done((bf16[128,1024]{1,0:T(8,128)(2,1)S(1)}, bf16[128,1024]{1,0:T(8,128)(2,1)S(1)}, u32[]{:S(2)}, u32[]{:S(2)}) %collective-permute-start.8) | collective-permute-done | bytes 262176 | tf_op jit(solution)/shard_map/ppermute | solution.py:276
  29.5 0.6 collective-permute-start.11
  30.3 1.6 %shard_map.85 = (f32[256,1024]{1,0:T(8,128)S(1)}, f32[1,1024]{1,0:T(1,128)S(1)}, bf16[1024,2048]{1,0:T(8,128)(2,1)S(1)}) custom-call(bf16[256,1024]{1,0:T(8,128)(2,1)S(1)} %constant_dynamic-update-slice_fusion.e0_ref, bf16[256,1024]{1,0:T(8,128)(2,1)S(1)} %constant_dynamic-update-slice_fusion.6.e1_ref, ...), custom_call_target="tpu_custom_call" | custom-call | flops 1073741824 | tf_op jit(solution)/shard_map/pallas_call | solution.py:285
  32.1 0.7 collective-permute-done.13.e3_ref
  32.8 1.6 %shard_map.86 = (f32[256,1024]{1,0:T(8,128)S(1)}, f32[1,1024]{1,0:T(1,128)S(1)}, bf16[1024,2048]{1,0:T(8,128)(2,1)S(1)}) custom-call(bf16[256,1024]{1,0:T(8,128)(2,1)S(1)} %collective-permute-done.10.e0_ref, bf16[256,1024]{1,0:T(8,128)(2,1)S(1)} %collective-permute-done.11.e1_ref, bf16[256,1024]{1,0:T(8,128)(2,1)S(1)} %collective-permute-done.12.e2_ref, ...), custom_call_target="tpu_custom_call" | custom-call | flops 1073741824 | tf_op jit(solution)/shard_map/pallas_call | solution.py:285
  34.5 12.9 %all_to_all.5.refs_0_ = f32[32,16,128]{2,1,0:T(8,128)S(1)} all-to-all(f32[32,16,128]{2,1,0:T(8,128)S(1)} %broadcast_in_dim.10), channel_id=1, replica_groups=mesh['zh'=4,'x'=4,'y'=4,'zl'=2,'c'=2] {'x','y','c'}, dimensions={0} | all-to-all | bytes 524288 | tf_op jit(solution)/shard_map/all_to_all | solution.py:301
  47.4 1.6 %shard_map.88 = (bf16[64,2176]{1,0:T(8,128)(2,1)S(1)}, bf16[64,2176]{1,0:T(8,128)(2,1)S(1)}, f32[1,128]{1,0:T(1,128)S(1)}) custom-call(f32[32,16,128]{2,1,0:T(8,128)S(1)} %all_to_all.5.refs_0_, f32[256,1024]{1,0:T(8,128)S(1)} %get-tuple-element.41.refs_1_, f32[256,1024]{1,0:T(8,128)S(1)} %get-tuple-element.42.refs_2_, ...), custom_call_target="tpu_custom_call" | custom-call | flops 1073741824 | tf_op jit(solution)/shard_map/pallas_call | solution.py:304
  49.0 2.8 %collective-permute-start.14 = (bf16[64,2176]{1,0:T(8,128)(2,1)S(1)}, bf16[64,2176]{1,0:T(8,128)(2,1)S(1)}, u32[]{:S(2)}, u32[]{:S(2)}) collective-permute-start(bf16[64,2176]{1,0:T(8,128)(2,1)S(1)} %get-tuple-element.46), channel_id=1, source_target_pairs={{0,2},{2,64},{64,66},{66,128},{128,130},{130,192},{192,194},{194,0... | collective-permute-start | bytes 835592 | tf_op jit(solution)/shard_map/ppermute | solution.py:314
  51.9 1.6 %shard_map.89.mine_ref = f32[128,2176]{1,0:T(8,128)S(1)} custom-call(f32[32,16,128]{2,1,0:T(8,128)S(1)} %all_to_all.5.refs_0_, f32[256,1024]{1,0:T(8,128)S(1)} %get-tuple-element.41.refs_1_, f32[256,1024]{1,0:T(8,128)S(1)} %get-tuple-element.42.refs_2_, bf16[1024,2048]{1,0:T(8,128)(2,1)S(1)} %get-tuple-element.43.refs_3_, ...), custom_call_target="tpu_custom_call" | custom-call | flops 1073741824 | tf_op jit(solution)/shard_map/pallas_call | solution.py:304
  53.5 4.7 %collective-permute-done.14.low_ref = bf16[64,2176]{1,0:T(8,128)(2,1)S(1)} collective-permute-done((bf16[64,2176]{1,0:T(8,128)(2,1)S(1)}, bf16[64,2176]{1,0:T(8,128)(2,1)S(1)}, u32[]{:S(2)}, u32[]{:S(2)}) %collective-permute-start.14) | collective-permute-done | bytes 278560 | tf_op jit(solution)/shard_map/ppermute | solution.py:314
  58.2 2.2 %collective-permute-done.15.high_ref = bf16[64,2176]{1,0:T(8,128)(2,1)S(1)} collective-permute-done((bf16[64,2176]{1,0:T(8,128)(2,1)S(1)}, bf16[64,2176]{1,0:T(8,128)(2,1)S(1)}, u32[]{:S(2)}, u32[]{:S(2)}) %collective-permute-start.15) | collective-permute-done | bytes 278560 | tf_op jit(solution)/shard_map/ppermute | solution.py:315
  60.7 4.7 %collective-permute-start.16 = (bf16[32,2176]{1,0:T(8,128)(2,1)S(1)}, bf16[32,2176]{1,0:T(8,128)(2,1)S(1)}, u32[]{:S(2)}, u32[]{:S(2)}) collective-permute-start(bf16[32,2176]{1,0:T(8,128)(2,1)S(1)} %get-tuple-element.50), channel_id=1, source_target_pairs={{0,128},{64,192},{128,0},{192,64},{1,129},{65,193},{129,1},{193,65... | collective-permute-start | bytes 417800 | tf_op jit(solution)/shard_map/ppermute | solution.py:326
  65.3 2.0 %collective-permute-start.17 = (bf16[32,2176]{1,0:T(8,128)(2,1)S(1)}, bf16[32,2176]{1,0:T(8,128)(2,1)S(1)}, u32[]{:S(2)}, u32[]{:S(2)}) collective-permute-start(bf16[32,2176]{1,0:T(8,128)(2,1)S(1)} %get-tuple-element.51), channel_id=1, source_target_pairs={{0,64},{64,128},{128,192},{192,0},{1,65},{65,129},{129,193},{193,1... | collective-permute-start | bytes 417800 | tf_op jit(solution)/shard_map/ppermute | solution.py:326
  67.4 2.1 %collective-permute-start.18 = (bf16[32,2176]{1,0:T(8,128)(2,1)S(1)}, bf16[32,2176]{1,0:T(8,128)(2,1)S(1)}, u32[]{:S(2)}, u32[]{:S(2)}) collective-permute-start(bf16[32,2176]{1,0:T(8,128)(2,1)S(1)} %get-tuple-element.52), channel_id=1, source_target_pairs={{0,192},{64,0},{128,64},{192,128},{1,193},{65,1},{129,65},{193,129... | collective-permute-start | bytes 417800 | tf_op jit(solution)/shard_map/ppermute | solution.py:326
  69.5 0.5 bitcast_add_fusion
  70.0 9.8 %collective-permute-done.17.g1_ref = bf16[32,2176]{1,0:T(8,128)(2,1)S(1)} collective-permute-done((bf16[32,2176]{1,0:T(8,128)(2,1)S(1)}, bf16[32,2176]{1,0:T(8,128)(2,1)S(1)}, u32[]{:S(2)}, u32[]{:S(2)}) %collective-permute-start.17) | collective-permute-done | bytes 139296 | tf_op jit(solution)/shard_map/ppermute | solution.py:326
  79.8 0.5 shard_map.91
  80.3 16.2 %all-gather = bf16[128,2048]{1,0:T(8,128)(2,1)S(1)} all-gather(bf16[32,2048]{1,0:T(8,128)(2,1)S(1)} %get-tuple-element.53), channel_id=2, replica_groups=mesh['zh'=4,'x'=4,'y'=4,'zl'=2,'c'=2] {'zh'}, dimensions={0}, use_global_device_ids=true | all-gather | bytes 655360 | tf_op jit(solution)/shard_map/all_gather | solution.py:334
  96.5 1.0 %shard_map.92 = (f32[128,1024]{1,0:T(8,128)}, f32[128,1024]{1,0:T(8,128)}) custom-call(bf16[4,32,2048]{2,1,0:T(8,128)(2,1)S(1)} %bitcast.8), custom_call_target="tpu_custom_call" | custom-call | tf_op jit(solution)/shard_map/pallas_call | solution.py:334
  (38 shorter events, 1.7 us)
Async XLA Ops:
  0.6 12.7 %collective-permute-start = (bf16[64,1024]{1,0:T(8,128)(2,1)}, bf16[64,1024]{1,0:T(8,128)(2,1)S(1)}, u32[]{:S(2)}, u32[]{:S(2)}) collective-permute-start(bf16[64,1024]{1,0:T(8,128)(2,1)} %param.5), channel_id=1, source_target_pairs={{0,32},{16,48},{32,0},{48,16},{1,33},{17,49},{33,1},{49,17},{2,34}... | collective-permute-start | bytes 393224 | tf_op jit(solution)/shard_map/ppermute | solution.py:260
  3.7 9.9 %collective-permute-start.1 = (bf16[64,1024]{1,0:T(8,128)(2,1)}, bf16[64,1024]{1,0:T(8,128)(2,1)S(1)}, u32[]{:S(2)}, u32[]{:S(2)}) collective-permute-start(bf16[64,1024]{1,0:T(8,128)(2,1)} %param.5), channel_id=1, source_target_pairs={{0,16},{16,32},{32,48},{48,0},{1,17},{17,33},{33,49},{49,1},{2,18}... | collective-permute-start | bytes 393224 | tf_op jit(solution)/shard_map/ppermute | solution.py:260
  4.3 9.3 %collective-permute-start.2 = (bf16[64,1024]{1,0:T(8,128)(2,1)}, bf16[64,1024]{1,0:T(8,128)(2,1)S(1)}, u32[]{:S(2)}, u32[]{:S(2)}) collective-permute-start(bf16[64,1024]{1,0:T(8,128)(2,1)} %param.5), channel_id=1, source_target_pairs={{0,48},{16,0},{32,16},{48,32},{1,49},{17,1},{33,17},{49,33},{2,50}... | collective-permute-start | bytes 393224 | tf_op jit(solution)/shard_map/ppermute | solution.py:260
  7.0 8.8 %collective-permute-start.3 = (bf16[64,1024]{1,0:T(8,128)(2,1)}, bf16[64,1024]{1,0:T(8,128)(2,1)S(1)}, u32[]{:S(2)}, u32[]{:S(2)}) collective-permute-start(bf16[64,1024]{1,0:T(8,128)(2,1)} %param.5), channel_id=1, source_target_pairs={{0,4},{4,8},{8,12},{12,0},{1,5},{5,9},{9,13},{13,1},{2,6},{6,10},{... | collective-permute-start | bytes 393224 | tf_op jit(solution)/shard_map/ppermute | solution.py:259
  8.6 7.2 %collective-permute-start.4 = (bf16[64,1024]{1,0:T(8,128)(2,1)}, bf16[64,1024]{1,0:T(8,128)(2,1)S(1)}, u32[]{:S(2)}, u32[]{:S(2)}) collective-permute-start(bf16[64,1024]{1,0:T(8,128)(2,1)} %param.5), channel_id=1, source_target_pairs={{0,12},{4,0},{8,4},{12,8},{1,13},{5,1},{9,5},{13,9},{2,14},{6,2},{... | collective-permute-start | bytes 393224 | tf_op jit(solution)/shard_map/ppermute | solution.py:259
  13.4 13.1 %collective-permute-start.5 = (bf16[128,2176]{1,0:T(8,128)(2,1)S(1)}, bf16[128,2176]{1,0:T(8,128)(2,1)S(1)}, u32[]{:S(2)}, u32[]{:S(2)}) collective-permute-start(bf16[128,2176]{1,0:T(8,128)(2,1)S(1)} %shard_map.84), channel_id=1, source_target_pairs={{0,2},{2,0},{1,3},{3,1},{4,6},{6,4},{5,7},{7,5},{8,10},{10,8},{9,1... | collective-permute-start | bytes 1671176 | tf_op jit(solution)/shard_map/ppermute | solution.py:274
  13.7 16.7 %copy-start.1 = (s32[64]{0:T(128)S(1)}, s32[64]{0:T(128)}, u32[]{:S(2)}) copy-start(s32[64]{0:T(128)} %param.6) | copy-start | bytes 772
  13.7 15.6 %collective-permute-start.6 = (bf16[256,1024]{1,0:T(8,128)(2,1)S(1)}, bf16[256,1024]{1,0:T(8,128)(2,1)S(1)}, u32[]{:S(2)}, u32[]{:S(2)}) collective-permute-start(bf16[256,1024]{1,0:T(8,128)(2,1)S(1)} %constant_dynamic-update-slice_fusion.e0_ref), channel_id=1, source_target_pairs={{0,8},{4,12},{8,0},{12,4},{1,9},{5,13},{9,1},{13,5},{2,10},{6,14},... | collective-permute-start | bytes 1572872 | tf_op jit(solution)/shard_map/ppermute | solution.py:275
  15.8 10.8 %collective-permute-start.7 = (bf16[128,1024]{1,0:T(8,128)(2,1)S(1)}, bf16[128,1024]{1,0:T(8,128)(2,1)S(1)}, u32[]{:S(2)}, u32[]{:S(2)}) collective-permute-start(bf16[128,1024]{1,0:T(8,128)(2,1)S(1)} %get-tuple-element.61), channel_id=1, source_target_pairs={{0,32},{16,48},{32,0},{48,16},{1,33},{17,49},{33,1},{49,17},{2,34}... | collective-permute-start | bytes 786440 | tf_op jit(solution)/shard_map/ppermute | solution.py:276
  16.2 13.1 %collective-permute-start.8 = (bf16[128,1024]{1,0:T(8,128)(2,1)S(1)}, bf16[128,1024]{1,0:T(8,128)(2,1)S(1)}, u32[]{:S(2)}, u32[]{:S(2)}) collective-permute-start(bf16[128,1024]{1,0:T(8,128)(2,1)S(1)} %get-tuple-element.61), channel_id=1, source_target_pairs={{0,16},{16,32},{32,48},{48,0},{1,17},{17,33},{33,49},{49,1},{2,18}... | collective-permute-start | bytes 786440 | tf_op jit(solution)/shard_map/ppermute | solution.py:276
  18.0 11.2 %collective-permute-start.9 = (bf16[128,1024]{1,0:T(8,128)(2,1)S(1)}, bf16[128,1024]{1,0:T(8,128)(2,1)S(1)}, u32[]{:S(2)}, u32[]{:S(2)}) collective-permute-start(bf16[128,1024]{1,0:T(8,128)(2,1)S(1)} %get-tuple-element.61), channel_id=1, source_target_pairs={{0,48},{16,0},{32,16},{48,32},{1,49},{17,1},{33,17},{49,33},{2,50}... | collective-permute-start | bytes 786440 | tf_op jit(solution)/shard_map/ppermute | solution.py:276
  26.5 5.4 %collective-permute-start.10 = (bf16[256,1024]{1,0:T(8,128)(2,1)S(1)}, bf16[256,1024]{1,0:T(8,128)(2,1)S(1)}, u32[]{:S(2)}, u32[]{:S(2)}) collective-permute-start(bf16[256,1024]{1,0:T(8,128)(2,1)S(1)} %constant_dynamic-update-slice_fusion.e0_ref), channel_id=1, source_target_pairs={{0,1},{1,0},{2,3},{3,2},{4,5},{5,4},{6,7},{7,6},{8,9},{9,8},{10,11... | collective-permute-start | bytes 1572872 | tf_op jit(solution)/shard_map/ppermute | solution.py:280
  29.3 2.6 %collective-permute-start.12 = (bf16[256,1024]{1,0:T(8,128)(2,1)S(1)}, bf16[256,1024]{1,0:T(8,128)(2,1)S(1)}, u32[]{:S(2)}, u32[]{:S(2)}) collective-permute-start(bf16[256,1024]{1,0:T(8,128)(2,1)S(1)} %constant_dynamic-update-slice_fusion.9.e2_ref), channel_id=1, source_target_pairs={{0,1},{1,0},{2,3},{3,2},{4,5},{5,4},{6,7},{7,6},{8,9},{9,8},{10,11... | collective-permute-start | bytes 1572872 | tf_op jit(solution)/shard_map/ppermute | solution.py:280
  29.5 2.6 %collective-permute-start.11 = (bf16[256,1024]{1,0:T(8,128)(2,1)S(1)}, bf16[256,1024]{1,0:T(8,128)(2,1)S(1)}, u32[]{:S(2)}, u32[]{:S(2)}) collective-permute-start(bf16[256,1024]{1,0:T(8,128)(2,1)S(1)} %constant_dynamic-update-slice_fusion.6.e1_ref), channel_id=1, source_target_pairs={{0,1},{1,0},{2,3},{3,2},{4,5},{5,4},{6,7},{7,6},{8,9},{9,8},{10,11... | collective-permute-start | bytes 1572872 | tf_op jit(solution)/shard_map/ppermute | solution.py:280
  30.0 2.8 %collective-permute-start.13 = (bf16[256,1024]{1,0:T(8,128)(2,1)S(1)}, bf16[256,1024]{1,0:T(8,128)(2,1)S(1)}, u32[]{:S(2)}, u32[]{:S(2)}) collective-permute-start(bf16[256,1024]{1,0:T(8,128)(2,1)S(1)} %collective-permute-done.6.e3_ref), channel_id=1, source_target_pairs={{0,1},{1,0},{2,3},{3,2},{4,5},{5,4},{6,7},{7,6},{8,9},{9,8},{10,11... | collective-permute-start | bytes 1572872 | tf_op jit(solution)/shard_map/ppermute | solution.py:280
  47.4 4.4 %copy-start = (bf16[64,1024]{1,0:T(8,128)(2,1)S(1)}, bf16[64,1024]{1,0:T(8,128)(2,1)}, u32[]{:S(2)}) copy-start(bf16[64,1024]{1,0:T(8,128)(2,1)} %param.5) | copy-start | bytes 393220
  49.0 9.2 %collective-permute-start.14 = (bf16[64,2176]{1,0:T(8,128)(2,1)S(1)}, bf16[64,2176]{1,0:T(8,128)(2,1)S(1)}, u32[]{:S(2)}, u32[]{:S(2)}) collective-permute-start(bf16[64,2176]{1,0:T(8,128)(2,1)S(1)} %get-tuple-element.46), channel_id=1, source_target_pairs={{0,2},{2,64},{64,66},{66,128},{128,130},{130,192},{192,194},{194,0... | collective-permute-start | bytes 835592 | tf_op jit(solution)/shard_map/ppermute | solution.py:314
  51.8 8.6 %collective-permute-start.15 = (bf16[64,2176]{1,0:T(8,128)(2,1)S(1)}, bf16[64,2176]{1,0:T(8,128)(2,1)S(1)}, u32[]{:S(2)}, u32[]{:S(2)}) collective-permute-start(bf16[64,2176]{1,0:T(8,128)(2,1)S(1)} %get-tuple-element.48), channel_id=1, source_target_pairs={{0,194},{2,0},{64,2},{66,64},{128,66},{130,128},{192,130},{194,192... | collective-permute-start | bytes 835592 | tf_op jit(solution)/shard_map/ppermute | solution.py:315
  60.7 9.3 %collective-permute-start.16 = (bf16[32,2176]{1,0:T(8,128)(2,1)S(1)}, bf16[32,2176]{1,0:T(8,128)(2,1)S(1)}, u32[]{:S(2)}, u32[]{:S(2)}) collective-permute-start(bf16[32,2176]{1,0:T(8,128)(2,1)S(1)} %get-tuple-element.50), channel_id=1, source_target_pairs={{0,128},{64,192},{128,0},{192,64},{1,129},{65,193},{129,1},{193,65... | collective-permute-start | bytes 417800 | tf_op jit(solution)/shard_map/ppermute | solution.py:326
  65.3 14.4 %collective-permute-start.17 = (bf16[32,2176]{1,0:T(8,128)(2,1)S(1)}, bf16[32,2176]{1,0:T(8,128)(2,1)S(1)}, u32[]{:S(2)}, u32[]{:S(2)}) collective-permute-start(bf16[32,2176]{1,0:T(8,128)(2,1)S(1)} %get-tuple-element.51), channel_id=1, source_target_pairs={{0,64},{64,128},{128,192},{192,0},{1,65},{65,129},{129,193},{193,1... | collective-permute-start | bytes 417800 | tf_op jit(solution)/shard_map/ppermute | solution.py:326
  67.4 12.4 %collective-permute-start.18 = (bf16[32,2176]{1,0:T(8,128)(2,1)S(1)}, bf16[32,2176]{1,0:T(8,128)(2,1)S(1)}, u32[]{:S(2)}, u32[]{:S(2)}) collective-permute-start(bf16[32,2176]{1,0:T(8,128)(2,1)S(1)} %get-tuple-element.52), channel_id=1, source_target_pairs={{0,192},{64,0},{128,64},{192,128},{1,193},{65,1},{129,65},{193,129... | collective-permute-start | bytes 417800 | tf_op jit(solution)/shard_map/ppermute | solution.py:326

commit v6 on v5

--- a/solution.py
+++ b/solution.py
@@ -89,14 +89,15 @@
     return lax.rem(x + 4 - back_x, 4) * 4 + lax.rem(y + 4 - back_y, 4)
 
 
-def score_kernel(e0_ref, e1_ref, e2_ref, e3_ref, coef_ref, s_ref, lse_ref, feats_ref):
-    rows, width = e0_ref.shape
+def score_kernel(*refs):
+    *e_refs, coef_ref, s_ref, lse_ref, feats_ref = refs
+    rows, width = e_refs[0].shape
     offset = jnp.sum(coef_ref[:, 2 * width :].astype(F32), axis=1, keepdims=True)
-    for i, e_ref in enumerate((e0_ref, e1_ref, e2_ref, e3_ref)):
+    for i, e_ref in enumerate(e_refs):
         at = slice(i * rows, (i + 1) * rows)
         feats_ref[at, :width] = square(e_ref[...])
         feats_ref[at, width:] = e_ref[...]
-    for i in range(2):
+    for i in range(len(e_refs) // 2):
         at = slice(i * 2 * rows, (i + 1) * 2 * rows)
         s = offset + lax.dot_general(
             coef_ref[:, : 2 * width], feats_ref[at, :], NT, preferred_element_type=F32
@@ -106,12 +107,14 @@
         lse_ref[:, at] = top + jnp.log(jnp.sum(jnp.exp(s - top), axis=0, keepdims=True))
 
 
-def pay_kernel(keep_ref, own_ref, other_ref, pay_ref, true_ref):
+def pay_kernel(keep_ref, own_ref, other_a_ref, other_b_ref, pay_ref, true_ref):
     lane = lax.broadcasted_iota(jnp.int32, (1, 128), 1)
     first = lax.axis_index("c") == 0
     for i in range(16):
         at = slice((i // 2) * 128, (i // 2 + 1) * 128)
-        own, other = own_ref[:, at], other_ref[:, at]
+        own = own_ref[:, at]
+        there = slice(at.start % 512, at.start % 512 + 128)
+        other = (other_a_ref if i < 8 else other_b_ref)[:, there]
         if i == 0:
             true_ref[...] = own
             own = jnp.where((lane < 64) & (keep_ref[...] == 0.0), DROPPED, own)
@@ -129,7 +132,7 @@
 
 
 def moment_body(at_comp, refs, lse_ref):
-    pay_ref, s_refs, feats_refs = refs[0], refs[1:3], refs[3:5]
+    pay_ref, s_refs, feats_refs = refs[0], refs[1:4], refs[4:7]
     comps = 128
     lse = logsumexp(pay_ref[...])
     lse_ref[0] = lse
@@ -140,13 +143,14 @@
     moments = None
     for i, (s_ref, feats_ref) in enumerate(zip(s_refs, feats_refs, strict=True)):
         half = core if i == 0 else 1 - core
+        skip = 4 if i == 2 else 0
         ps = []
-        for j in range(8):
+        for j in range(skip, skip + s_ref.shape[1] // 128):
             left, right = (slot(j // 2, 2 * (j % 2) + k) for k in range(2))
             there = jnp.where(
                 lane < 64, lse_ref[half, pl.ds(left, 1), :], lse_ref[1 - half, pl.ds(right, 1), :]
             )
-            s = s_ref[at_comp : at_comp + comps, j * 128 : (j + 1) * 128]
+            s = s_ref[at_comp : at_comp + comps, (j - skip) * 128 : (j - skip + 1) * 128]
             p = jnp.exp(s - there).astype(BF16)
             total = total + p.astype(F32)
             ps.append(p)
@@ -285,26 +289,26 @@
             call(
                 score_kernel,
                 (
-                    sds((2 * comps, n_rows), F32),
-                    sds((1, n_rows), F32),
-                    sds((n_rows, 2 * width), BF16),
+                    sds((2 * comps, len(es) * 4 * own), F32),
+                    sds((1, len(es) * 4 * own), F32),
+                    sds((len(es) * 4 * own, 2 * width), BF16),
                 ),
-                5,
-                flops,
+                len(es) + 1,
+                flops * len(es) // 4,
             )(*es, coef)
-            for es in (groups[:4], groups[4:])
+            for es in (groups[:4], groups[4:6], groups[6:])
         ]
     )
     flag = jnp.pad(keep.astype(F32), (0, own)).reshape(1, 2 * own)
     lse_row = sds((1, 128), F32)
-    pay, true = call(pay_kernel, (sds((16, 128), F32), lse_row), 3)(flag, *lses)
+    pay, true = call(pay_kernel, (sds((16, 128), F32), lse_row), 4)(flag, *lses)
     pays = lax.all_to_all(jnp.broadcast_to(pay[None], (32,) + pay.shape), plane + (core,), 0, 0)
 
     def moments(kernel, at, outs, *more):
         return call(
             functools.partial(kernel, at),
             outs,
-            5 + len(more),
+            7 + len(more),
             flops,
             scratch_shapes=[pltpu.VMEM((2, 16, 128), F32)],
         )(pays, *scores, *feats, *more)

time: 98.7 us -> 98.3 us (level)
    pallas_call x5 -> x6, Pallas kernels: 6.35 us -> 6.57 us  [the longest x3 3.31 us: local(): call(score_kernel, (sds((2 * comps, len(es) * 4 * own), F32), sds((1, len...]
  transfers between devices with their start and end apart: 19 -> 19, of which waited for: 7 -> 6; matrix products, arithmetic and copies ran while one was open for 4% -> 4% of each run, Pallas kernels for 3% -> 4%
where the time goes in v6:
time: 98.3 us; the launch traced here: 97.1 us
  blocking collectives  29.2 us (30%)
  starting transfers between devices  28 us (28%)
  waiting for transfers between devices  26.7 us (27%)
  Pallas kernels  8.54 us (9%)
  other arithmetic  2.85 us (3%)
  local copies, waits for them, and re-layouts  1.07 us (1%)
    all_gather x1, blocking collectives, local(): lax.all_gather(result, 'zh')  16.3 us
    all_to_all x1, blocking collectives, local(): lax.all_to_all(jnp.broadcast_to(pay[None], (32,) + pay.shape), plane + (c...  12.9 us
    ppermute x3, waiting for transfers between devices, local(): lax.ppermute(s, 'zh', ring(4, i))  9.76 us
    ppermute x3, starting transfers between devices, local(): lax.ppermute(s, 'zh', ring(4, i))  8.79 us
    ppermute x1, waiting for transfers between devices, local(): coef = jnp.concatenate([coef, lax.ppermute(coef, 'zl', ring(2, 1))], axis=0)  7.1 us
    ppermute x3, starting transfers between devices, local(): lax.ppermute(embeddings, 'x', ring(4, s))  6.35 us
    ppermute x1, waiting for transfers between devices, local(): low = lax.ppermute(up, z, ring(8, 1))  4.7 us
    ppermute x3, starting transfers between devices, local(): rest = [lax.ppermute(pair, 'x', ring(4, s)) for s in SHIFTS[1:]]  3.59 us
  transfers between devices with their start and end apart: 19, of which 6 were waited for; matrix products, arithmetic and copies ran while one was open for 4% of the time, Pallas kernels for 4%

profile of v6, /device:TPU:32, one launch (start us, length us, event | category | flops | bytes accessed | tf_op | source)
XLA Modules:
  0.0 97.1 jit_solution(12909157300085597870)
XLA Ops:
  0.6 3.1 %collective-permute-start = (bf16[64,1024]{1,0:T(8,128)(2,1)}, bf16[64,1024]{1,0:T(8,128)(2,1)S(1)}, u32[]{:S(2)}, u32[]{:S(2)}) collective-permute-start(bf16[64,1024]{1,0:T(8,128)(2,1)} %param.5), channel_id=1, source_target_pairs={{0,32},{16,48},{32,0},{48,16},{1,33},{17,49},{33,1},{49,17},{2,34}... | collective-permute-start | bytes 393224 | tf_op jit(solution)/shard_map/ppermute | solution.py:264
  3.7 0.6 collective-permute-start.1
  4.3 2.6 %collective-permute-start.2 = (bf16[64,1024]{1,0:T(8,128)(2,1)}, bf16[64,1024]{1,0:T(8,128)(2,1)S(1)}, u32[]{:S(2)}, u32[]{:S(2)}) collective-permute-start(bf16[64,1024]{1,0:T(8,128)(2,1)} %param.5), channel_id=1, source_target_pairs={{0,48},{16,0},{32,16},{48,32},{1,49},{17,1},{33,17},{49,33},{2,50}... | collective-permute-start | bytes 393224 | tf_op jit(solution)/shard_map/ppermute | solution.py:264
  7.0 1.6 %collective-permute-start.3 = (bf16[64,1024]{1,0:T(8,128)(2,1)}, bf16[64,1024]{1,0:T(8,128)(2,1)S(1)}, u32[]{:S(2)}, u32[]{:S(2)}) collective-permute-start(bf16[64,1024]{1,0:T(8,128)(2,1)} %param.5), channel_id=1, source_target_pairs={{0,4},{4,8},{8,12},{12,0},{1,5},{5,9},{9,13},{13,1},{2,6},{6,10},{... | collective-permute-start | bytes 393224 | tf_op jit(solution)/shard_map/ppermute | solution.py:263
  8.6 1.7 %collective-permute-start.4 = (bf16[64,1024]{1,0:T(8,128)(2,1)}, bf16[64,1024]{1,0:T(8,128)(2,1)S(1)}, u32[]{:S(2)}, u32[]{:S(2)}) collective-permute-start(bf16[64,1024]{1,0:T(8,128)(2,1)} %param.5), channel_id=1, source_target_pairs={{0,12},{4,0},{8,4},{12,8},{1,13},{5,1},{9,5},{13,9},{2,14},{6,2},{... | collective-permute-start | bytes 393224 | tf_op jit(solution)/shard_map/ppermute | solution.py:263
  10.2 1.5 %add_reduce_fusion = (f32[128]{0:T(128)S(1)}, bf16[128,1024]{1,0:T(8,128)(2,1)S(1)}, bf16[128,1024]{1,0:T(8,128)(2,1)S(1)}) fusion(f32[128,1024]{1,0:T(8,128)} %param.8, f32[128,1024]{1,0:T(8,128)} %param.7), kind=kLoop, calls=%fused_computation.1 | loop fusion | flops 1179520 | bytes 1573376 | tf_op jit(solution)/shard_map/reduce_sum | solution.py:270
  11.7 0.7 add_bitcast_fusion.offset_ref
  12.3 0.9 constant_dynamic-update-slice_fusion.3
  13.7 2.1 %collective-permute-start.6 = (bf16[256,1024]{1,0:T(8,128)(2,1)S(1)}, bf16[256,1024]{1,0:T(8,128)(2,1)S(1)}, u32[]{:S(2)}, u32[]{:S(2)}) collective-permute-start(bf16[256,1024]{1,0:T(8,128)(2,1)S(1)} %constant_dynamic-update-slice_fusion.refs_0_), channel_id=1, source_target_pairs={{0,8},{4,12},{8,0},{12,4},{1,9},{5,13},{9,1},{13,5},{2,10},{6,14},... | collective-permute-start | bytes 1572872 | tf_op jit(solution)/shard_map/ppermute | solution.py:279
  16.2 1.9 %collective-permute-start.8 = (bf16[128,1024]{1,0:T(8,128)(2,1)S(1)}, bf16[128,1024]{1,0:T(8,128)(2,1)S(1)}, u32[]{:S(2)}, u32[]{:S(2)}) collective-permute-start(bf16[128,1024]{1,0:T(8,128)(2,1)S(1)} %get-tuple-element.67), channel_id=1, source_target_pairs={{0,16},{16,32},{32,48},{48,0},{1,17},{17,33},{33,49},{49,1},{2,18}... | collective-permute-start | bytes 786440 | tf_op jit(solution)/shard_map/ppermute | solution.py:280
  18.0 1.3 %collective-permute-start.9 = (bf16[128,1024]{1,0:T(8,128)(2,1)S(1)}, bf16[128,1024]{1,0:T(8,128)(2,1)S(1)}, u32[]{:S(2)}, u32[]{:S(2)}) collective-permute-start(bf16[128,1024]{1,0:T(8,128)(2,1)S(1)} %get-tuple-element.67), channel_id=1, source_target_pairs={{0,48},{16,0},{32,16},{48,32},{1,49},{17,1},{33,17},{49,33},{2,50}... | collective-permute-start | bytes 786440 | tf_op jit(solution)/shard_map/ppermute | solution.py:280
  19.4 7.1 %collective-permute-done.5 = bf16[128,2176]{1,0:T(8,128)(2,1)S(1)} collective-permute-done((bf16[128,2176]{1,0:T(8,128)(2,1)S(1)}, bf16[128,2176]{1,0:T(8,128)(2,1)S(1)}, u32[]{:S(2)}, u32[]{:S(2)}) %collective-permute-start.5) | collective-permute-done | bytes 557088 | tf_op jit(solution)/shard_map/ppermute | solution.py:278
  26.6 2.7 %collective-permute-done.8 = bf16[128,1024]{1,0:T(8,128)(2,1)S(1)} collective-permute-done((bf16[128,1024]{1,0:T(8,128)(2,1)S(1)}, bf16[128,1024]{1,0:T(8,128)(2,1)S(1)}, u32[]{:S(2)}, u32[]{:S(2)}) %collective-permute-start.8) | collective-permute-done | bytes 262176 | tf_op jit(solution)/shard_map/ppermute | solution.py:280
  29.4 0.5 collective-permute-start.13
  30.0 0.4 collective-permute-start.11
  30.3 1.5 %shard_map.85 = (f32[256,1024]{1,0:T(8,128)S(1)}, f32[1,1024]{1,0:T(1,128)S(1)}, bf16[1024,2048]{1,0:T(8,128)(2,1)S(1)}) custom-call(bf16[256,1024]{1,0:T(8,128)(2,1)S(1)} %constant_dynamic-update-slice_fusion.refs_0_, bf16[256,1024]{1,0:T(8,128)(2,1)S(1)} %constant_dynamic-update-slice_fusion.6.refs_1_, ...), custom_call_target="tpu_custom_call" | custom-call | flops 1073741824 | tf_op jit(solution)/shard_map/pallas_call | solution.py:289
  32.1 0.9 shard_map.87
  33.0 0.9 shard_map.86
  34.0 12.9 %all_to_all.5.refs_0_ = f32[32,16,128]{2,1,0:T(8,128)S(1)} all-to-all(f32[32,16,128]{2,1,0:T(8,128)S(1)} %broadcast_in_dim.10), channel_id=1, replica_groups=mesh['zh'=4,'x'=4,'y'=4,'zl'=2,'c'=2] {'x','y','c'}, dimensions={0} | all-to-all | bytes 524288 | tf_op jit(solution)/shard_map/all_to_all | solution.py:305
  46.9 1.6 %shard_map.89 = (bf16[64,2176]{1,0:T(8,128)(2,1)S(1)}, bf16[64,2176]{1,0:T(8,128)(2,1)S(1)}, f32[1,128]{1,0:T(1,128)S(1)}) custom-call(f32[32,16,128]{2,1,0:T(8,128)S(1)} %all_to_all.5.refs_0_, f32[256,1024]{1,0:T(8,128)S(1)} %get-tuple-element.45.refs_1_, f32[256,512]{1,0:T(8,128)S(1)} %get-tuple-element.46.refs_2_, ...), custom_call_target="tpu_custom_call" | custom-call | flops 1073741824 | tf_op jit(solution)/shard_map/pallas_call | solution.py:308
  48.5 2.8 %collective-permute-start.14 = (bf16[64,2176]{1,0:T(8,128)(2,1)S(1)}, bf16[64,2176]{1,0:T(8,128)(2,1)S(1)}, u32[]{:S(2)}, u32[]{:S(2)}) collective-permute-start(bf16[64,2176]{1,0:T(8,128)(2,1)S(1)} %get-tuple-element.52), channel_id=1, source_target_pairs={{0,2},{2,64},{64,66},{66,128},{128,130},{130,192},{192,194},{194,0... | collective-permute-start | bytes 835592 | tf_op jit(solution)/shard_map/ppermute | solution.py:318
  51.4 1.6 %shard_map.90.mine_ref = f32[128,2176]{1,0:T(8,128)S(1)} custom-call(f32[32,16,128]{2,1,0:T(8,128)S(1)} %all_to_all.5.refs_0_, f32[256,1024]{1,0:T(8,128)S(1)} %get-tuple-element.45.refs_1_, f32[256,512]{1,0:T(8,128)S(1)} %get-tuple-element.46.refs_2_, f32[256,512]{1,0:T(8,128)S(1)} %get-tuple-element.47.refs_3_, ...), custom_call_target="tpu_custom_call" | custom-call | flops 1073741824 | tf_op jit(solution)/shard_map/pallas_call | solution.py:308
  53.0 4.7 %collective-permute-done.14.low_ref = bf16[64,2176]{1,0:T(8,128)(2,1)S(1)} collective-permute-done((bf16[64,2176]{1,0:T(8,128)(2,1)S(1)}, bf16[64,2176]{1,0:T(8,128)(2,1)S(1)}, u32[]{:S(2)}, u32[]{:S(2)}) %collective-permute-start.14) | collective-permute-done | bytes 278560 | tf_op jit(solution)/shard_map/ppermute | solution.py:318
  57.7 2.2 %collective-permute-done.15.high_ref = bf16[64,2176]{1,0:T(8,128)(2,1)S(1)} collective-permute-done((bf16[64,2176]{1,0:T(8,128)(2,1)S(1)}, bf16[64,2176]{1,0:T(8,128)(2,1)S(1)}, u32[]{:S(2)}, u32[]{:S(2)}) %collective-permute-start.15) | collective-permute-done | bytes 278560 | tf_op jit(solution)/shard_map/ppermute | solution.py:319
  60.2 4.7 %collective-permute-start.16 = (bf16[32,2176]{1,0:T(8,128)(2,1)S(1)}, bf16[32,2176]{1,0:T(8,128)(2,1)S(1)}, u32[]{:S(2)}, u32[]{:S(2)}) collective-permute-start(bf16[32,2176]{1,0:T(8,128)(2,1)S(1)} %get-tuple-element.56), channel_id=1, source_target_pairs={{0,128},{64,192},{128,0},{192,64},{1,129},{65,193},{129,1},{193,65... | collective-permute-start | bytes 417800 | tf_op jit(solution)/shard_map/ppermute | solution.py:330
  64.9 2.0 %collective-permute-start.17 = (bf16[32,2176]{1,0:T(8,128)(2,1)S(1)}, bf16[32,2176]{1,0:T(8,128)(2,1)S(1)}, u32[]{:S(2)}, u32[]{:S(2)}) collective-permute-start(bf16[32,2176]{1,0:T(8,128)(2,1)S(1)} %get-tuple-element.57), channel_id=1, source_target_pairs={{0,64},{64,128},{128,192},{192,0},{1,65},{65,129},{129,193},{193,1... | collective-permute-start | bytes 417800 | tf_op jit(solution)/shard_map/ppermute | solution.py:330
  66.9 2.1 %collective-permute-start.18 = (bf16[32,2176]{1,0:T(8,128)(2,1)S(1)}, bf16[32,2176]{1,0:T(8,128)(2,1)S(1)}, u32[]{:S(2)}, u32[]{:S(2)}) collective-permute-start(bf16[32,2176]{1,0:T(8,128)(2,1)S(1)} %get-tuple-element.58), channel_id=1, source_target_pairs={{0,192},{64,0},{128,64},{192,128},{1,193},{65,1},{129,65},{193,129... | collective-permute-start | bytes 417800 | tf_op jit(solution)/shard_map/ppermute | solution.py:330
  69.0 0.5 bitcast_add_fusion
  69.5 9.8 %collective-permute-done.17.g1_ref = bf16[32,2176]{1,0:T(8,128)(2,1)S(1)} collective-permute-done((bf16[32,2176]{1,0:T(8,128)(2,1)S(1)}, bf16[32,2176]{1,0:T(8,128)(2,1)S(1)}, u32[]{:S(2)}, u32[]{:S(2)}) %collective-permute-start.17) | collective-permute-done | bytes 139296 | tf_op jit(solution)/shard_map/ppermute | solution.py:330
  79.3 0.5 shard_map.92
  79.8 16.3 %all-gather = bf16[128,2048]{1,0:T(8,128)(2,1)S(1)} all-gather(bf16[32,2048]{1,0:T(8,128)(2,1)S(1)} %get-tuple-element.59), channel_id=2, replica_groups=mesh['zh'=4,'x'=4,'y'=4,'zl'=2,'c'=2] {'zh'}, dimensions={0}, use_global_device_ids=true | all-gather | bytes 655360 | tf_op jit(solution)/shard_map/all_gather | solution.py:338
  96.1 1.0 %shard_map.93 = (f32[128,1024]{1,0:T(8,128)}, f32[128,1024]{1,0:T(8,128)}) custom-call(bf16[4,32,2048]{2,1,0:T(8,128)(2,1)S(1)} %bitcast.8), custom_call_target="tpu_custom_call" | custom-call | tf_op jit(solution)/shard_map/pallas_call | solution.py:338
  (39 shorter events, 1.8 us)
Async XLA Ops:
  0.6 12.7 %collective-permute-start = (bf16[64,1024]{1,0:T(8,128)(2,1)}, bf16[64,1024]{1,0:T(8,128)(2,1)S(1)}, u32[]{:S(2)}, u32[]{:S(2)}) collective-permute-start(bf16[64,1024]{1,0:T(8,128)(2,1)} %param.5), channel_id=1, source_target_pairs={{0,32},{16,48},{32,0},{48,16},{1,33},{17,49},{33,1},{49,17},{2,34}... | collective-permute-start | bytes 393224 | tf_op jit(solution)/shard_map/ppermute | solution.py:264
  3.7 9.9 %collective-permute-start.1 = (bf16[64,1024]{1,0:T(8,128)(2,1)}, bf16[64,1024]{1,0:T(8,128)(2,1)S(1)}, u32[]{:S(2)}, u32[]{:S(2)}) collective-permute-start(bf16[64,1024]{1,0:T(8,128)(2,1)} %param.5), channel_id=1, source_target_pairs={{0,16},{16,32},{32,48},{48,0},{1,17},{17,33},{33,49},{49,1},{2,18}... | collective-permute-start | bytes 393224 | tf_op jit(solution)/shard_map/ppermute | solution.py:264
  4.3 9.3 %collective-permute-start.2 = (bf16[64,1024]{1,0:T(8,128)(2,1)}, bf16[64,1024]{1,0:T(8,128)(2,1)S(1)}, u32[]{:S(2)}, u32[]{:S(2)}) collective-permute-start(bf16[64,1024]{1,0:T(8,128)(2,1)} %param.5), channel_id=1, source_target_pairs={{0,48},{16,0},{32,16},{48,32},{1,49},{17,1},{33,17},{49,33},{2,50}... | collective-permute-start | bytes 393224 | tf_op jit(solution)/shard_map/ppermute | solution.py:264
  7.0 8.7 %collective-permute-start.3 = (bf16[64,1024]{1,0:T(8,128)(2,1)}, bf16[64,1024]{1,0:T(8,128)(2,1)S(1)}, u32[]{:S(2)}, u32[]{:S(2)}) collective-permute-start(bf16[64,1024]{1,0:T(8,128)(2,1)} %param.5), channel_id=1, source_target_pairs={{0,4},{4,8},{8,12},{12,0},{1,5},{5,9},{9,13},{13,1},{2,6},{6,10},{... | collective-permute-start | bytes 393224 | tf_op jit(solution)/shard_map/ppermute | solution.py:263
  8.6 7.2 %collective-permute-start.4 = (bf16[64,1024]{1,0:T(8,128)(2,1)}, bf16[64,1024]{1,0:T(8,128)(2,1)S(1)}, u32[]{:S(2)}, u32[]{:S(2)}) collective-permute-start(bf16[64,1024]{1,0:T(8,128)(2,1)} %param.5), channel_id=1, source_target_pairs={{0,12},{4,0},{8,4},{12,8},{1,13},{5,1},{9,5},{13,9},{2,14},{6,2},{... | collective-permute-start | bytes 393224 | tf_op jit(solution)/shard_map/ppermute | solution.py:263
  13.4 13.1 %collective-permute-start.5 = (bf16[128,2176]{1,0:T(8,128)(2,1)S(1)}, bf16[128,2176]{1,0:T(8,128)(2,1)S(1)}, u32[]{:S(2)}, u32[]{:S(2)}) collective-permute-start(bf16[128,2176]{1,0:T(8,128)(2,1)S(1)} %shard_map.84), channel_id=1, source_target_pairs={{0,2},{2,0},{1,3},{3,1},{4,6},{6,4},{5,7},{7,5},{8,10},{10,8},{9,1... | collective-permute-start | bytes 1671176 | tf_op jit(solution)/shard_map/ppermute | solution.py:278
  13.7 15.6 %collective-permute-start.6 = (bf16[256,1024]{1,0:T(8,128)(2,1)S(1)}, bf16[256,1024]{1,0:T(8,128)(2,1)S(1)}, u32[]{:S(2)}, u32[]{:S(2)}) collective-permute-start(bf16[256,1024]{1,0:T(8,128)(2,1)S(1)} %constant_dynamic-update-slice_fusion.refs_0_), channel_id=1, source_target_pairs={{0,8},{4,12},{8,0},{12,4},{1,9},{5,13},{9,1},{13,5},{2,10},{6,14},... | collective-permute-start | bytes 1572872 | tf_op jit(solution)/shard_map/ppermute | solution.py:279
  15.8 14.6 %copy-start.1 = (s32[64]{0:T(128)S(1)}, s32[64]{0:T(128)}, u32[]{:S(2)}) copy-start(s32[64]{0:T(128)} %param.6) | copy-start | bytes 772
  15.8 10.8 %collective-permute-start.7 = (bf16[128,1024]{1,0:T(8,128)(2,1)S(1)}, bf16[128,1024]{1,0:T(8,128)(2,1)S(1)}, u32[]{:S(2)}, u32[]{:S(2)}) collective-permute-start(bf16[128,1024]{1,0:T(8,128)(2,1)S(1)} %get-tuple-element.67), channel_id=1, source_target_pairs={{0,32},{16,48},{32,0},{48,16},{1,33},{17,49},{33,1},{49,17},{2,34}... | collective-permute-start | bytes 786440 | tf_op jit(solution)/shard_map/ppermute | solution.py:280
  16.2 13.1 %collective-permute-start.8 = (bf16[128,1024]{1,0:T(8,128)(2,1)S(1)}, bf16[128,1024]{1,0:T(8,128)(2,1)S(1)}, u32[]{:S(2)}, u32[]{:S(2)}) collective-permute-start(bf16[128,1024]{1,0:T(8,128)(2,1)S(1)} %get-tuple-element.67), channel_id=1, source_target_pairs={{0,16},{16,32},{32,48},{48,0},{1,17},{17,33},{33,49},{49,1},{2,18}... | collective-permute-start | bytes 786440 | tf_op jit(solution)/shard_map/ppermute | solution.py:280
  18.0 11.2 %collective-permute-start.9 = (bf16[128,1024]{1,0:T(8,128)(2,1)S(1)}, bf16[128,1024]{1,0:T(8,128)(2,1)S(1)}, u32[]{:S(2)}, u32[]{:S(2)}) collective-permute-start(bf16[128,1024]{1,0:T(8,128)(2,1)S(1)} %get-tuple-element.67), channel_id=1, source_target_pairs={{0,48},{16,0},{32,16},{48,32},{1,49},{17,1},{33,17},{49,33},{2,50}... | collective-permute-start | bytes 786440 | tf_op jit(solution)/shard_map/ppermute | solution.py:280
  26.5 6.5 %collective-permute-start.10 = (bf16[256,1024]{1,0:T(8,128)(2,1)S(1)}, bf16[256,1024]{1,0:T(8,128)(2,1)S(1)}, u32[]{:S(2)}, u32[]{:S(2)}) collective-permute-start(bf16[256,1024]{1,0:T(8,128)(2,1)S(1)} %constant_dynamic-update-slice_fusion.refs_0_), channel_id=1, source_target_pairs={{0,1},{1,0},{2,3},{3,2},{4,5},{5,4},{6,7},{7,6},{8,9},{9,8},{10,11... | collective-permute-start | bytes 1572872 | tf_op jit(solution)/shard_map/ppermute | solution.py:284
  29.3 2.5 %collective-permute-start.12 = (bf16[256,1024]{1,0:T(8,128)(2,1)S(1)}, bf16[256,1024]{1,0:T(8,128)(2,1)S(1)}, u32[]{:S(2)}, u32[]{:S(2)}) collective-permute-start(bf16[256,1024]{1,0:T(8,128)(2,1)S(1)} %constant_dynamic-update-slice_fusion.9.refs_2_), channel_id=1, source_target_pairs={{0,1},{1,0},{2,3},{3,2},{4,5},{5,4},{6,7},{7,6},{8,9},{9,8},{10,11... | collective-permute-start | bytes 1572872 | tf_op jit(solution)/shard_map/ppermute | solution.py:284
  29.4 2.6 %collective-permute-start.13 = (bf16[256,1024]{1,0:T(8,128)(2,1)S(1)}, bf16[256,1024]{1,0:T(8,128)(2,1)S(1)}, u32[]{:S(2)}, u32[]{:S(2)}) collective-permute-start(bf16[256,1024]{1,0:T(8,128)(2,1)S(1)} %collective-permute-done.6.refs_3_), channel_id=1, source_target_pairs={{0,1},{1,0},{2,3},{3,2},{4,5},{5,4},{6,7},{7,6},{8,9},{9,8},{10,11... | collective-permute-start | bytes 1572872 | tf_op jit(solution)/shard_map/ppermute | solution.py:284
  30.0 3.0 %collective-permute-start.11 = (bf16[256,1024]{1,0:T(8,128)(2,1)S(1)}, bf16[256,1024]{1,0:T(8,128)(2,1)S(1)}, u32[]{:S(2)}, u32[]{:S(2)}) collective-permute-start(bf16[256,1024]{1,0:T(8,128)(2,1)S(1)} %constant_dynamic-update-slice_fusion.6.refs_1_), channel_id=1, source_target_pairs={{0,1},{1,0},{2,3},{3,2},{4,5},{5,4},{6,7},{7,6},{8,9},{9,8},{10,11... | collective-permute-start | bytes 1572872 | tf_op jit(solution)/shard_map/ppermute | solution.py:284
  46.9 4.4 %copy-start = (bf16[64,1024]{1,0:T(8,128)(2,1)S(1)}, bf16[64,1024]{1,0:T(8,128)(2,1)}, u32[]{:S(2)}) copy-start(bf16[64,1024]{1,0:T(8,128)(2,1)} %param.5) | copy-start | bytes 393220
  48.5 9.2 %collective-permute-start.14 = (bf16[64,2176]{1,0:T(8,128)(2,1)S(1)}, bf16[64,2176]{1,0:T(8,128)(2,1)S(1)}, u32[]{:S(2)}, u32[]{:S(2)}) collective-permute-start(bf16[64,2176]{1,0:T(8,128)(2,1)S(1)} %get-tuple-element.52), channel_id=1, source_target_pairs={{0,2},{2,64},{64,66},{66,128},{128,130},{130,192},{192,194},{194,0... | collective-permute-start | bytes 835592 | tf_op jit(solution)/shard_map/ppermute | solution.py:318
  51.3 8.6 %collective-permute-start.15 = (bf16[64,2176]{1,0:T(8,128)(2,1)S(1)}, bf16[64,2176]{1,0:T(8,128)(2,1)S(1)}, u32[]{:S(2)}, u32[]{:S(2)}) collective-permute-start(bf16[64,2176]{1,0:T(8,128)(2,1)S(1)} %get-tuple-element.54), channel_id=1, source_target_pairs={{0,194},{2,0},{64,2},{66,64},{128,66},{130,128},{192,130},{194,192... | collective-permute-start | bytes 835592 | tf_op jit(solution)/shard_map/ppermute | solution.py:319
  60.2 9.3 %collective-permute-start.16 = (bf16[32,2176]{1,0:T(8,128)(2,1)S(1)}, bf16[32,2176]{1,0:T(8,128)(2,1)S(1)}, u32[]{:S(2)}, u32[]{:S(2)}) collective-permute-start(bf16[32,2176]{1,0:T(8,128)(2,1)S(1)} %get-tuple-element.56), channel_id=1, source_target_pairs={{0,128},{64,192},{128,0},{192,64},{1,129},{65,193},{129,1},{193,65... | collective-permute-start | bytes 417800 | tf_op jit(solution)/shard_map/ppermute | solution.py:330
  64.9 14.4 %collective-permute-start.17 = (bf16[32,2176]{1,0:T(8,128)(2,1)S(1)}, bf16[32,2176]{1,0:T(8,128)(2,1)S(1)}, u32[]{:S(2)}, u32[]{:S(2)}) collective-permute-start(bf16[32,2176]{1,0:T(8,128)(2,1)S(1)} %get-tuple-element.57), channel_id=1, source_target_pairs={{0,64},{64,128},{128,192},{192,0},{1,65},{65,129},{129,193},{193,1... | collective-permute-start | bytes 417800 | tf_op jit(solution)/shard_map/ppermute | solution.py:330
  66.9 12.4 %collective-permute-start.18 = (bf16[32,2176]{1,0:T(8,128)(2,1)S(1)}, bf16[32,2176]{1,0:T(8,128)(2,1)S(1)}, u32[]{:S(2)}, u32[]{:S(2)}) collective-permute-start(bf16[32,2176]{1,0:T(8,128)(2,1)S(1)} %get-tuple-element.58), channel_id=1, source_target_pairs={{0,192},{64,0},{128,64},{192,128},{1,193},{65,1},{129,65},{193,129... | collective-permute-start | bytes 417800 | tf_op jit(solution)/shard_map/ppermute | solution.py:330

commit v7 on v6

--- a/solution.py
+++ b/solution.py
@@ -13,7 +13,7 @@
 EXT = 128
 VMEM = pl.BlockSpec(memory_space=pltpu.VMEM)
 NT = (((1,), (1,)), ((), ()))
-SHIFTS = (0, 2, 1, 3)
+SHIFTS = (0, 1, 3, 2)
 SLOTS = (
     tuple((s, 0) for s in SHIFTS),
     ((0, 1), (0, 3), (2, 1), (2, 3)),
@@ -223,7 +223,7 @@
     me = lax.axis_index("zh")
     refs = (own_ref, g1_ref, g2_ref, g3_ref)
     for shift, ref in enumerate(refs):
-        ext_ref[lax.rem(me + 4 - shift, 4)] = ref[:8, feats:].astype(F32)
+        ext_ref[lax.rem(me + 4 - shift, 4)] = ref[:16, feats:].astype(F32)
     counts = sum(ext_ref[i, 0:1, :] + ext_ref[i, 1:2, :] for i in range(4))
     kept = sum(ext_ref[i, 2:3, :] + ext_ref[i, 3:4, :] for i in range(4))
     log_ref[...] = jnp.log((counts + 1.0) / (kept + float(n_comps)))
@@ -277,7 +277,7 @@
     line = jnp.concatenate(line, axis=0)
     coef = jnp.concatenate([coef, lax.ppermute(coef, "zl", ring(2, 1))], axis=0)
     far = lax.ppermute(line, "y", ring(4, 2))
-    rest = [lax.ppermute(pair, "x", ring(4, s)) for s in SHIFTS[1:]]
+    rest = [lax.ppermute(pair, "x", ring(4, s)) for s in (2, 1, 3)]
     coef, far, rest = lax.optimization_barrier((coef, far, rest))
 
     groups = [line, jnp.concatenate([pair, rest[0]]), jnp.concatenate(rest[1:]), far]
@@ -332,7 +332,7 @@
         functools.partial(finish_kernel, n_comps),
         (sds((quarter, 2 * width), BF16), sds((1, comps), F32)),
         4,
-        scratch_shapes=[pltpu.VMEM((4, 8, EXT), F32)],
+        scratch_shapes=[pltpu.VMEM((4, 16, EXT), F32)],
     )(own_q, *g)
     out = sds((comps, width), F32)
     new_means, new_vars = call(place_kernel, (out, out), 1)(lax.all_gather(result, "zh"))

time: 98.3 us -> 98 us (level)
    ppermute x1, waiting for transfers between devices: 7.1 us -> 5.66 us  [local(): coef = jnp.concatenate([coef, lax.ppermute(coef, 'zl', ring(2, 1))], axis=0)]
    ppermute x3, starting transfers between devices: 3.59 us -> 5.04 us  [local(): rest = [lax.ppermute(pair, 'x', ring(4, s)) for s in (2, 1, 3)]]
    ppermute x3, starting transfers between devices: 6.35 us -> 5.13 us  [local(): lax.ppermute(embeddings, 'x', ring(4, s))]
  transfers between devices with their start and end apart: 19 -> 19, of which waited for: 6 -> 7; matrix products, arithmetic and copies ran while one was open for 4% -> 4% of each run, Pallas kernels for 4% -> 4%
where the time goes in v7:
time: 98 us; the launch traced here: 96.9 us
  starting transfers between devices  28.9 us (29%)
  blocking collectives  28.7 us (29%)
  waiting for transfers between devices  26 us (27%)
  Pallas kernels  8.55 us (9%)
  other arithmetic  2.85 us (3%)
  local copies, waits for them, and re-layouts  1.07 us (1%)
    all_gather x1, blocking collectives, local(): lax.all_gather(result, 'zh')  16.3 us
    all_to_all x1, blocking collectives, local(): lax.all_to_all(jnp.broadcast_to(pay[None], (32,) + pay.shape), plane + (c...  12.5 us
    ppermute x3, waiting for transfers between devices, local(): lax.ppermute(s, 'zh', ring(4, i))  9.76 us
    ppermute x3, starting transfers between devices, local(): lax.ppermute(s, 'zh', ring(4, i))  8.72 us
    ppermute x1, waiting for transfers between devices, local(): coef = jnp.concatenate([coef, lax.ppermute(coef, 'zl', ring(2, 1))], axis=0)  5.66 us
    ppermute x3, starting transfers between devices, local(): lax.ppermute(embeddings, 'x', ring(4, s))  5.13 us
    ppermute x3, starting transfers between devices, local(): rest = [lax.ppermute(pair, 'x', ring(4, s)) for s in (2, 1, 3)]  5.04 us
    ppermute x1, waiting for transfers between devices, local(): low = lax.ppermute(up, z, ring(8, 1))  4.69 us
  transfers between devices with their start and end apart: 19, of which 7 were waited for; matrix products, arithmetic and copies ran while one was open for 4% of the time, Pallas kernels for 4%

profile of v7, /device:TPU:32, one launch (start us, length us, event | category | flops | bytes accessed | tf_op | source)
XLA Modules:
  0.0 96.9 jit_solution(6030707673282555803)
XLA Ops:
  0.6 1.6 %collective-permute-start = (bf16[64,1024]{1,0:T(8,128)(2,1)}, bf16[64,1024]{1,0:T(8,128)(2,1)S(1)}, u32[]{:S(2)}, u32[]{:S(2)}) collective-permute-start(bf16[64,1024]{1,0:T(8,128)(2,1)} %param.5), channel_id=1, source_target_pairs={{0,16},{16,32},{32,48},{48,0},{1,17},{17,33},{33,49},{49,1},{2,18}... | collective-permute-start | bytes 393224 | tf_op jit(solution)/shard_map/ppermute | solution.py:264
  2.2 1.7 %collective-permute-start.1 = (bf16[64,1024]{1,0:T(8,128)(2,1)}, bf16[64,1024]{1,0:T(8,128)(2,1)S(1)}, u32[]{:S(2)}, u32[]{:S(2)}) collective-permute-start(bf16[64,1024]{1,0:T(8,128)(2,1)} %param.5), channel_id=1, source_target_pairs={{0,48},{16,0},{32,16},{48,32},{1,49},{17,1},{33,17},{49,33},{2,50}... | collective-permute-start | bytes 393224 | tf_op jit(solution)/shard_map/ppermute | solution.py:264
  3.9 1.8 %collective-permute-start.2 = (bf16[64,1024]{1,0:T(8,128)(2,1)}, bf16[64,1024]{1,0:T(8,128)(2,1)S(1)}, u32[]{:S(2)}, u32[]{:S(2)}) collective-permute-start(bf16[64,1024]{1,0:T(8,128)(2,1)} %param.5), channel_id=1, source_target_pairs={{0,32},{16,48},{32,0},{48,16},{1,33},{17,49},{33,1},{49,17},{2,34}... | collective-permute-start | bytes 393224 | tf_op jit(solution)/shard_map/ppermute | solution.py:264
  5.8 1.6 %collective-permute-start.3 = (bf16[64,1024]{1,0:T(8,128)(2,1)}, bf16[64,1024]{1,0:T(8,128)(2,1)S(1)}, u32[]{:S(2)}, u32[]{:S(2)}) collective-permute-start(bf16[64,1024]{1,0:T(8,128)(2,1)} %param.5), channel_id=1, source_target_pairs={{0,4},{4,8},{8,12},{12,0},{1,5},{5,9},{9,13},{13,1},{2,6},{6,10},{... | collective-permute-start | bytes 393224 | tf_op jit(solution)/shard_map/ppermute | solution.py:263
  7.3 1.7 %collective-permute-start.4 = (bf16[64,1024]{1,0:T(8,128)(2,1)}, bf16[64,1024]{1,0:T(8,128)(2,1)S(1)}, u32[]{:S(2)}, u32[]{:S(2)}) collective-permute-start(bf16[64,1024]{1,0:T(8,128)(2,1)} %param.5), channel_id=1, source_target_pairs={{0,12},{4,0},{8,4},{12,8},{1,13},{5,1},{9,5},{13,9},{2,14},{6,2},{... | collective-permute-start | bytes 393224 | tf_op jit(solution)/shard_map/ppermute | solution.py:263
  9.0 1.5 %add_reduce_fusion = (f32[128]{0:T(128)S(1)}, bf16[128,1024]{1,0:T(8,128)(2,1)S(1)}, bf16[128,1024]{1,0:T(8,128)(2,1)S(1)}) fusion(f32[128,1024]{1,0:T(8,128)} %param.8, f32[128,1024]{1,0:T(8,128)} %param.7), kind=kLoop, calls=%fused_computation.1 | loop fusion | flops 1179520 | bytes 1573376 | tf_op jit(solution)/shard_map/reduce_sum | solution.py:270
  10.5 0.7 add_bitcast_fusion.offset_ref
  11.1 0.9 constant_dynamic-update-slice_fusion.3
  12.4 2.1 %collective-permute-start.6 = (bf16[256,1024]{1,0:T(8,128)(2,1)S(1)}, bf16[256,1024]{1,0:T(8,128)(2,1)S(1)}, u32[]{:S(2)}, u32[]{:S(2)}) collective-permute-start(bf16[256,1024]{1,0:T(8,128)(2,1)S(1)} %constant_dynamic-update-slice_fusion.refs_0_), channel_id=1, source_target_pairs={{0,8},{4,12},{8,0},{12,4},{1,9},{5,13},{9,1},{13,5},{2,10},{6,14},... | collective-permute-start | bytes 1572872 | tf_op jit(solution)/shard_map/ppermute | solution.py:279
  14.6 1.8 %collective-permute-start.7 = (bf16[128,1024]{1,0:T(8,128)(2,1)S(1)}, bf16[128,1024]{1,0:T(8,128)(2,1)S(1)}, u32[]{:S(2)}, u32[]{:S(2)}) collective-permute-start(bf16[128,1024]{1,0:T(8,128)(2,1)S(1)} %get-tuple-element.67), channel_id=1, source_target_pairs={{0,32},{16,48},{32,0},{48,16},{1,33},{17,49},{33,1},{49,17},{2,34}... | collective-permute-start | bytes 786440 | tf_op jit(solution)/shard_map/ppermute | solution.py:280
  16.4 1.1 %collective-permute-start.8 = (bf16[128,1024]{1,0:T(8,128)(2,1)S(1)}, bf16[128,1024]{1,0:T(8,128)(2,1)S(1)}, u32[]{:S(2)}, u32[]{:S(2)}) collective-permute-start(bf16[128,1024]{1,0:T(8,128)(2,1)S(1)} %get-tuple-element.67), channel_id=1, source_target_pairs={{0,16},{16,32},{32,48},{48,0},{1,17},{17,33},{33,49},{49,1},{2,18}... | collective-permute-start | bytes 786440 | tf_op jit(solution)/shard_map/ppermute | solution.py:280
  17.5 2.1 %collective-permute-start.9 = (bf16[128,1024]{1,0:T(8,128)(2,1)S(1)}, bf16[128,1024]{1,0:T(8,128)(2,1)S(1)}, u32[]{:S(2)}, u32[]{:S(2)}) collective-permute-start(bf16[128,1024]{1,0:T(8,128)(2,1)S(1)} %get-tuple-element.67), channel_id=1, source_target_pairs={{0,48},{16,0},{32,16},{48,32},{1,49},{17,1},{33,17},{49,33},{2,50}... | collective-permute-start | bytes 786440 | tf_op jit(solution)/shard_map/ppermute | solution.py:280
  19.6 5.7 %collective-permute-done.5 = bf16[128,2176]{1,0:T(8,128)(2,1)S(1)} collective-permute-done((bf16[128,2176]{1,0:T(8,128)(2,1)S(1)}, bf16[128,2176]{1,0:T(8,128)(2,1)S(1)}, u32[]{:S(2)}, u32[]{:S(2)}) %collective-permute-start.5) | collective-permute-done | bytes 557088 | tf_op jit(solution)/shard_map/ppermute | solution.py:278
  25.4 3.4 %collective-permute-done.8 = bf16[128,1024]{1,0:T(8,128)(2,1)S(1)} collective-permute-done((bf16[128,1024]{1,0:T(8,128)(2,1)S(1)}, bf16[128,1024]{1,0:T(8,128)(2,1)S(1)}, u32[]{:S(2)}, u32[]{:S(2)}) %collective-permute-start.8) | collective-permute-done | bytes 262176 | tf_op jit(solution)/shard_map/ppermute | solution.py:280
  29.0 0.5 collective-permute-start.13
  29.9 1.5 %shard_map.85 = (f32[256,1024]{1,0:T(8,128)S(1)}, f32[1,1024]{1,0:T(1,128)S(1)}, bf16[1024,2048]{1,0:T(8,128)(2,1)S(1)}) custom-call(bf16[256,1024]{1,0:T(8,128)(2,1)S(1)} %constant_dynamic-update-slice_fusion.refs_0_, bf16[256,1024]{1,0:T(8,128)(2,1)S(1)} %constant_dynamic-update-slice_fusion.6.refs_1_, ...), custom_call_target="tpu_custom_call" | custom-call | flops 1073741824 | tf_op jit(solution)/shard_map/pallas_call | solution.py:289
  31.6 0.9 shard_map.87
  32.6 0.9 shard_map.86
  33.6 12.5 %all_to_all.5.refs_0_ = f32[32,16,128]{2,1,0:T(8,128)S(1)} all-to-all(f32[32,16,128]{2,1,0:T(8,128)S(1)} %broadcast_in_dim.10), channel_id=1, replica_groups=mesh['zh'=4,'x'=4,'y'=4,'zl'=2,'c'=2] {'x','y','c'}, dimensions={0} | all-to-all | bytes 524288 | tf_op jit(solution)/shard_map/all_to_all | solution.py:305
  46.1 1.6 %shard_map.89 = (bf16[64,2176]{1,0:T(8,128)(2,1)S(1)}, bf16[64,2176]{1,0:T(8,128)(2,1)S(1)}, f32[1,128]{1,0:T(1,128)S(1)}) custom-call(f32[32,16,128]{2,1,0:T(8,128)S(1)} %all_to_all.5.refs_0_, f32[256,1024]{1,0:T(8,128)S(1)} %get-tuple-element.45.refs_1_, f32[256,512]{1,0:T(8,128)S(1)} %get-tuple-element.46.refs_2_, ...), custom_call_target="tpu_custom_call" | custom-call | flops 1073741824 | tf_op jit(solution)/shard_map/pallas_call | solution.py:308
  47.6 3.5 %collective-permute-start.14 = (bf16[64,2176]{1,0:T(8,128)(2,1)S(1)}, bf16[64,2176]{1,0:T(8,128)(2,1)S(1)}, u32[]{:S(2)}, u32[]{:S(2)}) collective-permute-start(bf16[64,2176]{1,0:T(8,128)(2,1)S(1)} %get-tuple-element.52), channel_id=1, source_target_pairs={{0,2},{2,64},{64,66},{66,128},{128,130},{130,192},{192,194},{194,0... | collective-permute-start | bytes 835592 | tf_op jit(solution)/shard_map/ppermute | solution.py:318
  51.3 1.6 %shard_map.90.mine_ref = f32[128,2176]{1,0:T(8,128)S(1)} custom-call(f32[32,16,128]{2,1,0:T(8,128)S(1)} %all_to_all.5.refs_0_, f32[256,1024]{1,0:T(8,128)S(1)} %get-tuple-element.45.refs_1_, f32[256,512]{1,0:T(8,128)S(1)} %get-tuple-element.46.refs_2_, f32[256,512]{1,0:T(8,128)S(1)} %get-tuple-element.47.refs_3_, ...), custom_call_target="tpu_custom_call" | custom-call | flops 1073741824 | tf_op jit(solution)/shard_map/pallas_call | solution.py:308
  52.9 4.7 %collective-permute-done.14.low_ref = bf16[64,2176]{1,0:T(8,128)(2,1)S(1)} collective-permute-done((bf16[64,2176]{1,0:T(8,128)(2,1)S(1)}, bf16[64,2176]{1,0:T(8,128)(2,1)S(1)}, u32[]{:S(2)}, u32[]{:S(2)}) %collective-permute-start.14) | collective-permute-done | bytes 278560 | tf_op jit(solution)/shard_map/ppermute | solution.py:318
  57.6 2.2 %collective-permute-done.15.high_ref = bf16[64,2176]{1,0:T(8,128)(2,1)S(1)} collective-permute-done((bf16[64,2176]{1,0:T(8,128)(2,1)S(1)}, bf16[64,2176]{1,0:T(8,128)(2,1)S(1)}, u32[]{:S(2)}, u32[]{:S(2)}) %collective-permute-start.15) | collective-permute-done | bytes 278560 | tf_op jit(solution)/shard_map/ppermute | solution.py:319
  60.1 4.6 %collective-permute-start.16 = (bf16[32,2176]{1,0:T(8,128)(2,1)S(1)}, bf16[32,2176]{1,0:T(8,128)(2,1)S(1)}, u32[]{:S(2)}, u32[]{:S(2)}) collective-permute-start(bf16[32,2176]{1,0:T(8,128)(2,1)S(1)} %get-tuple-element.56), channel_id=1, source_target_pairs={{0,128},{64,192},{128,0},{192,64},{1,129},{65,193},{129,1},{193,65... | collective-permute-start | bytes 417800 | tf_op jit(solution)/shard_map/ppermute | solution.py:330
  64.7 2.0 %collective-permute-start.17 = (bf16[32,2176]{1,0:T(8,128)(2,1)S(1)}, bf16[32,2176]{1,0:T(8,128)(2,1)S(1)}, u32[]{:S(2)}, u32[]{:S(2)}) collective-permute-start(bf16[32,2176]{1,0:T(8,128)(2,1)S(1)} %get-tuple-element.57), channel_id=1, source_target_pairs={{0,64},{64,128},{128,192},{192,0},{1,65},{65,129},{129,193},{193,1... | collective-permute-start | bytes 417800 | tf_op jit(solution)/shard_map/ppermute | solution.py:330
  66.7 2.1 %collective-permute-start.18 = (bf16[32,2176]{1,0:T(8,128)(2,1)S(1)}, bf16[32,2176]{1,0:T(8,128)(2,1)S(1)}, u32[]{:S(2)}, u32[]{:S(2)}) collective-permute-start(bf16[32,2176]{1,0:T(8,128)(2,1)S(1)} %get-tuple-element.58), channel_id=1, source_target_pairs={{0,192},{64,0},{128,64},{192,128},{1,193},{65,1},{129,65},{193,129... | collective-permute-start | bytes 417800 | tf_op jit(solution)/shard_map/ppermute | solution.py:330
  68.8 0.5 bitcast_add_fusion
  69.3 9.8 %collective-permute-done.17.g1_ref = bf16[32,2176]{1,0:T(8,128)(2,1)S(1)} collective-permute-done((bf16[32,2176]{1,0:T(8,128)(2,1)S(1)}, bf16[32,2176]{1,0:T(8,128)(2,1)S(1)}, u32[]{:S(2)}, u32[]{:S(2)}) %collective-permute-start.17) | collective-permute-done | bytes 139296 | tf_op jit(solution)/shard_map/ppermute | solution.py:330
  79.1 0.5 shard_map.92
  79.6 16.3 %all-gather = bf16[128,2048]{1,0:T(8,128)(2,1)S(1)} all-gather(bf16[32,2048]{1,0:T(8,128)(2,1)S(1)} %get-tuple-element.59), channel_id=2, replica_groups=mesh['zh'=4,'x'=4,'y'=4,'zl'=2,'c'=2] {'zh'}, dimensions={0}, use_global_device_ids=true | all-gather | bytes 655360 | tf_op jit(solution)/shard_map/all_gather | solution.py:338
  95.9 1.0 %shard_map.93 = (f32[128,1024]{1,0:T(8,128)}, f32[128,1024]{1,0:T(8,128)}) custom-call(bf16[4,32,2048]{2,1,0:T(8,128)(2,1)S(1)} %bitcast.8), custom_call_target="tpu_custom_call" | custom-call | tf_op jit(solution)/shard_map/pallas_call | solution.py:338
  (39 shorter events, 1.8 us)
Async XLA Ops:
  0.6 11.5 %collective-permute-start = (bf16[64,1024]{1,0:T(8,128)(2,1)}, bf16[64,1024]{1,0:T(8,128)(2,1)S(1)}, u32[]{:S(2)}, u32[]{:S(2)}) collective-permute-start(bf16[64,1024]{1,0:T(8,128)(2,1)} %param.5), channel_id=1, source_target_pairs={{0,16},{16,32},{32,48},{48,0},{1,17},{17,33},{33,49},{49,1},{2,18}... | collective-permute-start | bytes 393224 | tf_op jit(solution)/shard_map/ppermute | solution.py:264
  2.2 10.2 %collective-permute-start.1 = (bf16[64,1024]{1,0:T(8,128)(2,1)}, bf16[64,1024]{1,0:T(8,128)(2,1)S(1)}, u32[]{:S(2)}, u32[]{:S(2)}) collective-permute-start(bf16[64,1024]{1,0:T(8,128)(2,1)} %param.5), channel_id=1, source_target_pairs={{0,48},{16,0},{32,16},{48,32},{1,49},{17,1},{33,17},{49,33},{2,50}... | collective-permute-start | bytes 393224 | tf_op jit(solution)/shard_map/ppermute | solution.py:264
  3.9 8.5 %collective-permute-start.2 = (bf16[64,1024]{1,0:T(8,128)(2,1)}, bf16[64,1024]{1,0:T(8,128)(2,1)S(1)}, u32[]{:S(2)}, u32[]{:S(2)}) collective-permute-start(bf16[64,1024]{1,0:T(8,128)(2,1)} %param.5), channel_id=1, source_target_pairs={{0,32},{16,48},{32,0},{48,16},{1,33},{17,49},{33,1},{49,17},{2,34}... | collective-permute-start | bytes 393224 | tf_op jit(solution)/shard_map/ppermute | solution.py:264
  5.8 8.7 %collective-permute-start.3 = (bf16[64,1024]{1,0:T(8,128)(2,1)}, bf16[64,1024]{1,0:T(8,128)(2,1)S(1)}, u32[]{:S(2)}, u32[]{:S(2)}) collective-permute-start(bf16[64,1024]{1,0:T(8,128)(2,1)} %param.5), channel_id=1, source_target_pairs={{0,4},{4,8},{8,12},{12,0},{1,5},{5,9},{9,13},{13,1},{2,6},{6,10},{... | collective-permute-start | bytes 393224 | tf_op jit(solution)/shard_map/ppermute | solution.py:263
  7.3 7.2 %collective-permute-start.4 = (bf16[64,1024]{1,0:T(8,128)(2,1)}, bf16[64,1024]{1,0:T(8,128)(2,1)S(1)}, u32[]{:S(2)}, u32[]{:S(2)}) collective-permute-start(bf16[64,1024]{1,0:T(8,128)(2,1)} %param.5), channel_id=1, source_target_pairs={{0,12},{4,0},{8,4},{12,8},{1,13},{5,1},{9,5},{13,9},{2,14},{6,2},{... | collective-permute-start | bytes 393224 | tf_op jit(solution)/shard_map/ppermute | solution.py:263
  12.2 13.1 %collective-permute-start.5 = (bf16[128,2176]{1,0:T(8,128)(2,1)S(1)}, bf16[128,2176]{1,0:T(8,128)(2,1)S(1)}, u32[]{:S(2)}, u32[]{:S(2)}) collective-permute-start(bf16[128,2176]{1,0:T(8,128)(2,1)S(1)} %shard_map.84), channel_id=1, source_target_pairs={{0,2},{2,0},{1,3},{3,1},{4,6},{6,4},{5,7},{7,5},{8,10},{10,8},{9,1... | collective-permute-start | bytes 1671176 | tf_op jit(solution)/shard_map/ppermute | solution.py:278
  12.4 16.4 %collective-permute-start.6 = (bf16[256,1024]{1,0:T(8,128)(2,1)S(1)}, bf16[256,1024]{1,0:T(8,128)(2,1)S(1)}, u32[]{:S(2)}, u32[]{:S(2)}) collective-permute-start(bf16[256,1024]{1,0:T(8,128)(2,1)S(1)} %constant_dynamic-update-slice_fusion.refs_0_), channel_id=1, source_target_pairs={{0,8},{4,12},{8,0},{12,4},{1,9},{5,13},{9,1},{13,5},{2,10},{6,14},... | collective-permute-start | bytes 1572872 | tf_op jit(solution)/shard_map/ppermute | solution.py:279
  14.5 15.4 %copy-start.1 = (s32[64]{0:T(128)S(1)}, s32[64]{0:T(128)}, u32[]{:S(2)}) copy-start(s32[64]{0:T(128)} %param.6) | copy-start | bytes 772
  14.6 10.9 %collective-permute-start.7 = (bf16[128,1024]{1,0:T(8,128)(2,1)S(1)}, bf16[128,1024]{1,0:T(8,128)(2,1)S(1)}, u32[]{:S(2)}, u32[]{:S(2)}) collective-permute-start(bf16[128,1024]{1,0:T(8,128)(2,1)S(1)} %get-tuple-element.67), channel_id=1, source_target_pairs={{0,32},{16,48},{32,0},{48,16},{1,33},{17,49},{33,1},{49,17},{2,34}... | collective-permute-start | bytes 786440 | tf_op jit(solution)/shard_map/ppermute | solution.py:280
  16.4 12.5 %collective-permute-start.8 = (bf16[128,1024]{1,0:T(8,128)(2,1)S(1)}, bf16[128,1024]{1,0:T(8,128)(2,1)S(1)}, u32[]{:S(2)}, u32[]{:S(2)}) collective-permute-start(bf16[128,1024]{1,0:T(8,128)(2,1)S(1)} %get-tuple-element.67), channel_id=1, source_target_pairs={{0,16},{16,32},{32,48},{48,0},{1,17},{17,33},{33,49},{49,1},{2,18}... | collective-permute-start | bytes 786440 | tf_op jit(solution)/shard_map/ppermute | solution.py:280
  17.5 11.4 %collective-permute-start.9 = (bf16[128,1024]{1,0:T(8,128)(2,1)S(1)}, bf16[128,1024]{1,0:T(8,128)(2,1)S(1)}, u32[]{:S(2)}, u32[]{:S(2)}) collective-permute-start(bf16[128,1024]{1,0:T(8,128)(2,1)S(1)} %get-tuple-element.67), channel_id=1, source_target_pairs={{0,48},{16,0},{32,16},{48,32},{1,49},{17,1},{33,17},{49,33},{2,50}... | collective-permute-start | bytes 786440 | tf_op jit(solution)/shard_map/ppermute | solution.py:280
  25.3 7.3 %collective-permute-start.10 = (bf16[256,1024]{1,0:T(8,128)(2,1)S(1)}, bf16[256,1024]{1,0:T(8,128)(2,1)S(1)}, u32[]{:S(2)}, u32[]{:S(2)}) collective-permute-start(bf16[256,1024]{1,0:T(8,128)(2,1)S(1)} %constant_dynamic-update-slice_fusion.refs_0_), channel_id=1, source_target_pairs={{0,1},{1,0},{2,3},{3,2},{4,5},{5,4},{6,7},{7,6},{8,9},{9,8},{10,11... | collective-permute-start | bytes 1572872 | tf_op jit(solution)/shard_map/ppermute | solution.py:284
  28.9 2.5 %collective-permute-start.12 = (bf16[256,1024]{1,0:T(8,128)(2,1)S(1)}, bf16[256,1024]{1,0:T(8,128)(2,1)S(1)}, u32[]{:S(2)}, u32[]{:S(2)}) collective-permute-start(bf16[256,1024]{1,0:T(8,128)(2,1)S(1)} %constant_dynamic-update-slice_fusion.9.refs_2_), channel_id=1, source_target_pairs={{0,1},{1,0},{2,3},{3,2},{4,5},{5,4},{6,7},{7,6},{8,9},{9,8},{10,11... | collective-permute-start | bytes 1572872 | tf_op jit(solution)/shard_map/ppermute | solution.py:284
  29.0 2.6 %collective-permute-start.13 = (bf16[256,1024]{1,0:T(8,128)(2,1)S(1)}, bf16[256,1024]{1,0:T(8,128)(2,1)S(1)}, u32[]{:S(2)}, u32[]{:S(2)}) collective-permute-start(bf16[256,1024]{1,0:T(8,128)(2,1)S(1)} %collective-permute-done.6.refs_3_), channel_id=1, source_target_pairs={{0,1},{1,0},{2,3},{3,2},{4,5},{5,4},{6,7},{7,6},{8,9},{9,8},{10,11... | collective-permute-start | bytes 1572872 | tf_op jit(solution)/shard_map/ppermute | solution.py:284
  29.5 3.0 %collective-permute-start.11 = (bf16[256,1024]{1,0:T(8,128)(2,1)S(1)}, bf16[256,1024]{1,0:T(8,128)(2,1)S(1)}, u32[]{:S(2)}, u32[]{:S(2)}) collective-permute-start(bf16[256,1024]{1,0:T(8,128)(2,1)S(1)} %constant_dynamic-update-slice_fusion.6.refs_1_), channel_id=1, source_target_pairs={{0,1},{1,0},{2,3},{3,2},{4,5},{5,4},{6,7},{7,6},{8,9},{9,8},{10,11... | collective-permute-start | bytes 1572872 | tf_op jit(solution)/shard_map/ppermute | solution.py:284
  46.1 5.1 %copy-start = (bf16[64,1024]{1,0:T(8,128)(2,1)S(1)}, bf16[64,1024]{1,0:T(8,128)(2,1)}, u32[]{:S(2)}) copy-start(bf16[64,1024]{1,0:T(8,128)(2,1)} %param.5) | copy-start | bytes 393220
  47.6 9.9 %collective-permute-start.14 = (bf16[64,2176]{1,0:T(8,128)(2,1)S(1)}, bf16[64,2176]{1,0:T(8,128)(2,1)S(1)}, u32[]{:S(2)}, u32[]{:S(2)}) collective-permute-start(bf16[64,2176]{1,0:T(8,128)(2,1)S(1)} %get-tuple-element.52), channel_id=1, source_target_pairs={{0,2},{2,64},{64,66},{66,128},{128,130},{130,192},{192,194},{194,0... | collective-permute-start | bytes 835592 | tf_op jit(solution)/shard_map/ppermute | solution.py:318
  51.2 8.6 %collective-permute-start.15 = (bf16[64,2176]{1,0:T(8,128)(2,1)S(1)}, bf16[64,2176]{1,0:T(8,128)(2,1)S(1)}, u32[]{:S(2)}, u32[]{:S(2)}) collective-permute-start(bf16[64,2176]{1,0:T(8,128)(2,1)S(1)} %get-tuple-element.54), channel_id=1, source_target_pairs={{0,194},{2,0},{64,2},{66,64},{128,66},{130,128},{192,130},{194,192... | collective-permute-start | bytes 835592 | tf_op jit(solution)/shard_map/ppermute | solution.py:319
  60.1 9.2 %collective-permute-start.16 = (bf16[32,2176]{1,0:T(8,128)(2,1)S(1)}, bf16[32,2176]{1,0:T(8,128)(2,1)S(1)}, u32[]{:S(2)}, u32[]{:S(2)}) collective-permute-start(bf16[32,2176]{1,0:T(8,128)(2,1)S(1)} %get-tuple-element.56), channel_id=1, source_target_pairs={{0,128},{64,192},{128,0},{192,64},{1,129},{65,193},{129,1},{193,65... | collective-permute-start | bytes 417800 | tf_op jit(solution)/shard_map/ppermute | solution.py:330
  64.7 14.4 %collective-permute-start.17 = (bf16[32,2176]{1,0:T(8,128)(2,1)S(1)}, bf16[32,2176]{1,0:T(8,128)(2,1)S(1)}, u32[]{:S(2)}, u32[]{:S(2)}) collective-permute-start(bf16[32,2176]{1,0:T(8,128)(2,1)S(1)} %get-tuple-element.57), channel_id=1, source_target_pairs={{0,64},{64,128},{128,192},{192,0},{1,65},{65,129},{129,193},{193,1... | collective-permute-start | bytes 417800 | tf_op jit(solution)/shard_map/ppermute | solution.py:330
  66.7 12.4 %collective-permute-start.18 = (bf16[32,2176]{1,0:T(8,128)(2,1)S(1)}, bf16[32,2176]{1,0:T(8,128)(2,1)S(1)}, u32[]{:S(2)}, u32[]{:S(2)}) collective-permute-start(bf16[32,2176]{1,0:T(8,128)(2,1)S(1)} %get-tuple-element.58), channel_id=1, source_target_pairs={{0,192},{64,0},{128,64},{192,128},{1,193},{65,1},{129,65},{193,129... | collective-permute-start | bytes 417800 | tf_op jit(solution)/shard_map/ppermute | solution.py:330

commit v8 on v7

--- a/solution.py
+++ b/solution.py
@@ -240,13 +240,20 @@
     ).astype(BF16)
 
 
-def place_kernel(got_ref, mean_ref, var_ref):
+def place_kernel(got_ref, mean_hbm, var_hbm, mean_ref, var_ref, sems):
     _, quarter, _ = got_ref.shape
     width = mean_ref.shape[1]
+    copies = []
     for j in range(4):
         at = slice(j * quarter, (j + 1) * quarter)
+        there = pl.ds(j * quarter, quarter)
         mean_ref[at, :] = got_ref[j, :, :width].astype(F32)
         var_ref[at, :] = got_ref[j, :, width:].astype(F32)
+        for i, (ref, hbm) in enumerate(((mean_ref, mean_hbm), (var_ref, var_hbm))):
+            copies.append(pltpu.make_async_copy(ref.at[there], hbm.at[there], sems.at[2 * j + i]))
+            copies[-1].start()
+    for copy in copies:
+        copy.wait()
 
 
 def ring(n, shift):
@@ -335,7 +342,13 @@
         scratch_shapes=[pltpu.VMEM((4, 16, EXT), F32)],
     )(own_q, *g)
     out = sds((comps, width), F32)
-    new_means, new_vars = call(place_kernel, (out, out), 1)(lax.all_gather(result, "zh"))
+    new_means, new_vars = call(
+        place_kernel,
+        (out, out),
+        1,
+        out_specs=[pl.BlockSpec(memory_space=pl.ANY)] * 2,
+        scratch_shapes=[pltpu.VMEM((comps, width), F32)] * 2 + [pltpu.SemaphoreType.DMA((8,))],
+    )(lax.all_gather(result, "zh"))
 
     wide = embeddings.astype(F32)
     own_norm = 0.5 * jnp.sum(wide * wide, axis=1) + 0.5 * width * math.log(2.0 * math.pi)

time: 98 us -> 98.2 us (level)
  no operation moved by 1% of the time
where the time goes in v8:
time: 98.2 us; the launch traced here: 97.1 us
  starting transfers between devices  28.9 us (29%)
  blocking collectives  28.7 us (29%)
  waiting for transfers between devices  26 us (26%)
  Pallas kernels  8.55 us (9%)
  other arithmetic  2.85 us (3%)
  local copies, waits for them, and re-layouts  1.07 us (1%)
    all_gather x1, blocking collectives, local(): lax.all_gather(result, 'zh')  16.3 us
    all_to_all x1, blocking collectives, local(): lax.all_to_all(jnp.broadcast_to(pay[None], (32,) + pay.shape), plane + (c...  12.5 us
    ppermute x3, waiting for transfers between devices, local(): lax.ppermute(s, 'zh', ring(4, i))  9.76 us
    ppermute x3, starting transfers between devices, local(): lax.ppermute(s, 'zh', ring(4, i))  8.72 us
    ppermute x1, waiting for transfers between devices, local(): coef = jnp.concatenate([coef, lax.ppermute(coef, 'zl', ring(2, 1))], axis=0)  5.66 us
    ppermute x3, starting transfers between devices, local(): lax.ppermute(embeddings, 'x', ring(4, s))  5.13 us
    ppermute x3, starting transfers between devices, local(): rest = [lax.ppermute(pair, 'x', ring(4, s)) for s in (2, 1, 3)]  5.04 us
    ppermute x1, waiting for transfers between devices, local(): low = lax.ppermute(up, z, ring(8, 1))  4.69 us
  transfers between devices with their start and end apart: 19, of which 7 were waited for; matrix products, arithmetic and copies ran while one was open for 4% of the time, Pallas kernels for 4%

profile of v8, /device:TPU:32, one launch (start us, length us, event | category | flops | bytes accessed | tf_op | source)
XLA Modules:
  0.0 97.1 jit_solution(550528948091922972)
XLA Ops:
  0.6 1.6 %collective-permute-start = (bf16[64,1024]{1,0:T(8,128)(2,1)}, bf16[64,1024]{1,0:T(8,128)(2,1)S(1)}, u32[]{:S(2)}, u32[]{:S(2)}) collective-permute-start(bf16[64,1024]{1,0:T(8,128)(2,1)} %param.5), channel_id=1, source_target_pairs={{0,16},{16,32},{32,48},{48,0},{1,17},{17,33},{33,49},{49,1},{2,18}... | collective-permute-start | bytes 393224 | tf_op jit(solution)/shard_map/ppermute | solution.py:271
  2.2 1.7 %collective-permute-start.1 = (bf16[64,1024]{1,0:T(8,128)(2,1)}, bf16[64,1024]{1,0:T(8,128)(2,1)S(1)}, u32[]{:S(2)}, u32[]{:S(2)}) collective-permute-start(bf16[64,1024]{1,0:T(8,128)(2,1)} %param.5), channel_id=1, source_target_pairs={{0,48},{16,0},{32,16},{48,32},{1,49},{17,1},{33,17},{49,33},{2,50}... | collective-permute-start | bytes 393224 | tf_op jit(solution)/shard_map/ppermute | solution.py:271
  3.9 1.8 %collective-permute-start.2 = (bf16[64,1024]{1,0:T(8,128)(2,1)}, bf16[64,1024]{1,0:T(8,128)(2,1)S(1)}, u32[]{:S(2)}, u32[]{:S(2)}) collective-permute-start(bf16[64,1024]{1,0:T(8,128)(2,1)} %param.5), channel_id=1, source_target_pairs={{0,32},{16,48},{32,0},{48,16},{1,33},{17,49},{33,1},{49,17},{2,34}... | collective-permute-start | bytes 393224 | tf_op jit(solution)/shard_map/ppermute | solution.py:271
  5.8 1.6 %collective-permute-start.3 = (bf16[64,1024]{1,0:T(8,128)(2,1)}, bf16[64,1024]{1,0:T(8,128)(2,1)S(1)}, u32[]{:S(2)}, u32[]{:S(2)}) collective-permute-start(bf16[64,1024]{1,0:T(8,128)(2,1)} %param.5), channel_id=1, source_target_pairs={{0,4},{4,8},{8,12},{12,0},{1,5},{5,9},{9,13},{13,1},{2,6},{6,10},{... | collective-permute-start | bytes 393224 | tf_op jit(solution)/shard_map/ppermute | solution.py:270
  7.3 1.7 %collective-permute-start.4 = (bf16[64,1024]{1,0:T(8,128)(2,1)}, bf16[64,1024]{1,0:T(8,128)(2,1)S(1)}, u32[]{:S(2)}, u32[]{:S(2)}) collective-permute-start(bf16[64,1024]{1,0:T(8,128)(2,1)} %param.5), channel_id=1, source_target_pairs={{0,12},{4,0},{8,4},{12,8},{1,13},{5,1},{9,5},{13,9},{2,14},{6,2},{... | collective-permute-start | bytes 393224 | tf_op jit(solution)/shard_map/ppermute | solution.py:270
  9.0 1.5 %add_reduce_fusion = (f32[128]{0:T(128)S(1)}, bf16[128,1024]{1,0:T(8,128)(2,1)S(1)}, bf16[128,1024]{1,0:T(8,128)(2,1)S(1)}) fusion(f32[128,1024]{1,0:T(8,128)} %param.8, f32[128,1024]{1,0:T(8,128)} %param.7), kind=kLoop, calls=%fused_computation.1 | loop fusion | flops 1179520 | bytes 1573376 | tf_op jit(solution)/shard_map/reduce_sum | solution.py:277
  10.5 0.7 add_bitcast_fusion.offset_ref
  11.1 0.9 constant_dynamic-update-slice_fusion.3
  12.4 2.1 %collective-permute-start.6 = (bf16[256,1024]{1,0:T(8,128)(2,1)S(1)}, bf16[256,1024]{1,0:T(8,128)(2,1)S(1)}, u32[]{:S(2)}, u32[]{:S(2)}) collective-permute-start(bf16[256,1024]{1,0:T(8,128)(2,1)S(1)} %constant_dynamic-update-slice_fusion.refs_0_), channel_id=1, source_target_pairs={{0,8},{4,12},{8,0},{12,4},{1,9},{5,13},{9,1},{13,5},{2,10},{6,14},... | collective-permute-start | bytes 1572872 | tf_op jit(solution)/shard_map/ppermute | solution.py:286
  14.6 1.8 %collective-permute-start.7 = (bf16[128,1024]{1,0:T(8,128)(2,1)S(1)}, bf16[128,1024]{1,0:T(8,128)(2,1)S(1)}, u32[]{:S(2)}, u32[]{:S(2)}) collective-permute-start(bf16[128,1024]{1,0:T(8,128)(2,1)S(1)} %get-tuple-element.67), channel_id=1, source_target_pairs={{0,32},{16,48},{32,0},{48,16},{1,33},{17,49},{33,1},{49,17},{2,34}... | collective-permute-start | bytes 786440 | tf_op jit(solution)/shard_map/ppermute | solution.py:287
  16.4 1.1 %collective-permute-start.8 = (bf16[128,1024]{1,0:T(8,128)(2,1)S(1)}, bf16[128,1024]{1,0:T(8,128)(2,1)S(1)}, u32[]{:S(2)}, u32[]{:S(2)}) collective-permute-start(bf16[128,1024]{1,0:T(8,128)(2,1)S(1)} %get-tuple-element.67), channel_id=1, source_target_pairs={{0,16},{16,32},{32,48},{48,0},{1,17},{17,33},{33,49},{49,1},{2,18}... | collective-permute-start | bytes 786440 | tf_op jit(solution)/shard_map/ppermute | solution.py:287
  17.5 2.1 %collective-permute-start.9 = (bf16[128,1024]{1,0:T(8,128)(2,1)S(1)}, bf16[128,1024]{1,0:T(8,128)(2,1)S(1)}, u32[]{:S(2)}, u32[]{:S(2)}) collective-permute-start(bf16[128,1024]{1,0:T(8,128)(2,1)S(1)} %get-tuple-element.67), channel_id=1, source_target_pairs={{0,48},{16,0},{32,16},{48,32},{1,49},{17,1},{33,17},{49,33},{2,50}... | collective-permute-start | bytes 786440 | tf_op jit(solution)/shard_map/ppermute | solution.py:287
  19.6 5.7 %collective-permute-done.5 = bf16[128,2176]{1,0:T(8,128)(2,1)S(1)} collective-permute-done((bf16[128,2176]{1,0:T(8,128)(2,1)S(1)}, bf16[128,2176]{1,0:T(8,128)(2,1)S(1)}, u32[]{:S(2)}, u32[]{:S(2)}) %collective-permute-start.5) | collective-permute-done | bytes 557088 | tf_op jit(solution)/shard_map/ppermute | solution.py:285
  25.4 3.4 %collective-permute-done.8 = bf16[128,1024]{1,0:T(8,128)(2,1)S(1)} collective-permute-done((bf16[128,1024]{1,0:T(8,128)(2,1)S(1)}, bf16[128,1024]{1,0:T(8,128)(2,1)S(1)}, u32[]{:S(2)}, u32[]{:S(2)}) %collective-permute-start.8) | collective-permute-done | bytes 262176 | tf_op jit(solution)/shard_map/ppermute | solution.py:287
  29.0 0.5 collective-permute-start.13
  29.9 1.5 %shard_map.85 = (f32[256,1024]{1,0:T(8,128)S(1)}, f32[1,1024]{1,0:T(1,128)S(1)}, bf16[1024,2048]{1,0:T(8,128)(2,1)S(1)}) custom-call(bf16[256,1024]{1,0:T(8,128)(2,1)S(1)} %constant_dynamic-update-slice_fusion.refs_0_, bf16[256,1024]{1,0:T(8,128)(2,1)S(1)} %constant_dynamic-update-slice_fusion.6.refs_1_, ...), custom_call_target="tpu_custom_call" | custom-call | flops 1073741824 | tf_op jit(solution)/shard_map/pallas_call | solution.py:296
  31.6 0.9 shard_map.87
  32.6 0.9 shard_map.86
  33.6 12.5 %all_to_all.5.refs_0_ = f32[32,16,128]{2,1,0:T(8,128)S(1)} all-to-all(f32[32,16,128]{2,1,0:T(8,128)S(1)} %broadcast_in_dim.10), channel_id=1, replica_groups=mesh['zh'=4,'x'=4,'y'=4,'zl'=2,'c'=2] {'x','y','c'}, dimensions={0} | all-to-all | bytes 524288 | tf_op jit(solution)/shard_map/all_to_all | solution.py:312
  46.1 1.6 %shard_map.89 = (bf16[64,2176]{1,0:T(8,128)(2,1)S(1)}, bf16[64,2176]{1,0:T(8,128)(2,1)S(1)}, f32[1,128]{1,0:T(1,128)S(1)}) custom-call(f32[32,16,128]{2,1,0:T(8,128)S(1)} %all_to_all.5.refs_0_, f32[256,1024]{1,0:T(8,128)S(1)} %get-tuple-element.45.refs_1_, f32[256,512]{1,0:T(8,128)S(1)} %get-tuple-element.46.refs_2_, ...), custom_call_target="tpu_custom_call" | custom-call | flops 1073741824 | tf_op jit(solution)/shard_map/pallas_call | solution.py:315
  47.6 3.5 %collective-permute-start.14 = (bf16[64,2176]{1,0:T(8,128)(2,1)S(1)}, bf16[64,2176]{1,0:T(8,128)(2,1)S(1)}, u32[]{:S(2)}, u32[]{:S(2)}) collective-permute-start(bf16[64,2176]{1,0:T(8,128)(2,1)S(1)} %get-tuple-element.52), channel_id=1, source_target_pairs={{0,2},{2,64},{64,66},{66,128},{128,130},{130,192},{192,194},{194,0... | collective-permute-start | bytes 835592 | tf_op jit(solution)/shard_map/ppermute | solution.py:325
  51.3 1.6 %shard_map.90.mine_ref = f32[128,2176]{1,0:T(8,128)S(1)} custom-call(f32[32,16,128]{2,1,0:T(8,128)S(1)} %all_to_all.5.refs_0_, f32[256,1024]{1,0:T(8,128)S(1)} %get-tuple-element.45.refs_1_, f32[256,512]{1,0:T(8,128)S(1)} %get-tuple-element.46.refs_2_, f32[256,512]{1,0:T(8,128)S(1)} %get-tuple-element.47.refs_3_, ...), custom_call_target="tpu_custom_call" | custom-call | flops 1073741824 | tf_op jit(solution)/shard_map/pallas_call | solution.py:315
  52.9 4.7 %collective-permute-done.14.low_ref = bf16[64,2176]{1,0:T(8,128)(2,1)S(1)} collective-permute-done((bf16[64,2176]{1,0:T(8,128)(2,1)S(1)}, bf16[64,2176]{1,0:T(8,128)(2,1)S(1)}, u32[]{:S(2)}, u32[]{:S(2)}) %collective-permute-start.14) | collective-permute-done | bytes 278560 | tf_op jit(solution)/shard_map/ppermute | solution.py:325
  57.6 2.2 %collective-permute-done.15.high_ref = bf16[64,2176]{1,0:T(8,128)(2,1)S(1)} collective-permute-done((bf16[64,2176]{1,0:T(8,128)(2,1)S(1)}, bf16[64,2176]{1,0:T(8,128)(2,1)S(1)}, u32[]{:S(2)}, u32[]{:S(2)}) %collective-permute-start.15) | collective-permute-done | bytes 278560 | tf_op jit(solution)/shard_map/ppermute | solution.py:326
  60.1 4.6 %collective-permute-start.16 = (bf16[32,2176]{1,0:T(8,128)(2,1)S(1)}, bf16[32,2176]{1,0:T(8,128)(2,1)S(1)}, u32[]{:S(2)}, u32[]{:S(2)}) collective-permute-start(bf16[32,2176]{1,0:T(8,128)(2,1)S(1)} %get-tuple-element.56), channel_id=1, source_target_pairs={{0,128},{64,192},{128,0},{192,64},{1,129},{65,193},{129,1},{193,65... | collective-permute-start | bytes 417800 | tf_op jit(solution)/shard_map/ppermute | solution.py:337
  64.7 2.0 %collective-permute-start.17 = (bf16[32,2176]{1,0:T(8,128)(2,1)S(1)}, bf16[32,2176]{1,0:T(8,128)(2,1)S(1)}, u32[]{:S(2)}, u32[]{:S(2)}) collective-permute-start(bf16[32,2176]{1,0:T(8,128)(2,1)S(1)} %get-tuple-element.57), channel_id=1, source_target_pairs={{0,64},{64,128},{128,192},{192,0},{1,65},{65,129},{129,193},{193,1... | collective-permute-start | bytes 417800 | tf_op jit(solution)/shard_map/ppermute | solution.py:337
  66.7 2.1 %collective-permute-start.18 = (bf16[32,2176]{1,0:T(8,128)(2,1)S(1)}, bf16[32,2176]{1,0:T(8,128)(2,1)S(1)}, u32[]{:S(2)}, u32[]{:S(2)}) collective-permute-start(bf16[32,2176]{1,0:T(8,128)(2,1)S(1)} %get-tuple-element.58), channel_id=1, source_target_pairs={{0,192},{64,0},{128,64},{192,128},{1,193},{65,1},{129,65},{193,129... | collective-permute-start | bytes 417800 | tf_op jit(solution)/shard_map/ppermute | solution.py:337
  68.8 0.5 bitcast_add_fusion
  69.3 9.8 %collective-permute-done.17.g1_ref = bf16[32,2176]{1,0:T(8,128)(2,1)S(1)} collective-permute-done((bf16[32,2176]{1,0:T(8,128)(2,1)S(1)}, bf16[32,2176]{1,0:T(8,128)(2,1)S(1)}, u32[]{:S(2)}, u32[]{:S(2)}) %collective-permute-start.17) | collective-permute-done | bytes 139296 | tf_op jit(solution)/shard_map/ppermute | solution.py:337
  79.1 0.5 shard_map.92
  79.6 16.3 %all-gather = bf16[128,2048]{1,0:T(8,128)(2,1)S(1)} all-gather(bf16[32,2048]{1,0:T(8,128)(2,1)S(1)} %get-tuple-element.59), channel_id=2, replica_groups=mesh['zh'=4,'x'=4,'y'=4,'zl'=2,'c'=2] {'zh'}, dimensions={0}, use_global_device_ids=true | all-gather | bytes 655360 | tf_op jit(solution)/shard_map/all_gather | solution.py:351
  95.9 1.0 %shard_map.93 = (f32[128,1024]{1,0:T(8,128)}, f32[128,1024]{1,0:T(8,128)}) custom-call(bf16[4,32,2048]{2,1,0:T(8,128)(2,1)S(1)} %bitcast.8), custom_call_target="tpu_custom_call" | custom-call | tf_op jit(solution)/shard_map/pallas_call | solution.py:345
  (39 shorter events, 1.8 us)
Async XLA Ops:
  0.6 11.5 %collective-permute-start = (bf16[64,1024]{1,0:T(8,128)(2,1)}, bf16[64,1024]{1,0:T(8,128)(2,1)S(1)}, u32[]{:S(2)}, u32[]{:S(2)}) collective-permute-start(bf16[64,1024]{1,0:T(8,128)(2,1)} %param.5), channel_id=1, source_target_pairs={{0,16},{16,32},{32,48},{48,0},{1,17},{17,33},{33,49},{49,1},{2,18}... | collective-permute-start | bytes 393224 | tf_op jit(solution)/shard_map/ppermute | solution.py:271
  2.2 10.2 %collective-permute-start.1 = (bf16[64,1024]{1,0:T(8,128)(2,1)}, bf16[64,1024]{1,0:T(8,128)(2,1)S(1)}, u32[]{:S(2)}, u32[]{:S(2)}) collective-permute-start(bf16[64,1024]{1,0:T(8,128)(2,1)} %param.5), channel_id=1, source_target_pairs={{0,48},{16,0},{32,16},{48,32},{1,49},{17,1},{33,17},{49,33},{2,50}... | collective-permute-start | bytes 393224 | tf_op jit(solution)/shard_map/ppermute | solution.py:271
  3.9 8.5 %collective-permute-start.2 = (bf16[64,1024]{1,0:T(8,128)(2,1)}, bf16[64,1024]{1,0:T(8,128)(2,1)S(1)}, u32[]{:S(2)}, u32[]{:S(2)}) collective-permute-start(bf16[64,1024]{1,0:T(8,128)(2,1)} %param.5), channel_id=1, source_target_pairs={{0,32},{16,48},{32,0},{48,16},{1,33},{17,49},{33,1},{49,17},{2,34}... | collective-permute-start | bytes 393224 | tf_op jit(solution)/shard_map/ppermute | solution.py:271
  5.8 8.7 %collective-permute-start.3 = (bf16[64,1024]{1,0:T(8,128)(2,1)}, bf16[64,1024]{1,0:T(8,128)(2,1)S(1)}, u32[]{:S(2)}, u32[]{:S(2)}) collective-permute-start(bf16[64,1024]{1,0:T(8,128)(2,1)} %param.5), channel_id=1, source_target_pairs={{0,4},{4,8},{8,12},{12,0},{1,5},{5,9},{9,13},{13,1},{2,6},{6,10},{... | collective-permute-start | bytes 393224 | tf_op jit(solution)/shard_map/ppermute | solution.py:270
  7.3 7.2 %collective-permute-start.4 = (bf16[64,1024]{1,0:T(8,128)(2,1)}, bf16[64,1024]{1,0:T(8,128)(2,1)S(1)}, u32[]{:S(2)}, u32[]{:S(2)}) collective-permute-start(bf16[64,1024]{1,0:T(8,128)(2,1)} %param.5), channel_id=1, source_target_pairs={{0,12},{4,0},{8,4},{12,8},{1,13},{5,1},{9,5},{13,9},{2,14},{6,2},{... | collective-permute-start | bytes 393224 | tf_op jit(solution)/shard_map/ppermute | solution.py:270
  12.2 13.1 %collective-permute-start.5 = (bf16[128,2176]{1,0:T(8,128)(2,1)S(1)}, bf16[128,2176]{1,0:T(8,128)(2,1)S(1)}, u32[]{:S(2)}, u32[]{:S(2)}) collective-permute-start(bf16[128,2176]{1,0:T(8,128)(2,1)S(1)} %shard_map.84), channel_id=1, source_target_pairs={{0,2},{2,0},{1,3},{3,1},{4,6},{6,4},{5,7},{7,5},{8,10},{10,8},{9,1... | collective-permute-start | bytes 1671176 | tf_op jit(solution)/shard_map/ppermute | solution.py:285
  12.4 16.4 %collective-permute-start.6 = (bf16[256,1024]{1,0:T(8,128)(2,1)S(1)}, bf16[256,1024]{1,0:T(8,128)(2,1)S(1)}, u32[]{:S(2)}, u32[]{:S(2)}) collective-permute-start(bf16[256,1024]{1,0:T(8,128)(2,1)S(1)} %constant_dynamic-update-slice_fusion.refs_0_), channel_id=1, source_target_pairs={{0,8},{4,12},{8,0},{12,4},{1,9},{5,13},{9,1},{13,5},{2,10},{6,14},... | collective-permute-start | bytes 1572872 | tf_op jit(solution)/shard_map/ppermute | solution.py:286
  14.5 15.4 %copy-start.1 = (s32[64]{0:T(128)S(1)}, s32[64]{0:T(128)}, u32[]{:S(2)}) copy-start(s32[64]{0:T(128)} %param.6) | copy-start | bytes 772
  14.6 10.9 %collective-permute-start.7 = (bf16[128,1024]{1,0:T(8,128)(2,1)S(1)}, bf16[128,1024]{1,0:T(8,128)(2,1)S(1)}, u32[]{:S(2)}, u32[]{:S(2)}) collective-permute-start(bf16[128,1024]{1,0:T(8,128)(2,1)S(1)} %get-tuple-element.67), channel_id=1, source_target_pairs={{0,32},{16,48},{32,0},{48,16},{1,33},{17,49},{33,1},{49,17},{2,34}... | collective-permute-start | bytes 786440 | tf_op jit(solution)/shard_map/ppermute | solution.py:287
  16.4 12.5 %collective-permute-start.8 = (bf16[128,1024]{1,0:T(8,128)(2,1)S(1)}, bf16[128,1024]{1,0:T(8,128)(2,1)S(1)}, u32[]{:S(2)}, u32[]{:S(2)}) collective-permute-start(bf16[128,1024]{1,0:T(8,128)(2,1)S(1)} %get-tuple-element.67), channel_id=1, source_target_pairs={{0,16},{16,32},{32,48},{48,0},{1,17},{17,33},{33,49},{49,1},{2,18}... | collective-permute-start | bytes 786440 | tf_op jit(solution)/shard_map/ppermute | solution.py:287
  17.5 11.4 %collective-permute-start.9 = (bf16[128,1024]{1,0:T(8,128)(2,1)S(1)}, bf16[128,1024]{1,0:T(8,128)(2,1)S(1)}, u32[]{:S(2)}, u32[]{:S(2)}) collective-permute-start(bf16[128,1024]{1,0:T(8,128)(2,1)S(1)} %get-tuple-element.67), channel_id=1, source_target_pairs={{0,48},{16,0},{32,16},{48,32},{1,49},{17,1},{33,17},{49,33},{2,50}... | collective-permute-start | bytes 786440 | tf_op jit(solution)/shard_map/ppermute | solution.py:287
  25.3 7.3 %collective-permute-start.10 = (bf16[256,1024]{1,0:T(8,128)(2,1)S(1)}, bf16[256,1024]{1,0:T(8,128)(2,1)S(1)}, u32[]{:S(2)}, u32[]{:S(2)}) collective-permute-start(bf16[256,1024]{1,0:T(8,128)(2,1)S(1)} %constant_dynamic-update-slice_fusion.refs_0_), channel_id=1, source_target_pairs={{0,1},{1,0},{2,3},{3,2},{4,5},{5,4},{6,7},{7,6},{8,9},{9,8},{10,11... | collective-permute-start | bytes 1572872 | tf_op jit(solution)/shard_map/ppermute | solution.py:291
  28.9 2.5 %collective-permute-start.12 = (bf16[256,1024]{1,0:T(8,128)(2,1)S(1)}, bf16[256,1024]{1,0:T(8,128)(2,1)S(1)}, u32[]{:S(2)}, u32[]{:S(2)}) collective-permute-start(bf16[256,1024]{1,0:T(8,128)(2,1)S(1)} %constant_dynamic-update-slice_fusion.9.refs_2_), channel_id=1, source_target_pairs={{0,1},{1,0},{2,3},{3,2},{4,5},{5,4},{6,7},{7,6},{8,9},{9,8},{10,11... | collective-permute-start | bytes 1572872 | tf_op jit(solution)/shard_map/ppermute | solution.py:291
  29.0 2.6 %collective-permute-start.13 = (bf16[256,1024]{1,0:T(8,128)(2,1)S(1)}, bf16[256,1024]{1,0:T(8,128)(2,1)S(1)}, u32[]{:S(2)}, u32[]{:S(2)}) collective-permute-start(bf16[256,1024]{1,0:T(8,128)(2,1)S(1)} %collective-permute-done.6.refs_3_), channel_id=1, source_target_pairs={{0,1},{1,0},{2,3},{3,2},{4,5},{5,4},{6,7},{7,6},{8,9},{9,8},{10,11... | collective-permute-start | bytes 1572872 | tf_op jit(solution)/shard_map/ppermute | solution.py:291
  29.5 3.0 %collective-permute-start.11 = (bf16[256,1024]{1,0:T(8,128)(2,1)S(1)}, bf16[256,1024]{1,0:T(8,128)(2,1)S(1)}, u32[]{:S(2)}, u32[]{:S(2)}) collective-permute-start(bf16[256,1024]{1,0:T(8,128)(2,1)S(1)} %constant_dynamic-update-slice_fusion.6.refs_1_), channel_id=1, source_target_pairs={{0,1},{1,0},{2,3},{3,2},{4,5},{5,4},{6,7},{7,6},{8,9},{9,8},{10,11... | collective-permute-start | bytes 1572872 | tf_op jit(solution)/shard_map/ppermute | solution.py:291
  46.1 5.1 %copy-start = (bf16[64,1024]{1,0:T(8,128)(2,1)S(1)}, bf16[64,1024]{1,0:T(8,128)(2,1)}, u32[]{:S(2)}) copy-start(bf16[64,1024]{1,0:T(8,128)(2,1)} %param.5) | copy-start | bytes 393220
  47.6 9.9 %collective-permute-start.14 = (bf16[64,2176]{1,0:T(8,128)(2,1)S(1)}, bf16[64,2176]{1,0:T(8,128)(2,1)S(1)}, u32[]{:S(2)}, u32[]{:S(2)}) collective-permute-start(bf16[64,2176]{1,0:T(8,128)(2,1)S(1)} %get-tuple-element.52), channel_id=1, source_target_pairs={{0,2},{2,64},{64,66},{66,128},{128,130},{130,192},{192,194},{194,0... | collective-permute-start | bytes 835592 | tf_op jit(solution)/shard_map/ppermute | solution.py:325
  51.2 8.6 %collective-permute-start.15 = (bf16[64,2176]{1,0:T(8,128)(2,1)S(1)}, bf16[64,2176]{1,0:T(8,128)(2,1)S(1)}, u32[]{:S(2)}, u32[]{:S(2)}) collective-permute-start(bf16[64,2176]{1,0:T(8,128)(2,1)S(1)} %get-tuple-element.54), channel_id=1, source_target_pairs={{0,194},{2,0},{64,2},{66,64},{128,66},{130,128},{192,130},{194,192... | collective-permute-start | bytes 835592 | tf_op jit(solution)/shard_map/ppermute | solution.py:326
  60.1 9.2 %collective-permute-start.16 = (bf16[32,2176]{1,0:T(8,128)(2,1)S(1)}, bf16[32,2176]{1,0:T(8,128)(2,1)S(1)}, u32[]{:S(2)}, u32[]{:S(2)}) collective-permute-start(bf16[32,2176]{1,0:T(8,128)(2,1)S(1)} %get-tuple-element.56), channel_id=1, source_target_pairs={{0,128},{64,192},{128,0},{192,64},{1,129},{65,193},{129,1},{193,65... | collective-permute-start | bytes 417800 | tf_op jit(solution)/shard_map/ppermute | solution.py:337
  64.7 14.4 %collective-permute-start.17 = (bf16[32,2176]{1,0:T(8,128)(2,1)S(1)}, bf16[32,2176]{1,0:T(8,128)(2,1)S(1)}, u32[]{:S(2)}, u32[]{:S(2)}) collective-permute-start(bf16[32,2176]{1,0:T(8,128)(2,1)S(1)} %get-tuple-element.57), channel_id=1, source_target_pairs={{0,64},{64,128},{128,192},{192,0},{1,65},{65,129},{129,193},{193,1... | collective-permute-start | bytes 417800 | tf_op jit(solution)/shard_map/ppermute | solution.py:337
  66.7 12.4 %collective-permute-start.18 = (bf16[32,2176]{1,0:T(8,128)(2,1)S(1)}, bf16[32,2176]{1,0:T(8,128)(2,1)S(1)}, u32[]{:S(2)}, u32[]{:S(2)}) collective-permute-start(bf16[32,2176]{1,0:T(8,128)(2,1)S(1)} %get-tuple-element.58), channel_id=1, source_target_pairs={{0,192},{64,0},{128,64},{192,128},{1,193},{65,1},{129,65},{193,129... | collective-permute-start | bytes 417800 | tf_op jit(solution)/shard_map/ppermute | solution.py:337
